TPU v7x, 32 devices: a whole 2x2x4 slice. The times are simulated.
32 devices in a mesh: row: 4 (over z), col: 8 (over y, x, core).
Axes of the slice: x: 2, y: 2, z: 4, core: 2. Of those that a mesh axis runs over, the one named last changes fastest.
Arguments:
- tiles: bfloat16 [4096, 128, 128], P(('row', 'col')), may hold values from -6 to 6
- tile_target: int32 [4096, 1], P(('row', 'col')), may hold values from 0 to 31; in each aligned block of 128 rows (0 to 127, 128 to 255, ...) at most 8 rows name the same one
- tile_place: int32 [4096], P(('row', 'col')), may hold values from 0 to 95
- density: bfloat16 [4096, 8192], P('col', 'row'), may hold values from -0.125 to 0.125
Outputs:
- contracted: bfloat16 [24576, 8192], P('col', 'row')
Inputs may be any that keep to these rules, and one draw needn't show every extreme that they name: `tile_target`: among the tiles of one device, at most 8 name the same grid position, and some device has exactly 8 tiles for one position.
All inputs are finite; a program needn't handle non-finite values.
Results may differ from a plain program's by a relative error of at most 0.0046.
Values may be sent and summed in bfloat16 or wider, within the bound.
No kernel may reach another device: no remote copies, remote signals or barrier semaphores. Data moves between devices by JAX's collectives and lax.ppermute only.
A program may use at most 256 MiB of HBM per device.

v0:
```python
import jax
import jax.numpy as jnp
from jax import lax
from jax.sharding import PartitionSpec as P

ROW_BLOCKS_DEV = 24
K_BLOCKS = 4
STEPS = 4
POSITIONS = 96


def passed_along(value, axis, steps):
    count = lax.axis_size(axis)
    pairs = [(source, (source + steps) % count) for source in range(count)]
    return lax.ppermute(value, axis, pairs)


def on_device(tiles, tile_target, tile_place, density):
    row_count = lax.axis_size("row")
    col_count = lax.axis_size("col")
    devices = row_count * col_count
    tile_count = tiles.shape[0]
    tile_size = tiles.shape[1]
    capacity = max(2, (2 * tile_count + devices - 1) // devices)
    slots = devices * capacity
    targets = tile_target[:, 0]
    order = jnp.arange(tile_count, dtype=jnp.int32)
    same_target = targets[:, None] == targets[None, :]
    earlier = order[None, :] < order[:, None]
    ranks = jnp.sum((same_target & earlier).astype(jnp.int32), axis=1)
    slot_of = targets * capacity + ranks
    hits = slot_of[None, :] == jnp.arange(slots, dtype=jnp.int32)[:, None]
    filled = jnp.any(hits, axis=1)
    source = jnp.sum(jnp.where(hits, order[None, :], 0), axis=1)
    padded_tiles = jnp.concatenate(
        [tiles, jnp.zeros((1, tile_size, tile_size), tiles.dtype)], axis=0
    )
    send_tiles = jnp.take(padded_tiles, jnp.where(filled, source, tile_count), axis=0)
    send_places = jnp.where(filled, jnp.take(tile_place, source), -1)
    flat_tiles = send_tiles.reshape(devices, capacity, tile_size, tile_size)
    flat_places = send_places.reshape(devices, capacity)
    got_tiles, got_places = (
        lax.all_to_all(flat_tiles, ("row", "col"), split_axis=0, concat_axis=0, tiled=True),
        lax.all_to_all(flat_places, ("row", "col"), split_axis=0, concat_axis=0, tiled=True),
    )
    got_tiles = got_tiles.reshape(slots, tile_size * tile_size)
    got_places = got_places.reshape(slots)
    selector = (got_places[None, :] == jnp.arange(POSITIONS, dtype=jnp.int32)[:, None]).astype(
        jnp.bfloat16
    )
    dense = jnp.dot(selector, got_tiles, preferred_element_type=jnp.float32)
    dense = dense.reshape(ROW_BLOCKS_DEV, K_BLOCKS, tile_size, tile_size).transpose(0, 2, 1, 3)
    panel = dense.reshape(ROW_BLOCKS_DEV * tile_size, K_BLOCKS * tile_size).astype(jnp.bfloat16)
    total = jnp.zeros((panel.shape[0], density.shape[1]), jnp.float32)
    left, right = (panel, density)
    for offset in range(STEPS):
        total = total + jnp.dot(left, right, preferred_element_type=jnp.float32)
        if offset + 1 < STEPS:
            left = passed_along(left, "row", -1)
            right = passed_along(right, "col", -1)
    return total.astype(jnp.bfloat16)


def solution(mesh):
    in_specs = (
        P(("row", "col"), None, None),
        P(("row", "col"), None),
        P(("row", "col")),
        P("col", "row"),
    )
    out_specs = P("col", "row")
    return jax.shard_map(
        on_device, mesh=mesh, in_specs=in_specs, out_specs=out_specs, check_vma=False
    )
```

profile of v0, /device:TPU:0, one launch (start us, length us, event | category | flops | bytes accessed | tf_op | source)
XLA Modules:
  0.0 516.6 jit_solution(9136868664578088765)
XLA Ops:
  0.0 0.9 convert_reduce_fusion
  0.9 0.7 multiply_add_fusion.1
  1.7 0.1 select_reduce_fusion
  2.0 1.9 gather_fusion
  4.0 0.6 select_select_fusion
  4.6 7.3 %all-to-all-start = ((s32[32,1,8]{2,1,0:T(1,128)}), s32[32,1,8]{2,1,0:T(1,128)S(1)}, u32[]{:S(2)}, u32[]{:S(2)}) async-start(s32[32,1,8]{2,1,0:T(1,128)} %bitcast.3), calls=%async_computation | async-start | bytes 32768 | tf_op jit(solution)/shard_map/all_to_all | solution.py:44
  12.0 5.7 %concatenate.3 = bf16[129,128,128]{2,1,0:T(8,128)(2,1)} pad(bf16[128,128,128]{2,1,0:T(8,128)(2,1)} %param.4, bf16[]{:T(256)} %constant.40.clone.1), padding=0_1x0_0x0_0 | pad | bytes 8421378 | tf_op jit(solution)/shard_map/concatenate | solution.py:35
  17.8 10.8 %gather_fusion.1 = bf16[256,128,128]{2,1,0:T(8,128)(2,1)} fusion(bf16[129,128,128]{2,1,0:T(8,128)(2,1)} %concatenate.3, s32[1024]{0:T(1024)S(1)} %pad_clamp_fusion), kind=kCustom, calls=%fused_computation.1 | custom fusion | bytes 16778240 | tf_op jit(solution)/shard_map/jit(_take)/gather | solution.py:38
  28.6 7.6 %broadcast_select_fusion = bf16[32,8,128,128]{3,2,1,0:T(8,128)(2,1)} fusion(bf16[32,8,128,128]{3,2,1,0:T(8,128)(2,1)} %bitcast.41, pred[32,8]{1,0:T(8,128)(4,1)S(1)} %compare_and_fusion), kind=kLoop, calls=%fused_computation.4 | loop fusion | flops 4194304 | bytes 16777472 | tf_op jit(solution)/shard_map/jit(_take)/select_n | solution.py:38
  36.2 6.1 %all-to-all-start.1 = ((bf16[32,8,128,128]{3,2,1,0:T(8,128)(2,1)}), bf16[32,8,128,128]{3,2,1,0:T(8,128)(2,1)}, u32[]{:S(2)}, u32[]{:S(2)}) async-start(bf16[32,8,128,128]{3,2,1,0:T(8,128)(2,1)} %broadcast_select_fusion), calls=%async_computation.1 | async-start | bytes 16777216 | tf_op jit(solution)/shard_map/all_to_all | solution.py:43
  42.4 0.5 broadcast.149
  42.9 0.7 reduce.3
  43.6 184.6 %all-to-all-done.1 = bf16[32,8,128,128]{3,2,1,0:T(8,128)(2,1)} async-done(((bf16[32,8,128,128]{3,2,1,0:T(8,128)(2,1)}), bf16[32,8,128,128]{3,2,1,0:T(8,128)(2,1)}, u32[]{:S(2)}, u32[]{:S(2)}) %all-to-all-start.1) | async-done | bytes 8388640 | tf_op jit(solution)/shard_map/all_to_all | solution.py:43
  228.2 23.3 %copy.20 = bf16[32,8,128,128]{3,1,2,0:T(8,128)(2,1)} copy(bf16[32,8,128,128]{3,2,1,0:T(8,128)(2,1)} %all-to-all-done.1) | data formatting | bytes 16777216
  251.6 11.9 %copy.12 = bf16[16384,256]{1,0:T(8,128)(2,1)} copy(bf16[16384,256]{0,1:T(8,128)(2,1)} %bitcast.42) | data formatting | bytes 16777216 | tf_op jit(solution)/shard_map/dot_general | solution.py:51
  263.5 7.7 %convert_bitcast_fusion = bf16[24,128,4,128]{3,0,1,2:T(8,128)(2,1)} fusion(bf16[128,128,256,1]{2,1,0,3:T(8,128)(2,1)} %bitcast.45, s32[24,4]{0,1:T(4,128)S(1)} %multiply_add_fusion, s32[256]{0:T(256)S(1)} %eq.58), kind=kOutput, calls=%fused_computation.6 | convolution fusion | flops 806903808 | bytes 11535744 | tf_op jit(solution)/shard_map/dot_general | solution.py:51
  271.2 4.3 copy.13
  275.6 0.9 copy.21
  276.5 0.7 copy-done.2
  277.2 0.5 collective-permute-start.1
  277.6 68.5 %collective-permute-done = bf16[3072,512]{0,1:T(8,128)(2,1)S(1)} collective-permute-done((bf16[3072,512]{0,1:T(8,128)(2,1)S(1)}, bf16[3072,512]{0,1:T(8,128)(2,1)S(1)}, u32[]{:S(2)}, u32[]{:S(2)}) %collective-permute-start) | collective-permute-done | bytes 3145760 | tf_op jit(solution)/shard_map/ppermute | solution.py:15
  346.2 2.1 collective-permute-start.2
  348.2 0.4 collective-permute-start.3
  348.7 23.6 %collective-permute-done.3 = bf16[512,2048]{1,0:T(8,128)(2,1)S(1)} collective-permute-done((bf16[512,2048]{1,0:T(8,128)(2,1)S(1)}, bf16[512,2048]{1,0:T(8,128)(2,1)S(1)}, u32[]{:S(2)}, u32[]{:S(2)}) %collective-permute-start.3) | collective-permute-done | bytes 2097184 | tf_op jit(solution)/shard_map/ppermute | solution.py:15
  372.2 2.8 collective-permute-start.5
  375.0 39.9 %collective-permute-done.2 = bf16[3072,512]{0,1:T(8,128)(2,1)S(1)} collective-permute-done((bf16[3072,512]{0,1:T(8,128)(2,1)S(1)}, bf16[3072,512]{0,1:T(8,128)(2,1)S(1)}, u32[]{:S(2)}, u32[]{:S(2)}) %collective-permute-start.2) | collective-permute-done | bytes 3145760 | tf_op jit(solution)/shard_map/ppermute | solution.py:15
  414.9 4.2 collective-permute-start.4
  419.1 11.9 %fusion.6 = f32[3072,2048]{1,0:T(8,128)} fusion(bf16[512,2048]{1,0:T(8,128)(2,1)S(1)} %copy-done.2, bf16[64,8,24,128]{3,2,1,0:T(8,128)(2,1)S(1)} %bitcast.44), kind=kOutput, calls=%fused_computation.29 | convolution fusion | flops 6442450944 | bytes 30408704 | tf_op jit(solution)/shard_map/dot_general | solution.py:57
  431.0 11.7 %fusion.7 = f32[3072,2048]{1,0:T(8,128)} fusion(bf16[3072,512]{0,1:T(8,128)(2,1)S(1)} %collective-permute-done, bf16[512,2048]{1,0:T(8,128)(2,1)S(1)} %collective-permute-done.1), kind=kOutput, calls=%fused_computation.30 | convolution fusion | flops 6442450944 | bytes 30408704 | tf_op jit(solution)/shard_map/dot_general | solution.py:57
  442.7 11.7 %fusion.8 = f32[3072,2048]{1,0:T(8,128)} fusion(bf16[3072,512]{0,1:T(8,128)(2,1)S(1)} %collective-permute-done.2, bf16[512,2048]{1,0:T(8,128)(2,1)S(1)} %collective-permute-done.3), kind=kOutput, calls=%fused_computation.31 | convolution fusion | flops 6442450944 | bytes 30408704 | tf_op jit(solution)/shard_map/dot_general | solution.py:57
  454.4 30.3 %collective-permute-done.4 = bf16[3072,512]{0,1:T(8,128)(2,1)} collective-permute-done((bf16[3072,512]{0,1:T(8,128)(2,1)S(1)}, bf16[3072,512]{0,1:T(8,128)(2,1)}, u32[]{:S(2)}, u32[]{:S(2)}) %collective-permute-start.4) | collective-permute-done | bytes 3145760 | tf_op jit(solution)/shard_map/ppermute | solution.py:15
  484.8 31.4 %add_convert_fusion = bf16[3072,2048]{1,0:T(8,128)(2,1)} fusion(f32[3072,2048]{1,0:T(8,128)} %fusion.8, f32[3072,2048]{1,0:T(8,128)} %fusion.6, f32[3072,2048]{1,0:T(8,128)} %fusion.7, bf16[3072,512]{0,1:T(8,128)(2,1)} %collective-permute-done.4, bf16[512,2048]{1,0:T(8,128)(2,1)} %collective-permute-done.5), kind=kOutput, calls=%fused_computation.2 | convolution fusion | flops 6467616768 | bytes 93323264 | tf_op jit(solution)/shard_map/dot_general | solution.py:57
  (21 shorter events, 0.7 us)
Async XLA Ops:
  0.0 2.0 copy-start
  4.6 31.6 %all-to-all-start = ((s32[32,1,8]{2,1,0:T(1,128)}), s32[32,1,8]{2,1,0:T(1,128)S(1)}, u32[]{:S(2)}, u32[]{:S(2)}) async-start(s32[32,1,8]{2,1,0:T(1,128)} %bitcast.3), calls=%async_computation | async-start | bytes 32768 | tf_op jit(solution)/shard_map/all_to_all | solution.py:44
  36.2 192.0 %all-to-all-start.1 = ((bf16[32,8,128,128]{3,2,1,0:T(8,128)(2,1)}), bf16[32,8,128,128]{3,2,1,0:T(8,128)(2,1)}, u32[]{:S(2)}, u32[]{:S(2)}) async-start(bf16[32,8,128,128]{3,2,1,0:T(8,128)(2,1)} %broadcast_select_fusion), calls=%async_computation.1 | async-start | bytes 16777216 | tf_op jit(solution)/shard_map/all_to_all | solution.py:43
  275.6 1.6 copy-start.2
  276.5 69.7 %collective-permute-start = (bf16[3072,512]{0,1:T(8,128)(2,1)S(1)}, bf16[3072,512]{0,1:T(8,128)(2,1)S(1)}, u32[]{:S(2)}, u32[]{:S(2)}) collective-permute-start(bf16[3072,512]{0,1:T(8,128)(2,1)S(1)} %bitcast.46), channel_id=1, source_target_pairs={{0,24},{8,0},{16,8},{24,16},{1,25},{9,1},{17,9},{25,17},{2,26},{10... | collective-permute-start | bytes 9437192 | tf_op jit(solution)/shard_map/ppermute | solution.py:15
  277.2 71.1 %collective-permute-start.1 = (bf16[512,2048]{1,0:T(8,128)(2,1)S(1)}, bf16[512,2048]{1,0:T(8,128)(2,1)S(1)}, u32[]{:S(2)}, u32[]{:S(2)}) collective-permute-start(bf16[512,2048]{1,0:T(8,128)(2,1)S(1)} %copy-done.2), channel_id=1, source_target_pairs={{0,7},{1,0},{2,1},{3,2},{4,3},{5,4},{6,5},{7,6},{8,15},{9,8},{10,9... | collective-permute-start | bytes 6291464 | tf_op jit(solution)/shard_map/ppermute | solution.py:15
  346.2 68.7 %collective-permute-start.2 = (bf16[3072,512]{0,1:T(8,128)(2,1)S(1)}, bf16[3072,512]{0,1:T(8,128)(2,1)S(1)}, u32[]{:S(2)}, u32[]{:S(2)}) collective-permute-start(bf16[3072,512]{0,1:T(8,128)(2,1)S(1)} %collective-permute-done), channel_id=1, source_target_pairs={{0,24},{8,0},{16,8},{24,16},{1,25},{9,1},{17,9},{25,17},{2,26},{10... | collective-permute-start | bytes 9437192 | tf_op jit(solution)/shard_map/ppermute | solution.py:15
  348.2 24.0 %collective-permute-start.3 = (bf16[512,2048]{1,0:T(8,128)(2,1)S(1)}, bf16[512,2048]{1,0:T(8,128)(2,1)S(1)}, u32[]{:S(2)}, u32[]{:S(2)}) collective-permute-start(bf16[512,2048]{1,0:T(8,128)(2,1)S(1)} %collective-permute-done.1), channel_id=1, source_target_pairs={{0,7},{1,0},{2,1},{3,2},{4,3},{5,4},{6,5},{7,6},{8,15},{9,8},{10,9... | collective-permute-start | bytes 6291464 | tf_op jit(solution)/shard_map/ppermute | solution.py:15
  372.2 82.2 %collective-permute-start.5 = (bf16[512,2048]{1,0:T(8,128)(2,1)S(1)}, bf16[512,2048]{1,0:T(8,128)(2,1)}, u32[]{:S(2)}, u32[]{:S(2)}) collective-permute-start(bf16[512,2048]{1,0:T(8,128)(2,1)S(1)} %collective-permute-done.3), channel_id=1, source_target_pairs={{0,7},{1,0},{2,1},{3,2},{4,3},{5,4},{6,5},{7,6},{8,15},{9,8},{10,9... | collective-permute-start | bytes 6291464 | tf_op jit(solution)/shard_map/ppermute | solution.py:15
  414.9 69.9 %collective-permute-start.4 = (bf16[3072,512]{0,1:T(8,128)(2,1)S(1)}, bf16[3072,512]{0,1:T(8,128)(2,1)}, u32[]{:S(2)}, u32[]{:S(2)}) collective-permute-start(bf16[3072,512]{0,1:T(8,128)(2,1)S(1)} %collective-permute-done.2), channel_id=1, source_target_pairs={{0,24},{8,0},{16,8},{24,16},{1,25},{9,1},{17,9},{25,17},{2,26},{10... | collective-permute-start | bytes 9437192 | tf_op jit(solution)/shard_map/ppermute | solution.py:15
  484.8 31.4 %copy-start.1 = (s32[128]{0:T(128)S(1)}, s32[128]{0:T(128)}, u32[]{:S(2)}) copy-start(s32[128]{0:T(128)} %param.6) | copy-start | bytes 1540
where the time goes:
time: 522 us; the launch traced here: 517 us
  waiting for transfers between devices  347 us (66%)
  matrix products  74.5 us (14%)
  local copies, waits for them, and re-layouts  60.5 us (12%)
  starting transfers between devices  23.5 us (5%)
  other arithmetic  10.7 us (2%)
    all_to_all x1, waiting for transfers between devices, on_device(): lax.all_to_all(flat_tiles, ('row', 'col'), split_axis=0, concat_axis=0, t...  185 us
    ppermute x6, waiting for transfers between devices, passed_along(): return lax.ppermute(value, axis, pairs)  162 us
    dot_general x4, matrix products, on_device(): total = total + jnp.dot(left, right, preferred_element_type=jnp.float32)  66.7 us
    unnamed x8, local copies, waits for them, and re-layouts  24.9 us
    dot_general x1, local copies, waits for them, and re-layouts, on_device(): dense = jnp.dot(selector, got_tiles, preferred_element_type=jnp.float32)  11.9 us
    gather x1, local copies, waits for them, and re-layouts, on_device(): jnp.take(padded_tiles, jnp.where(filled, source, tile_count), axis=0)  10.8 us
  transfers between devices with their start and end apart: 8, of which 5 were waited for; matrix products, arithmetic and copies ran while one was open for 12% of the time, Pallas kernels for 0%

commit v1 on v0

v1 whole, which is shorter than its diff:
```python
import functools

import jax
import jax.numpy as jnp
from jax import lax
from jax.experimental import pallas as pl
from jax.experimental.pallas import tpu as pltpu
from jax.sharding import PartitionSpec as P

ROW_BLOCKS_DEV = 24
K_BLOCKS = 4
STEPS = 4
POSITIONS = 96

INWARD = [(0, 1), (3, 2)]
ACROSS = [(1, 2), (2, 1)]
OUTWARD = [(1, 0), (2, 3)]
LAG = 2
ROW_TILE = 4
VMEM_BYTES = 56 * 1024 * 1024


def passed_along(value, axis, steps):
    count = lax.axis_size(axis)
    pairs = [(source, (source + steps) % count) for source in range(count)]
    return lax.ppermute(value, axis, pairs)


def tile_capacity(tile_count, devices):
    return max(2, (2 * tile_count + devices - 1) // devices)


def ranks_of(targets):
    order = jnp.arange(targets.shape[0], dtype=jnp.int32)
    same_target = targets[:, None] == targets[None, :]
    earlier = order[None, :] < order[:, None]
    return jnp.sum((same_target & earlier).astype(jnp.int32), axis=1)


def on_device_ring(tiles, tile_target, tile_place, density):
    row_count = lax.axis_size("row")
    col_count = lax.axis_size("col")
    devices = row_count * col_count
    tile_count = tiles.shape[0]
    tile_size = tiles.shape[1]
    capacity = tile_capacity(tile_count, devices)
    slots = devices * capacity
    targets = tile_target[:, 0]
    order = jnp.arange(tile_count, dtype=jnp.int32)
    slot_of = targets * capacity + ranks_of(targets)
    hits = slot_of[None, :] == jnp.arange(slots, dtype=jnp.int32)[:, None]
    filled = jnp.any(hits, axis=1)
    source = jnp.sum(jnp.where(hits, order[None, :], 0), axis=1)
    send_tiles = jnp.take(tiles, source, axis=0)
    send_places = jnp.where(filled, jnp.take(tile_place, source), -1)
    got_tiles, got_places = (
        lax.all_to_all(send_tiles, ("row", "col"), split_axis=0, concat_axis=0, tiled=True),
        lax.all_to_all(send_places, ("row", "col"), split_axis=0, concat_axis=0, tiled=True),
    )
    got_tiles = got_tiles.reshape(slots, tile_size * tile_size)
    selector = (got_places[None, :] == jnp.arange(POSITIONS, dtype=jnp.int32)[:, None]).astype(
        jnp.bfloat16
    )
    dense = jnp.dot(selector, got_tiles, preferred_element_type=jnp.float32)
    dense = dense.reshape(ROW_BLOCKS_DEV, K_BLOCKS, tile_size, tile_size).transpose(0, 2, 1, 3)
    panel = dense.reshape(ROW_BLOCKS_DEV * tile_size, K_BLOCKS * tile_size).astype(jnp.bfloat16)
    total = jnp.zeros((panel.shape[0], density.shape[1]), jnp.float32)
    left, right = (panel, density)
    for offset in range(STEPS):
        total = total + jnp.dot(left, right, preferred_element_type=jnp.float32)
        if offset + 1 < STEPS:
            left = passed_along(left, "row", -1)
            right = passed_along(right, "col", -1)
    return total.astype(jnp.bfloat16)


def picked(tiles, source):
    count = source.shape[0]

    def kernel(source_ref, tiles_ref, out_ref, sem):
        def one(slot, carry):
            pltpu.make_async_copy(
                tiles_ref.at[source_ref[slot]], out_ref.at[slot], sem
            ).start()
            return carry

        lax.fori_loop(0, count, one, 0)
        pltpu.make_async_copy(tiles_ref.at[pl.ds(0, count)], out_ref, sem).wait()

    return pl.pallas_call(
        kernel,
        out_shape=jax.ShapeDtypeStruct((count,) + tiles.shape[1:], tiles.dtype),
        grid_spec=pltpu.PrefetchScalarGridSpec(
            num_scalar_prefetch=1,
            grid=(),
            in_specs=[pl.BlockSpec(memory_space=pl.ANY)],
            out_specs=pl.BlockSpec(memory_space=pl.ANY),
            scratch_shapes=[pltpu.SemaphoreType.DMA],
        ),
        name="pick_tiles",
    )(source, tiles)


def listed_sums(got, first_index, second_index, low, sizes):
    tile = got[0].shape[1:]
    slots = got[0].shape[0]
    entries = sum(sizes)
    parts = len(got)
    chunks = len(sizes)

    def kernel(first_ref, second_ref, *refs):
        got_refs = refs[:parts]
        out_refs = refs[parts : parts + 2 * chunks]
        total = refs[-1]
        for index_ref, outs in (
            (first_ref, out_refs[:chunks]),
            (second_ref, out_refs[chunks:]),
        ):

            def clear(entry, carry):
                total[entry] = jnp.zeros(tile, jnp.float32)
                return carry

            lax.fori_loop(0, entries, clear, 0)
            for part, got_ref in enumerate(got_refs):

                def add(slot, carry, part=part, got_ref=got_ref, index_ref=index_ref):
                    entry = index_ref[part * slots + slot] - low

                    @pl.when((entry >= 0) & (entry < entries))
                    def _():
                        total[entry] = total[entry] + got_ref[slot].astype(jnp.float32)

                    return carry

                lax.fori_loop(0, slots, add, 0)
            start = 0
            for size, out in zip(sizes, outs):

                def store(entry, carry, start=start, out=out):
                    out[entry] = total[start + entry].astype(out.dtype)
                    return carry

                lax.fori_loop(0, size, store, 0)
                start += size

    whole = pl.BlockSpec(memory_space=pltpu.VMEM)
    out = pl.pallas_call(
        kernel,
        out_shape=[jax.ShapeDtypeStruct((size,) + tile, got[0].dtype) for size in sizes] * 2,
        grid_spec=pltpu.PrefetchScalarGridSpec(
            num_scalar_prefetch=2,
            grid=(),
            in_specs=[whole] * parts,
            out_specs=[whole] * (2 * chunks),
            scratch_shapes=[pltpu.VMEM((entries,) + tile, jnp.float32)],
        ),
        compiler_params=pltpu.CompilerParams(vmem_limit_bytes=VMEM_BYTES),
        name="sum_tiles",
    )(first_index, second_index, *got)
    return list(out[:chunks]), list(out[chunks:])


def added(one, other):
    return (one.astype(jnp.float32) + other.astype(jnp.float32)).astype(one.dtype)


def chain_sums(first, second, token):
    count = len(first)
    near, inward, across, outward = {}, {}, {}, {}
    for step in range(count + 3 * LAG):
        sent, crossed, back, done = (step - lag * LAG for lag in range(4))
        held = {"token": token}
        if sent < count:
            held["sent"] = first[sent]
        if 0 <= crossed < count:
            held["inward"] = inward[crossed]
        if 0 <= back < count:
            held["across"] = across[back]
        if 0 <= done < count:
            held["outward"] = outward[done]
        held = lax.optimization_barrier(held)
        token = held["token"]
        if sent < count:
            inward[sent] = lax.ppermute(held["sent"], "row", INWARD)
        if 0 <= crossed < count:
            near[crossed] = added(first[crossed], held["inward"])
            across[crossed] = lax.ppermute(near[crossed], "row", ACROSS)
            token = near[crossed]
        if 0 <= back < count:
            across[back] = held["across"]
            outward[back] = lax.ppermute(added(second[back], held["across"]), "row", OUTWARD)
        if 0 <= done < count:
            outward[done] = held["outward"]
    in_order = [[part[step] for step in range(count)] for part in (near, across, outward)]
    return in_order, token


def contracted_rows(rows, at_end, first_at, second_at, slabs, chunks, low, before, out_dtype):
    near, across, outward = chunks
    sizes = [chunk.shape[0] for chunk in near]
    entries = sum(sizes)
    tile = near[0].shape[1]
    count = len(near)
    depth = K_BLOCKS * tile
    columns = slabs[0].shape[1]
    row_count = len(slabs)
    panels = len(rows)
    block = (ROW_TILE * tile, columns)
    col_tile = min(512, columns)

    def kernel(place_ref, first_ref, second_ref, *refs):
        near_refs, across_refs, outward_refs = (
            refs[part * count : (part + 1) * count] for part in range(3)
        )
        refs = refs[3 * count :]
        slab_refs = refs[:row_count]
        refs = refs[row_count:]
        if before is not None:
            before_ref, refs = refs[0], refs[1:]
        out_ref, near_held, far_held, slab_held, left, sems = refs
        step = pl.program_id(0)
        me, end = place_ref[0], place_ref[1]

        @pl.when(step == 0)
        def _():
            start = 0
            for part in range(count):
                there = pl.ds(start, sizes[part])
                pltpu.make_async_copy(
                    near_refs[part], near_held.at[there], sems.at[2 * part]
                ).start()

                @pl.when(end == 1)
                def _():
                    pltpu.make_async_copy(
                        outward_refs[part], far_held.at[there], sems.at[2 * part + 1]
                    ).start()

                @pl.when(end == 0)
                def _():
                    pltpu.make_async_copy(
                        across_refs[part], far_held.at[there], sems.at[2 * part + 1]
                    ).start()

                start += sizes[part]
            for at, row in enumerate(rows):
                offset = lax.rem(row - me + row_count, row_count)
                for which in range(row_count):

                    @pl.when(offset == which)
                    def _():
                        pltpu.make_async_copy(
                            slab_refs[which],
                            slab_held.at[pl.ds(at * depth, depth)],
                            sems.at[2 * count + at],
                        ).start()

            near_held[entries] = jnp.zeros((tile, tile), near_held.dtype)
            far_held[entries] = jnp.zeros((tile, tile), far_held.dtype)
            start = 0
            for part in range(count):
                there = pl.ds(start, sizes[part])
                pltpu.make_async_copy(
                    near_refs[part], near_held.at[there], sems.at[2 * part]
                ).wait()
                pltpu.make_async_copy(
                    near_refs[part], far_held.at[there], sems.at[2 * part + 1]
                ).wait()
                start += sizes[part]
            for at in range(panels):
                pltpu.make_async_copy(
                    slab_refs[0],
                    slab_held.at[pl.ds(at * depth, depth)],
                    sems.at[2 * count + at],
                ).wait()

        def fill(row_block, carry):
            for at, row in enumerate(rows):
                for k in range(K_BLOCKS):
                    place = row * POSITIONS + (step * ROW_TILE + row_block) * K_BLOCKS + k
                    one = jnp.minimum(first_ref[place] - low, entries)
                    other = jnp.minimum(second_ref[place] - low, entries)
                    left[
                        pl.ds(pl.multiple_of(row_block * tile, tile), tile),
                        (at * K_BLOCKS + k) * tile : (at * K_BLOCKS + k + 1) * tile,
                    ] = added(near_held[one], far_held[other])
            return carry

        lax.fori_loop(0, ROW_TILE, fill, 0)
        for column in range(0, columns, col_tile):
            part = slice(column, column + col_tile)
            product = jnp.dot(
                left[...], slab_held[:, part], preferred_element_type=jnp.float32
            )
            if before is not None:
                product = product + before_ref[:, part]
            out_ref[:, part] = product.astype(out_ref.dtype)

    anywhere = pl.BlockSpec(memory_space=pl.ANY)
    blocked = pl.BlockSpec(block, lambda step, *_: (step, 0))
    extra = () if before is None else (before,)
    place = jnp.stack([lax.axis_index("row"), at_end]).astype(jnp.int32)
    return pl.pallas_call(
        kernel,
        out_shape=jax.ShapeDtypeStruct((ROW_BLOCKS_DEV * tile, columns), out_dtype),
        grid_spec=pltpu.PrefetchScalarGridSpec(
            num_scalar_prefetch=3,
            grid=(ROW_BLOCKS_DEV // ROW_TILE,),
            in_specs=[anywhere] * (3 * count + row_count) + [blocked] * len(extra),
            out_specs=blocked,
            scratch_shapes=[
                pltpu.VMEM((entries + 1, tile, tile), near[0].dtype),
                pltpu.VMEM((entries + 1, tile, tile), near[0].dtype),
                pltpu.VMEM((panels * depth, columns), slabs[0].dtype),
                pltpu.VMEM((ROW_TILE * tile, panels * depth), near[0].dtype),
                pltpu.SemaphoreType.DMA((2 * count + panels,)),
            ],
        ),
        compiler_params=pltpu.CompilerParams(vmem_limit_bytes=VMEM_BYTES),
        cost_estimate=pl.CostEstimate(
            flops=2 * ROW_BLOCKS_DEV * tile * panels * depth * columns,
            bytes_accessed=2 * entries * tile * tile * 2,
            transcendentals=0,
        ),
        name="contract_panels",
    )(place, first_at, second_at, *near, *across, *outward, *slabs, *extra)


def on_device_chain(tiles, tile_target, tile_place, density):
    row_count = lax.axis_size("row")
    col_count = lax.axis_size("col")
    devices = row_count * col_count
    tile_count, tile_size = tiles.shape[:2]
    capacity = tile_capacity(tile_count, devices)
    plane_slots = col_count * capacity
    all_entries = row_count * POSITIONS
    me = lax.axis_index("row")
    column = lax.axis_index("col")
    at_end = ((me == 0) | (me == row_count - 1)).astype(jnp.int32)

    targets = tile_target[:, 0]
    order = jnp.arange(tile_count, dtype=jnp.int32)
    slot_of = targets * capacity + ranks_of(targets)
    hits = slot_of[None, :] == jnp.arange(devices * capacity, dtype=jnp.int32)[:, None]
    source = jnp.sum(jnp.where(hits, order[None, :], 0), axis=1).reshape(row_count, plane_slots)
    codes = lax.all_gather(slot_of * POSITIONS + tile_place, ("row", "col"), tiled=True)
    got = []
    for row in range(row_count):
        sent = picked(tiles, source[row])
        if got:
            sent, got[-1] = lax.optimization_barrier((sent, got[-1]))
        got.append(lax.all_to_all(sent, "col", split_axis=0, concat_axis=0, tiled=True))

    slabs = [density]
    density, got[2] = lax.optimization_barrier((density, got[2]))
    for offset in range(1, STEPS):
        slabs.append(passed_along(slabs[-1] if offset > 1 else density, "col", -1))

    codes = codes.reshape(row_count, col_count * tile_count)
    code_target = codes // (POSITIONS * capacity)
    code_place = codes % POSITIONS
    by_target = (code_target[:, None, :] == jnp.arange(devices, dtype=jnp.int32)[None, :, None])
    by_place = (code_place[:, None, :] == jnp.arange(POSITIONS, dtype=jnp.int32)[None, :, None])
    held = jnp.einsum(
        "ptn,pqn->ptq",
        by_target.astype(jnp.bfloat16),
        by_place.astype(jnp.bfloat16),
        preferred_element_type=jnp.float32,
    )
    rightward = jnp.sum(held[: row_count - 1], axis=0) > 0
    leftward = jnp.sum(held[1:], axis=0) > 0
    used = jnp.stack([rightward, leftward]).astype(jnp.int32)
    used = used.reshape(2, row_count, col_count, POSITIONS)
    tallies = jnp.sum(used, axis=3)
    earliest = [row * (POSITIONS // 2) for row in range(row_count)]
    starts, end = [], jnp.zeros((2, col_count), jnp.int32)
    for row in range(row_count):
        starts.append(jnp.maximum(end, earliest[row]))
        end = starts[-1] + tallies[:, row]
    needed = jnp.max(end)
    starts = jnp.stack(starts, axis=1)
    mine = lax.dynamic_index_in_dim(used, column, 2, keepdims=False)
    my_starts = lax.dynamic_index_in_dim(starts, column, 2, keepdims=False)
    before_it = jnp.arange(POSITIONS)[:, None] < jnp.arange(POSITIONS)[None, :]
    earlier = jnp.sum(jnp.where(before_it[None, None], mine[..., None], 0), axis=2)
    listed = jnp.where(mine > 0, my_starts[..., None] + earlier, all_entries)
    is_low = me < row_count // 2
    first_at = jnp.where(is_low, listed[0], listed[1])
    second_at = jnp.where(is_low, listed[1], listed[0])

    near_codes = lax.dynamic_index_in_dim(codes, me, 0, keepdims=False)
    near_codes = near_codes.reshape(col_count, 1, tile_count)
    wanted = jnp.arange(row_count, dtype=jnp.int32)[:, None] * col_count + column
    wanted = (wanted * capacity + jnp.arange(capacity, dtype=jnp.int32)[None, :]).reshape(1, -1, 1)
    found = (near_codes // POSITIONS) == wanted
    got_place = jnp.sum(jnp.where(found, near_codes % POSITIONS + 1, 0), axis=2) - 1
    got_place = got_place.reshape(col_count, row_count, capacity).transpose(1, 0, 2)
    got_place = got_place.reshape(row_count, plane_slots, 1)
    at_place = got_place == jnp.arange(POSITIONS, dtype=jnp.int32)[None, None, :]

    def entries_of(table):
        entry = jnp.sum(jnp.where(at_place, table[:, None, :] + 1, 0), axis=2) - 1
        return entry.reshape(-1)

    first_index, second_index = entries_of(first_at), entries_of(second_at)
    first_at, second_at = first_at.reshape(-1), second_at.reshape(-1)

    segments = [
        (1, [8, 8, 16, 16]),
        (2, [16, 16, 16]),
        (3, [16, 16, 16]),
        (4, [16] * 5),
        (4, [16] * 4 + [8, 4, 4]),
    ]
    low = 0
    first, second = [], []
    for parts, sizes in segments:
        one, other = listed_sums(got[:parts], first_index, second_index, low, sizes)
        first += one
        second += other
        low += sum(sizes)
    main_entries = low
    chunks, token = chain_sums(first, second, first_index)

    half = row_count // 2
    sizes = [chunk.shape[0] for chunk in first]
    bounds = [sum(sizes[:at]) for at in range(len(sizes) + 1)]
    early = bounds.index(half * POSITIONS)
    late = bounds.index(earliest[half])
    early_rows, late_rows = tuple(range(half)), tuple(range(half, row_count))
    common = (at_end, first_at, second_at, slabs)
    partial = contracted_rows(
        early_rows, *common, [part[:early] for part in chunks], 0, None, jnp.float32
    )
    chunks = [part[late:] for part in chunks]

    def finish(near, across, outward):
        return contracted_rows(
            late_rows, *common, (near, across, outward), earliest[half], partial, density.dtype
        )

    def with_rest(near, across, outward):
        rest = all_entries - main_entries
        sizes = [16] * (rest // 16 - 1) + [8, 8]
        one, other = listed_sums(got, first_index, second_index, main_entries, sizes)
        more, _ = chain_sums(one, other, first_index)
        return finish(near + more[0], across + more[1], outward + more[2])

    return lax.cond(needed <= main_entries, finish, with_rest, *chunks)


def solution(mesh):
    in_specs = (
        P(("row", "col"), None, None),
        P(("row", "col"), None),
        P(("row", "col")),
        P("col", "row"),
    )
    out_specs = P("col", "row")
    on_device = on_device_chain if mesh.shape["row"] == STEPS else on_device_ring
    return jax.shard_map(
        on_device, mesh=mesh, in_specs=in_specs, out_specs=out_specs, check_vma=False
    )
```

time: 522 us -> 741 us (1.42)
  Pallas kernels: 0 us -> 372 us
  waiting for transfers between devices: 347 us -> 92.2 us
  starting transfers between devices: 23.5 us -> 172 us
  matrix products: 74.5 us -> 0.42 us
  blocking collectives: 0 us -> 58.5 us
  local copies, waits for them, and re-layouts: 60.5 us -> 6.8 us
  other arithmetic: 10.7 us -> 33.2 us
    pallas_call x0 -> x11, Pallas kernels: none -> 372 us  [the longest x4 261 us: picked(): pl.pallas_call(kernel, out_shape=jax.ShapeDtypeStruct((count,) + tiles.sh...]
    all_to_all x2 -> x4, waiting for transfers between devices: 185 us -> 0.01 us  [on_device_chain(): lax.all_to_all(sent, 'col', split_axis=0, concat_axis=0, tiled=True)]
    ppermute x6 -> x3, waiting for transfers between devices: 162 us -> 0.01 us  [passed_along(): return lax.ppermute(value, axis, pairs)]
    ppermute x0 -> x66, starting transfers between devices: none -> 154 us  [the longest x22 107 us: chain_sums(): inward[sent] = lax.ppermute(held['sent'], 'row', INWARD)]
    ppermute x0 -> x66, waiting for transfers between devices: none -> 92.1 us  [the longest x22 64.7 us: chain_sums(): lax.ppermute(added(second[back], held['across']), 'row', OUTWARD)]
    dot_general x5 -> x1, matrix products: 74.5 us -> 0.42 us  [on_device_chain(): jnp.einsum('ptn,pqn->ptq', by_target.astype(jnp.bfloat16), by_place.astyp...]
    all_gather x0 -> x1, blocking collectives: none -> 58.5 us  [on_device_chain(): lax.all_gather(slot_of * POSITIONS + tile_place, ('row', 'col'), tiled=True)]
    convert_element_type x0 -> x45, other arithmetic: none -> 27 us  [the longest x44 27 us: added(): (one.astype(jnp.float32) + other.astype(jnp.float32)).astype(one.dtype)]
  transfers between devices with their start and end apart: 8 -> 73, of which waited for: 5 -> 21; matrix products, arithmetic and copies ran while one was open for 12% -> 4% of each run, Pallas kernels for 0% -> 34%
where the time goes in v1:
time: 741 us; the launch traced here: 739 us
  Pallas kernels  372 us (50%)
  starting transfers between devices  172 us (23%)
  waiting for transfers between devices  92.2 us (12%)
  blocking collectives  58.5 us (8%)
  other arithmetic  33.2 us (4%)
    pallas_call x4, Pallas kernels, picked(): pl.pallas_call(kernel, out_shape=jax.ShapeDtypeStruct((count,) + tiles.sh...  261 us
    ppermute x22, starting transfers between devices, chain_sums(): inward[sent] = lax.ppermute(held['sent'], 'row', INWARD)  107 us
    ppermute x22, waiting for transfers between devices, chain_sums(): lax.ppermute(added(second[back], held['across']), 'row', OUTWARD)  64.7 us
    pallas_call x5, Pallas kernels, listed_sums(): pl.pallas_call(kernel, out_shape=[jax.ShapeDtypeStruct((size,) + tile, go...  58.6 us
    all_gather x1, blocking collectives, on_device_chain(): lax.all_gather(slot_of * POSITIONS + tile_place, ('row', 'col'), tiled=True)  58.5 us
    pallas_call x2, Pallas kernels, contracted_rows(): pl.pallas_call(kernel, out_shape=jax.ShapeDtypeStruct((ROW_BLOCKS_DEV * t...  52.3 us
    ppermute x22, starting transfers between devices, chain_sums(): lax.ppermute(added(second[back], held['across']), 'row', OUTWARD)  29.3 us
    ppermute x22, waiting for transfers between devices, chain_sums(): inward[sent] = lax.ppermute(held['sent'], 'row', INWARD)  27.4 us
  transfers between devices with their start and end apart: 73, of which 21 were waited for; matrix products, arithmetic and copies ran while one was open for 4% of the time, Pallas kernels for 34%

profile of v1, /device:TPU:0, one launch (start us, length us, event | category | flops | bytes accessed | tf_op | source)
XLA Modules:
  0.0 738.6 jit_solution(4680951467807137079)
XLA Ops:
  2.4 65.3 %pick_tiles.5 = bf16[64,128,128]{2,1,0:T(8,128)(2,1)} custom-call(s32[64]{0:T(128)} %get-tuple-element.676.source_ref, bf16[128,128,128]{2,1,0:T(8,128)(2,1)} %tiles_ref.7), custom_call_target="tpu_custom_call" | custom-call | tf_op jit(solution)/shard_map/pick_tiles/pallas_call | solution.py:90
  73.0 58.5 %all-gather = s32[32,1,128]{2,1,0:T(1,128)S(1)} all-gather(s32[1,1,128]{2,1,0:T(1,128)S(1)} %get-tuple-element.663), channel_id=1, replica_groups=mesh['row'=4,'col'=8] {'row','col'}, dimensions={0}, use_global_device_ids=true | all-gather | bytes 16896 | tf_op jit(solution)/shard_map/all_gather | solution.py:347
  133.2 65.3 %pick_tiles.4 = bf16[64,128,128]{2,1,0:T(8,128)(2,1)} custom-call(s32[64]{0:T(128)} %get-tuple-element.677.source_ref, bf16[128,128,128]{2,1,0:T(8,128)(2,1)} %tiles_ref.7), custom_call_target="tpu_custom_call" | custom-call | tf_op jit(solution)/shard_map/pick_tiles/pallas_call | solution.py:90
  205.8 5.5 sum_tiles.9
  212.7 6.6 collective-permute-done.19
  225.7 65.3 %pick_tiles.6 = bf16[64,128,128]{2,1,0:T(8,128)(2,1)} custom-call(s32[64]{0:T(128)} %get-tuple-element.675.source_ref, bf16[128,128,128]{2,1,0:T(8,128)(2,1)} %tiles_ref.7), custom_call_target="tpu_custom_call" | custom-call | tf_op jit(solution)/shard_map/pick_tiles/pallas_call | solution.py:90
  299.8 65.4 %pick_tiles.7 = bf16[64,128,128]{2,1,0:T(8,128)(2,1)} custom-call(s32[64]{0:T(128)} %get-tuple-element.674.source_ref, bf16[128,128,128]{2,1,0:T(8,128)(2,1)} %tiles_ref.7), custom_call_target="tpu_custom_call" | custom-call | tf_op jit(solution)/shard_map/pick_tiles/pallas_call | solution.py:90
  367.1 9.3 %sum_tiles.8 = (bf16[16,128,128]{2,1,0:T(8,128)(2,1)}, bf16[16,128,128]{2,1,0:T(8,128)(2,1)}, bf16[16,128,128]{2,1,0:T(8,128)(2,1)}, bf16[16,128,128]{2,1,0:T(8,...) custom-call(s32[256]{0:T(256)S(1)} %sub.33.first_ref, s32[256]{0:T(256)S(1)} %sub.35.second_ref, ...), custom_call_target="tpu_custom_call" | custom-call | tf_op jit(solution)/shard_map/sum_tiles/pallas_call | solution.py:148
  389.1 10.8 %collective-permute-done.29.refs_26_ = bf16[8,128,128]{2,1,0:T(8,128)(2,1)S(1)} collective-permute-done((bf16[8,128,128]{2,1,0:T(8,128)(2,1)S(1)}, bf16[8,128,128]{2,1,0:T(8,128)(2,1)S(1)}, u32[]{:S(2)}, u32[]{:S(2)}) %collective-permute-start.29) | collective-permute-done | bytes 262176 | tf_op jit(solution)/shard_map/ppermute | solution.py:192
  413.4 11.9 %sum_tiles.7 = (bf16[16,128,128]{2,1,0:T(8,128)(2,1)}, bf16[16,128,128]{2,1,0:T(8,128)(2,1)}, bf16[16,128,128]{2,1,0:T(8,128)(2,1)}, bf16[16,128,128]{2,1,0:T(8,...) custom-call(s32[256]{0:T(256)S(1)} %sub.33.first_ref, s32[256]{0:T(256)S(1)} %sub.35.second_ref, ...), custom_call_target="tpu_custom_call" | custom-call | tf_op jit(solution)/shard_map/sum_tiles/pallas_call | solution.py:148
  428.8 6.2 collective-permute-start.31
  436.5 5.4 collective-permute-done.35.refs_28_
  453.3 8.5 %collective-permute-start.40 = (bf16[16,128,128]{2,1,0:T(8,128)(2,1)}, bf16[16,128,128]{2,1,0:T(8,128)(2,1)}, u32[]{:S(2)}, u32[]{:S(2)}) collective-permute-start(bf16[16,128,128]{2,1,0:T(8,128)(2,1)} %get-tuple-element.559), channel_id=1, source_target_pairs={{0,8},{24,16},{1,9},{25,17},{2,10},{26,18},{3,11},{27,19},{4,12},{... | collective-permute-start | bytes 1572872 | tf_op jit(solution)/shard_map/ppermute | solution.py:185
  464.9 16.0 %sum_tiles.10 = (bf16[16,128,128]{2,1,0:T(8,128)(2,1)}, bf16[16,128,128]{2,1,0:T(8,128)(2,1)}, bf16[16,128,128]{2,1,0:T(8,128)(2,1)}, bf16[16,128,128]{2,1,0:T(8...) custom-call(s32[256]{0:T(256)S(1)} %sub.33.first_ref, ...), custom_call_target="tpu_custom_call" | custom-call | tf_op jit(solution)/shard_map/sum_tiles/pallas_call | solution.py:148
  483.2 7.0 collective-permute-start.43
  493.9 7.6 %collective-permute-start.46 = (bf16[16,128,128]{2,1,0:T(8,128)(2,1)S(1)}, bf16[16,128,128]{2,1,0:T(8,128)(2,1)S(1)}, u32[]{:S(2)}, u32[]{:S(2)}) collective-permute-start(bf16[16,128,128]{2,1,0:T(8,128)(2,1)S(1)} %copy-done.95), channel_id=1, source_target_pairs={{0,8},{24,16},{1,9},{25,17},{2,10},{26,18},{3,11},{27,19},{4,12},{... | collective-permute-start | bytes 1572872 | tf_op jit(solution)/shard_map/ppermute | solution.py:185
  521.9 8.3 %collective-permute-start.52 = (bf16[16,128,128]{2,1,0:T(8,128)(2,1)}, bf16[16,128,128]{2,1,0:T(8,128)(2,1)}, u32[]{:S(2)}, u32[]{:S(2)}) collective-permute-start(bf16[16,128,128]{2,1,0:T(8,128)(2,1)} %get-tuple-element.579), channel_id=1, source_target_pairs={{0,8},{24,16},{1,9},{25,17},{2,10},{26,18},{3,11},{27,19},{4,12},{... | collective-permute-start | bytes 1572872 | tf_op jit(solution)/shard_map/ppermute | solution.py:185
  532.3 15.9 %sum_tiles.11 = (bf16[16,128,128]{2,1,0:T(8,128)(2,1)}, bf16[16,128,128]{2,1,0:T(8,128)(2,1)}, bf16[16,128,128]{2,1,0:T(8,128)(2,1)}, bf16[16,128,128]{2,1,0:T(8...) custom-call(s32[256]{0:T(256)S(1)} %sub.33.first_ref, ...), custom_call_target="tpu_custom_call" | custom-call | tf_op jit(solution)/shard_map/sum_tiles/pallas_call | solution.py:148
  550.5 7.1 collective-permute-start.55
  562.5 7.5 %collective-permute-start.58 = (bf16[16,128,128]{2,1,0:T(8,128)(2,1)S(1)}, bf16[16,128,128]{2,1,0:T(8,128)(2,1)S(1)}, u32[]{:S(2)}, u32[]{:S(2)}) collective-permute-start(bf16[16,128,128]{2,1,0:T(8,128)(2,1)S(1)} %copy-done.92), channel_id=1, source_target_pairs={{0,8},{24,16},{1,9},{25,17},{2,10},{26,18},{3,11},{27,19},{4,12},{... | collective-permute-start | bytes 1572872 | tf_op jit(solution)/shard_map/ppermute | solution.py:185
  585.9 7.5 %collective-permute-start.64 = (bf16[16,128,128]{2,1,0:T(8,128)(2,1)S(1)}, bf16[16,128,128]{2,1,0:T(8,128)(2,1)S(1)}, u32[]{:S(2)}, u32[]{:S(2)}) collective-permute-start(bf16[16,128,128]{2,1,0:T(8,128)(2,1)S(1)} %copy-done.85), channel_id=1, source_target_pairs={{0,8},{24,16},{1,9},{25,17},{2,10},{26,18},{3,11},{27,19},{4,12},{... | collective-permute-start | bytes 1572872 | tf_op jit(solution)/shard_map/ppermute | solution.py:185
  596.0 7.6 %collective-permute-done.64 = bf16[16,128,128]{2,1,0:T(8,128)(2,1)S(1)} collective-permute-done((bf16[16,128,128]{2,1,0:T(8,128)(2,1)S(1)}, bf16[16,128,128]{2,1,0:T(8,128)(2,1)S(1)}, u32[]{:S(2)}, u32[]{:S(2)}) %collective-permute-start.64) | collective-permute-done | bytes 524320 | tf_op jit(solution)/shard_map/ppermute | solution.py:185
  613.3 6.4 collective-permute-start.70
  619.8 6.5 collective-permute-done.68
  627.3 6.7 collective-permute-done.71
  637.3 5.4 collective-permute-start.73
  645.9 6.4 collective-permute-start.76
  662.3 6.9 collective-permute-done.81
  671.3 6.4 collective-permute-done.79
  685.6 24.8 %contract_panels.5 = f32[3072,2048]{1,0:T(8,128)} custom-call(s32[2]{0:T(128)} %pad_add_fusion.2.place_ref, s32[384]{0:T(512)S(1)} %select_n.119.first_ref, s32[384]{0:T(512)S(1)} %select_n.120.second_ref, bf16[8,128,128]{2,1,0:T(8,128)(2,1)} %copy-done.54, bf16[8,128,128]{2,1,0:T(8,128)(2,1)} %copy-done.56, bf16[16,128,128]{2,1,0:T(8,128)(2,1)} %copy-done.33, ...), custom_call_target="tpu_custom_call" | custom-call | flops 12884901888 | bytes 12582912 | tf_op jit(solution)/shard_map/contract_panels/pallas_call | solution.py:304
  710.3 28.1 %conditional.1 = (bf16[3072,2048]{1,0:T(8,128)(2,1)}) conditional(s32[]{:T(128)} %convert_element_type.521, (s32[]{:T(128)}, s32[256]{0:T(256)S(1)}, s32[256]{0:T(256)S(1)}, bf16[64,128,128]{2,1,0:T(8,128)(2,1)S(1)}, bf16[64,128,128]{2,1,0:T(8,128)(2,1)}, /*index=5*/bf16[64,128,128]{2,1,0:T(8,128)(2,1)}, bf16[64,128,128]{2,1,0:T(8,128)(2,1)}, ...), branch_computations={%region_10.11_spmd, %region_11.12_spmd} | conditional | flops 12895387648 | bytes 120587776 | solution.py:450
  711.0 27.5 %contract_panels.4 = bf16[3072,2048]{1,0:T(8,128)(2,1)} custom-call(s32[2]{0:T(128)} %pad_add_fusion.1.place_ref, s32[384]{0:T(512)S(1)} %get-tuple-element.325.first_ref, s32[384]{0:T(512)S(1)} %get-tuple-element.326.second_ref, bf16[16,128,128]{2,1,0:T(8,128)(2,1)S(1)} %get-tuple-element.327.refs_0_, bf16[16,128,128]{2,1,0:T(8,128)(2,1)} %get-tuple-element.328.refs_1_, ...), custom_call_target="tpu_custom_call" | custom-call | flops 12884901888 | bytes 13631488 | tf_op jit(solution)/shard_map/cond/branch_1_fun/contract_panels/pallas_call | solution.py:304
  (406 shorter events, 170.3 us)
Async XLA Ops:
  67.7 131.6 %all-to-all-start = ((bf16[64,128,128]{2,1,0:T(8,128)(2,1)}), bf16[64,128,128]{2,1,0:T(8,128)(2,1)S(1)}, u32[]{:S(2)}, u32[]{:S(2)}) async-start(bf16[64,128,128]{2,1,0:T(8,128)(2,1)} %pick_tiles.5), calls=%async_computation | async-start | bytes 4194304 | tf_op jit(solution)/shard_map/all_to_all | solution.py:353
  199.3 91.7 %all-to-all-start.1 = ((bf16[64,128,128]{2,1,0:T(8,128)(2,1)}), bf16[64,128,128]{2,1,0:T(8,128)(2,1)}, u32[]{:S(2)}, u32[]{:S(2)}) async-start(bf16[64,128,128]{2,1,0:T(8,128)(2,1)} %pick_tiles.4), calls=%async_computation.1 | async-start | bytes 4194304 | tf_op jit(solution)/shard_map/all_to_all | solution.py:353
  219.3 157.2 %collective-permute-start.23 = (bf16[16,128,128]{2,1,0:T(8,128)(2,1)}, bf16[16,128,128]{2,1,0:T(8,128)(2,1)}, u32[]{:S(2)}, u32[]{:S(2)}) collective-permute-start(bf16[16,128,128]{2,1,0:T(8,128)(2,1)} %get-tuple-element.531), channel_id=1, source_target_pairs={{0,8},{24,16},{1,9},{25,17},{2,10},{26,18},{3,11},{27,19},{4,12},{... | collective-permute-start | bytes 1572872 | tf_op jit(solution)/shard_map/ppermute | solution.py:185
  224.4 72.9 %collective-permute-start.18 = (bf16[8,128,128]{2,1,0:T(8,128)(2,1)}, bf16[8,128,128]{2,1,0:T(8,128)(2,1)S(1)}, u32[]{:S(2)}, u32[]{:S(2)}) collective-permute-start(bf16[8,128,128]{2,1,0:T(8,128)(2,1)} %get-tuple-element.524), channel_id=1, source_target_pairs={{0,8},{24,16},{1,9},{25,17},{2,10},{26,18},{3,11},{27,19},{4,12},{... | collective-permute-start | bytes 786440 | tf_op jit(solution)/shard_map/ppermute | solution.py:185
  291.0 118.0 %all-to-all-start.2 = ((bf16[64,128,128]{2,1,0:T(8,128)(2,1)}), bf16[64,128,128]{2,1,0:T(8,128)(2,1)}, u32[]{:S(2)}, u32[]{:S(2)}) async-start(bf16[64,128,128]{2,1,0:T(8,128)(2,1)} %pick_tiles.6), calls=%async_computation.2 | async-start | bytes 4194304 | tf_op jit(solution)/shard_map/all_to_all | solution.py:353
  296.5 79.9 %collective-permute-start.22 = (bf16[8,128,128]{2,1,0:T(8,128)(2,1)S(1)}, bf16[8,128,128]{2,1,0:T(8,128)(2,1)S(1)}, u32[]{:S(2)}, u32[]{:S(2)}) collective-permute-start(bf16[8,128,128]{2,1,0:T(8,128)(2,1)S(1)} %add_convert_fusion.51.refs_0_), channel_id=1, source_target_pairs={{8,16},{16,8},{9,17},{17,9},{10,18},{18,10},{11,19},{19,11},{12,20... | collective-permute-start | bytes 786440 | tf_op jit(solution)/shard_map/ppermute | solution.py:188
  297.3 81.2 %collective-permute-start.21 = (bf16[16,128,128]{2,1,0:T(8,128)(2,1)S(1)}, bf16[16,128,128]{2,1,0:T(8,128)(2,1)}, u32[]{:S(2)}, u32[]{:S(2)}) collective-permute-start(bf16[16,128,128]{2,1,0:T(8,128)(2,1)S(1)} %copy-done.94), channel_id=1, source_target_pairs={{0,8},{24,16},{1,9},{25,17},{2,10},{26,18},{3,11},{27,19},{4,12},{... | collective-permute-start | bytes 1572872 | tf_op jit(solution)/shard_map/ppermute | solution.py:185
  377.8 24.3 %collective-permute-start.27 = (bf16[16,128,128]{2,1,0:T(8,128)(2,1)S(1)}, bf16[16,128,128]{2,1,0:T(8,128)(2,1)S(1)}, u32[]{:S(2)}, u32[]{:S(2)}) collective-permute-start(bf16[16,128,128]{2,1,0:T(8,128)(2,1)S(1)} %add_convert_fusion.45.refs_2_), channel_id=1, source_target_pairs={{8,16},{16,8},{9,17},{17,9},{10,18},{18,10},{11,19},{19,11},{12,20... | collective-permute-start | bytes 1572872 | tf_op jit(solution)/shard_map/ppermute | solution.py:188
  378.5 23.6 %collective-permute-start.28 = (bf16[16,128,128]{2,1,0:T(8,128)(2,1)}, bf16[16,128,128]{2,1,0:T(8,128)(2,1)S(1)}, u32[]{:S(2)}, u32[]{:S(2)}) collective-permute-start(bf16[16,128,128]{2,1,0:T(8,128)(2,1)} %get-tuple-element.538), channel_id=1, source_target_pairs={{0,8},{24,16},{1,9},{25,17},{2,10},{26,18},{3,11},{27,19},{4,12},{... | collective-permute-start | bytes 1572872 | tf_op jit(solution)/shard_map/ppermute | solution.py:185
  384.4 40.9 %collective-permute-start.26 = (bf16[8,128,128]{2,1,0:T(8,128)(2,1)}, bf16[8,128,128]{2,1,0:T(8,128)(2,1)S(1)}, u32[]{:S(2)}, u32[]{:S(2)}) collective-permute-start(bf16[8,128,128]{2,1,0:T(8,128)(2,1)} %add_convert_fusion.49), channel_id=1, source_target_pairs={{8,0},{16,24},{9,1},{17,25},{10,2},{18,26},{11,3},{19,27},{12,4},{... | collective-permute-start | bytes 786440 | tf_op jit(solution)/shard_map/ppermute | solution.py:192
  388.4 38.2 %collective-permute-start.24 = (bf16[16,128,128]{2,1,0:T(8,128)(2,1)S(1)}, bf16[16,128,128]{2,1,0:T(8,128)(2,1)S(1)}, u32[]{:S(2)}, u32[]{:S(2)}) collective-permute-start(bf16[16,128,128]{2,1,0:T(8,128)(2,1)S(1)} %add_convert_fusion.44.refs_3_), channel_id=1, source_target_pairs={{8,16},{16,8},{9,17},{17,9},{10,18},{18,10},{11,19},{19,11},{12,20... | collective-permute-start | bytes 1572872 | tf_op jit(solution)/shard_map/ppermute | solution.py:188
  399.8 26.7 %collective-permute-start.25 = (bf16[16,128,128]{2,1,0:T(8,128)(2,1)}, bf16[16,128,128]{2,1,0:T(8,128)(2,1)}, u32[]{:S(2)}, u32[]{:S(2)}) collective-permute-start(bf16[16,128,128]{2,1,0:T(8,128)(2,1)} %get-tuple-element.535), channel_id=1, source_target_pairs={{0,8},{24,16},{1,9},{25,17},{2,10},{26,18},{3,11},{27,19},{4,12},{... | collective-permute-start | bytes 1572872 | tf_op jit(solution)/shard_map/ppermute | solution.py:185
  403.1 32.1 %collective-permute-start.33 = (bf16[16,128,128]{2,1,0:T(8,128)(2,1)}, bf16[16,128,128]{2,1,0:T(8,128)(2,1)}, u32[]{:S(2)}, u32[]{:S(2)}) collective-permute-start(bf16[16,128,128]{2,1,0:T(8,128)(2,1)} %add_convert_fusion.43.refs_4_), channel_id=1, source_target_pairs={{8,16},{16,8},{9,17},{17,9},{10,18},{18,10},{11,19},{19,11},{12,20... | collective-permute-start | bytes 1572872 | tf_op jit(solution)/shard_map/ppermute | solution.py:188
  404.5 32.0 %collective-permute-start.34 = (bf16[16,128,128]{2,1,0:T(8,128)(2,1)}, bf16[16,128,128]{2,1,0:T(8,128)(2,1)}, u32[]{:S(2)}, u32[]{:S(2)}) collective-permute-start(bf16[16,128,128]{2,1,0:T(8,128)(2,1)} %get-tuple-element.548), channel_id=1, source_target_pairs={{0,8},{24,16},{1,9},{25,17},{2,10},{26,18},{3,11},{27,19},{4,12},{... | collective-permute-start | bytes 1572872 | tf_op jit(solution)/shard_map/ppermute | solution.py:185
  409.0 55.9 %all-to-all-start.3 = ((bf16[64,128,128]{2,1,0:T(8,128)(2,1)}), bf16[64,128,128]{2,1,0:T(8,128)(2,1)}, u32[]{:S(2)}, u32[]{:S(2)}) async-start(bf16[64,128,128]{2,1,0:T(8,128)(2,1)} %pick_tiles.7), calls=%async_computation.3 | async-start | bytes 4194304 | tf_op jit(solution)/shard_map/all_to_all | solution.py:353
  428.1 22.4 %collective-permute-start.30 = (bf16[16,128,128]{2,1,0:T(8,128)(2,1)S(1)}, bf16[16,128,128]{2,1,0:T(8,128)(2,1)S(1)}, u32[]{:S(2)}, u32[]{:S(2)}) collective-permute-start(bf16[16,128,128]{2,1,0:T(8,128)(2,1)S(1)} %add_convert_fusion.42.refs_5_), channel_id=1, source_target_pairs={{8,16},{16,8},{9,17},{17,9},{10,18},{18,10},{11,19},{19,11},{12,20... | collective-permute-start | bytes 1572872 | tf_op jit(solution)/shard_map/ppermute | solution.py:188
  428.8 23.0 %collective-permute-start.31 = (bf16[16,128,128]{2,1,0:T(8,128)(2,1)}, bf16[16,128,128]{2,1,0:T(8,128)(2,1)S(1)}, u32[]{:S(2)}, u32[]{:S(2)}) collective-permute-start(bf16[16,128,128]{2,1,0:T(8,128)(2,1)} %get-tuple-element.544), channel_id=1, source_target_pairs={{0,8},{24,16},{1,9},{25,17},{2,10},{26,18},{3,11},{27,19},{4,12},{... | collective-permute-start | bytes 1572872 | tf_op jit(solution)/shard_map/ppermute | solution.py:185
  444.8 36.2 %collective-permute-start.37 = (bf16[16,128,128]{2,1,0:T(8,128)(2,1)}, bf16[16,128,128]{2,1,0:T(8,128)(2,1)}, u32[]{:S(2)}, u32[]{:S(2)}) collective-permute-start(bf16[16,128,128]{2,1,0:T(8,128)(2,1)} %get-tuple-element.554), channel_id=1, source_target_pairs={{0,8},{24,16},{1,9},{25,17},{2,10},{26,18},{3,11},{27,19},{4,12},{... | collective-permute-start | bytes 1572872 | tf_op jit(solution)/shard_map/ppermute | solution.py:185
  450.6 30.4 %collective-permute-start.38 = (bf16[16,128,128]{2,1,0:T(8,128)(2,1)}, bf16[16,128,128]{2,1,0:T(8,128)(2,1)}, u32[]{:S(2)}, u32[]{:S(2)}) collective-permute-start(bf16[16,128,128]{2,1,0:T(8,128)(2,1)} %add_convert_fusion.37), channel_id=1, source_target_pairs={{8,0},{16,24},{9,1},{17,25},{10,2},{18,26},{11,3},{19,27},{12,4},{... | collective-permute-start | bytes 1572872 | tf_op jit(solution)/shard_map/ppermute | solution.py:192
  452.6 30.5 %collective-permute-start.39 = (bf16[16,128,128]{2,1,0:T(8,128)(2,1)S(1)}, bf16[16,128,128]{2,1,0:T(8,128)(2,1)S(1)}, u32[]{:S(2)}, u32[]{:S(2)}) collective-permute-start(bf16[16,128,128]{2,1,0:T(8,128)(2,1)S(1)} %add_convert_fusion.38.refs_7_), channel_id=1, source_target_pairs={{8,16},{16,8},{9,17},{17,9},{10,18},{18,10},{11,19},{19,11},{12,20... | collective-permute-start | bytes 1572872 | tf_op jit(solution)/shard_map/ppermute | solution.py:188
  453.3 29.8 %collective-permute-start.40 = (bf16[16,128,128]{2,1,0:T(8,128)(2,1)}, bf16[16,128,128]{2,1,0:T(8,128)(2,1)}, u32[]{:S(2)}, u32[]{:S(2)}) collective-permute-start(bf16[16,128,128]{2,1,0:T(8,128)(2,1)} %get-tuple-element.559), channel_id=1, source_target_pairs={{0,8},{24,16},{1,9},{25,17},{2,10},{26,18},{3,11},{27,19},{4,12},{... | collective-permute-start | bytes 1572872 | tf_op jit(solution)/shard_map/ppermute | solution.py:185
  483.2 19.7 %collective-permute-start.43 = (bf16[16,128,128]{2,1,0:T(8,128)(2,1)}, bf16[16,128,128]{2,1,0:T(8,128)(2,1)S(1)}, u32[]{:S(2)}, u32[]{:S(2)}) collective-permute-start(bf16[16,128,128]{2,1,0:T(8,128)(2,1)} %get-tuple-element.564), channel_id=1, source_target_pairs={{0,8},{24,16},{1,9},{25,17},{2,10},{26,18},{3,11},{27,19},{4,12},{... | collective-permute-start | bytes 1572872 | tf_op jit(solution)/shard_map/ppermute | solution.py:185
  502.9 59.6 %collective-permute-start.84 = (bf16[512,2048]{1,0:T(8,128)(2,1)S(1)}, bf16[512,2048]{1,0:T(8,128)(2,1)S(1)}, u32[]{:S(2)}, u32[]{:S(2)}) collective-permute-start(bf16[512,2048]{1,0:T(8,128)(2,1)S(1)} %copy-done), channel_id=1, source_target_pairs={{0,7},{1,0},{2,1},{3,2},{4,3},{5,4},{6,5},{7,6},{8,15},{9,8},{10,9... | collective-permute-start | bytes 6291464 | tf_op jit(solution)/shard_map/ppermute | solution.py:26
  517.4 30.8 %collective-permute-start.50 = (bf16[16,128,128]{2,1,0:T(8,128)(2,1)}, bf16[16,128,128]{2,1,0:T(8,128)(2,1)}, u32[]{:S(2)}, u32[]{:S(2)}) collective-permute-start(bf16[16,128,128]{2,1,0:T(8,128)(2,1)} %add_convert_fusion.29), channel_id=1, source_target_pairs={{8,0},{16,24},{9,1},{17,25},{10,2},{18,26},{11,3},{19,27},{12,4},{... | collective-permute-start | bytes 1572872 | tf_op jit(solution)/shard_map/ppermute | solution.py:192
  518.7 31.7 %collective-permute-start.51 = (bf16[16,128,128]{2,1,0:T(8,128)(2,1)}, bf16[16,128,128]{2,1,0:T(8,128)(2,1)}, u32[]{:S(2)}, u32[]{:S(2)}) collective-permute-start(bf16[16,128,128]{2,1,0:T(8,128)(2,1)} %add_convert_fusion.30.refs_11_), channel_id=1, source_target_pairs={{8,16},{16,8},{9,17},{17,9},{10,18},{18,10},{11,19},{19,11},{12,20... | collective-permute-start | bytes 1572872 | tf_op jit(solution)/shard_map/ppermute | solution.py:188
  521.9 28.5 %collective-permute-start.52 = (bf16[16,128,128]{2,1,0:T(8,128)(2,1)}, bf16[16,128,128]{2,1,0:T(8,128)(2,1)}, u32[]{:S(2)}, u32[]{:S(2)}) collective-permute-start(bf16[16,128,128]{2,1,0:T(8,128)(2,1)} %get-tuple-element.579), channel_id=1, source_target_pairs={{0,8},{24,16},{1,9},{25,17},{2,10},{26,18},{3,11},{27,19},{4,12},{... | collective-permute-start | bytes 1572872 | tf_op jit(solution)/shard_map/ppermute | solution.py:185
  549.7 20.4 %collective-permute-start.54 = (bf16[16,128,128]{2,1,0:T(8,128)(2,1)S(1)}, bf16[16,128,128]{2,1,0:T(8,128)(2,1)S(1)}, u32[]{:S(2)}, u32[]{:S(2)}) collective-permute-start(bf16[16,128,128]{2,1,0:T(8,128)(2,1)S(1)} %add_convert_fusion.28.refs_12_), channel_id=1, source_target_pairs={{8,16},{16,8},{9,17},{17,9},{10,18},{18,10},{11,19},{19,11},{12,20... | collective-permute-start | bytes 1572872 | tf_op jit(solution)/shard_map/ppermute | solution.py:188
  550.5 20.9 %collective-permute-start.55 = (bf16[16,128,128]{2,1,0:T(8,128)(2,1)}, bf16[16,128,128]{2,1,0:T(8,128)(2,1)S(1)}, u32[]{:S(2)}, u32[]{:S(2)}) collective-permute-start(bf16[16,128,128]{2,1,0:T(8,128)(2,1)} %get-tuple-element.584), channel_id=1, source_target_pairs={{0,8},{24,16},{1,9},{25,17},{2,10},{26,18},{3,11},{27,19},{4,12},{... | collective-permute-start | bytes 1572872 | tf_op jit(solution)/shard_map/ppermute | solution.py:185
  571.4 40.5 %collective-permute-start.85 = (bf16[512,2048]{1,0:T(8,128)(2,1)S(1)}, bf16[512,2048]{1,0:T(8,128)(2,1)}, u32[]{:S(2)}, u32[]{:S(2)}) collective-permute-start(bf16[512,2048]{1,0:T(8,128)(2,1)S(1)} %collective-permute-done.84.refs_40_), channel_id=1, source_target_pairs={{0,7},{1,0},{2,1},{3,2},{4,3},{5,4},{6,5},{7,6},{8,15},{9,8},{10,9... | collective-permute-start | bytes 6291464 | tf_op jit(solution)/shard_map/ppermute | solution.py:26
  611.9 22.1 %collective-permute-start.71 = (bf16[16,128,128]{2,1,0:T(8,128)(2,1)S(1)}, bf16[16,128,128]{2,1,0:T(8,128)(2,1)S(1)}, u32[]{:S(2)}, u32[]{:S(2)}) collective-permute-start(bf16[16,128,128]{2,1,0:T(8,128)(2,1)S(1)} %add_convert_fusion.15), channel_id=1, source_target_pairs={{8,0},{16,24},{9,1},{17,25},{10,2},{18,26},{11,3},{19,27},{12,4},{... | collective-permute-start | bytes 1572872 | tf_op jit(solution)/shard_map/ppermute | solution.py:192
  619.7 65.8 %collective-permute-start.86 = (bf16[512,2048]{1,0:T(8,128)(2,1)}, bf16[512,2048]{1,0:T(8,128)(2,1)}, u32[]{:S(2)}, u32[]{:S(2)}) collective-permute-start(bf16[512,2048]{1,0:T(8,128)(2,1)} %collective-permute-done.85.refs_41_), channel_id=1, source_target_pairs={{0,7},{1,0},{2,1},{3,2},{4,3},{5,4},{6,5},{7,6},{8,15},{9,8},{10,9... | collective-permute-start | bytes 6291464 | tf_op jit(solution)/shard_map/ppermute | solution.py:26
  635.8 22.2 %collective-permute-start.77 = (bf16[16,128,128]{2,1,0:T(8,128)(2,1)S(1)}, bf16[16,128,128]{2,1,0:T(8,128)(2,1)}, u32[]{:S(2)}, u32[]{:S(2)}) collective-permute-start(bf16[16,128,128]{2,1,0:T(8,128)(2,1)S(1)} %add_convert_fusion.13), channel_id=1, source_target_pairs={{8,0},{16,24},{9,1},{17,25},{10,2},{18,26},{11,3},{19,27},{12,4},{... | collective-permute-start | bytes 1572872 | tf_op jit(solution)/shard_map/ppermute | solution.py:192
  (138 other events, 2148.2 us)

commit v2 on v0

v2 whole, which is shorter than its diff:
```python
import functools

import jax
import jax.numpy as jnp
from jax import lax
from jax.experimental import pallas as pl
from jax.experimental.pallas import tpu as pltpu
from jax.sharding import PartitionSpec as P

ROW_BLOCKS_DEV = 24
K_BLOCKS = 4
STEPS = 4
POSITIONS = 96

INWARD = [(0, 1), (3, 2)]
ACROSS = [(1, 2), (2, 1)]
OUTWARD = [(1, 0), (2, 3)]
LAG = 2

CHUNK = 24
ALONE, ONE_BEFORE, FIRST_PAIR, LAST_PAIR = 24, 72, 120, 192
LIST_ENTRIES = FIRST_PAIR + LAST_PAIR
NOWHERE = 1 << 15
ROW_TILE = 4
SUM_VMEM_BYTES = 56 * 1024 * 1024
CONTRACT_VMEM_BYTES = 44 * 1024 * 1024
SMALL = pl.CostEstimate(flops=1000, bytes_accessed=1000, transcendentals=0)


def passed_along(value, axis, steps):
    count = lax.axis_size(axis)
    pairs = [(source, (source + steps) % count) for source in range(count)]
    return lax.ppermute(value, axis, pairs)


def tile_capacity(tile_count, devices):
    return max(2, (2 * tile_count + devices - 1) // devices)


def ranks_of(targets):
    order = jnp.arange(targets.shape[0], dtype=jnp.int32)
    same_target = targets[:, None] == targets[None, :]
    earlier = order[None, :] < order[:, None]
    return jnp.sum((same_target & earlier).astype(jnp.int32), axis=1)


def on_device_ring(tiles, tile_target, tile_place, density):
    row_count = lax.axis_size("row")
    col_count = lax.axis_size("col")
    devices = row_count * col_count
    tile_count = tiles.shape[0]
    tile_size = tiles.shape[1]
    capacity = tile_capacity(tile_count, devices)
    slots = devices * capacity
    targets = tile_target[:, 0]
    order = jnp.arange(tile_count, dtype=jnp.int32)
    slot_of = targets * capacity + ranks_of(targets)
    hits = slot_of[None, :] == jnp.arange(slots, dtype=jnp.int32)[:, None]
    filled = jnp.any(hits, axis=1)
    source = jnp.sum(jnp.where(hits, order[None, :], 0), axis=1)
    send_tiles = jnp.take(tiles, source, axis=0)
    send_places = jnp.where(filled, jnp.take(tile_place, source), -1)
    got_tiles, got_places = (
        lax.all_to_all(send_tiles, ("row", "col"), split_axis=0, concat_axis=0, tiled=True),
        lax.all_to_all(send_places, ("row", "col"), split_axis=0, concat_axis=0, tiled=True),
    )
    got_tiles = got_tiles.reshape(slots, tile_size * tile_size)
    selector = (got_places[None, :] == jnp.arange(POSITIONS, dtype=jnp.int32)[:, None]).astype(
        jnp.bfloat16
    )
    dense = jnp.dot(selector, got_tiles, preferred_element_type=jnp.float32)
    dense = dense.reshape(ROW_BLOCKS_DEV, K_BLOCKS, tile_size, tile_size).transpose(0, 2, 1, 3)
    panel = dense.reshape(ROW_BLOCKS_DEV * tile_size, K_BLOCKS * tile_size).astype(jnp.bfloat16)
    total = jnp.zeros((panel.shape[0], density.shape[1]), jnp.float32)
    left, right = (panel, density)
    for offset in range(STEPS):
        total = total + jnp.dot(left, right, preferred_element_type=jnp.float32)
        if offset + 1 < STEPS:
            left = passed_along(left, "row", -1)
            right = passed_along(right, "col", -1)
    return total.astype(jnp.bfloat16)


def picked(tiles, source):
    count = source.shape[0]

    def kernel(source_ref, tiles_ref, out_ref):
        def one(slot, carry):
            out_ref[slot] = tiles_ref[source_ref[slot]]
            return carry

        lax.fori_loop(0, count, one, 0, unroll=4)

    return pl.pallas_call(
        kernel,
        out_shape=jax.ShapeDtypeStruct((count,) + tiles.shape[1:], tiles.dtype),
        grid_spec=pltpu.PrefetchScalarGridSpec(
            num_scalar_prefetch=1,
            grid=(),
            in_specs=[pl.BlockSpec(memory_space=pltpu.VMEM)],
            out_specs=pl.BlockSpec(memory_space=pltpu.VMEM),
        ),
        compiler_params=pltpu.CompilerParams(vmem_limit_bytes=SUM_VMEM_BYTES),
        cost_estimate=SMALL,
        name="pick_tiles",
    )(source, tiles)


def hops_before(chunk):
    at = chunk * CHUNK
    at = at if at < FIRST_PAIR else at - FIRST_PAIR
    return 0 if at < ALONE else 1 if at < ONE_BEFORE else 2


def listed_sums(got, order, bounds, wanted, after):
    tile = got[0].shape[1:]
    slots = got[0].shape[0]
    parts = len(got)
    count = len(wanted)

    def kernel(order_ref, bounds_ref, *refs):
        got_refs, out_refs = refs[:parts], refs[-2 - count : -2]
        held, sems = refs[-2:]
        copies = [
            pltpu.make_async_copy(got_ref, held.at[pl.ds(part * slots, slots)], sems.at[part])
            for part, got_ref in enumerate(got_refs)
        ]
        for copy in copies:
            copy.start()
        for copy in copies:
            copy.wait()
        for (which, chunk), out in zip(wanted, out_refs):

            def total(entry, carry, which=which, chunk=chunk, out=out):
                def add(at, value):
                    return value + held[order_ref[which, at]].astype(jnp.float32)

                at = chunk * CHUNK + entry
                value = lax.fori_loop(
                    bounds_ref[which, at],
                    bounds_ref[which, at + 1],
                    add,
                    jnp.zeros(tile, jnp.float32),
                )
                out[entry] = value.astype(out.dtype)
                return carry

            lax.fori_loop(0, CHUNK, total, 0)

    out = pl.pallas_call(
        kernel,
        out_shape=[jax.ShapeDtypeStruct((CHUNK,) + tile, got[0].dtype)] * count,
        grid_spec=pltpu.PrefetchScalarGridSpec(
            num_scalar_prefetch=2,
            grid=(),
            in_specs=[pl.BlockSpec(memory_space=pl.ANY)] * (parts + len(after)),
            out_specs=[pl.BlockSpec(memory_space=pltpu.VMEM)] * count,
            scratch_shapes=[
                pltpu.VMEM((parts * slots,) + tile, got[0].dtype),
                pltpu.SemaphoreType.DMA((parts,)),
            ],
        ),
        compiler_params=pltpu.CompilerParams(vmem_limit_bytes=SUM_VMEM_BYTES),
        cost_estimate=SMALL,
        name="sum_tiles",
    )(order, bounds, *got, *after)
    return dict(zip(wanted, out))


def added(one, other, after):
    def kernel(one_ref, other_ref, *refs):
        out_ref = refs[-1]

        def add(entry, carry):
            out_ref[entry] = one_ref[entry] + other_ref[entry]
            return carry

        lax.fori_loop(0, one.shape[0], add, 0, unroll=4)

    held = pl.BlockSpec(memory_space=pltpu.VMEM)
    return pl.pallas_call(
        kernel,
        out_shape=jax.ShapeDtypeStruct(one.shape, one.dtype),
        in_specs=[held, held] + [pl.BlockSpec(memory_space=pl.ANY)] * len(after),
        out_specs=held,
        compiler_params=pltpu.CompilerParams(vmem_limit_bytes=SUM_VMEM_BYTES),
        cost_estimate=SMALL,
        name="add_tiles",
    )(one, other, *after)


def chain_sums(sums_of, groups, slabs):
    count = LIST_ENTRIES // CHUNK
    pair_at = FIRST_PAIR // CHUNK
    near, inward, across, outward = {}, {}, {}, {}
    listed = {}
    last = None

    def sums(group):
        nonlocal last
        listed.update(sums_of(group, [] if last is None else [last]))
        last = listed[group[0]]

    def summed(one, other, after):
        nonlocal last
        last = added(one, other, [last] + after)
        return last

    def enter(chunk):
        if chunk < count and hops_before(chunk) == 2:
            inward[chunk] = lax.ppermute(listed[0, chunk], "row", INWARD)

    def cross(chunk):
        if chunk < count and hops_before(chunk):
            near[chunk] = listed[0, chunk]
            if hops_before(chunk) == 2:
                near[chunk] = summed(near[chunk], inward[chunk], [])
            across[chunk] = lax.ppermute(near[chunk], "row", ACROSS)

    def leave(chunk):
        moving = listed[1, chunk]
        if hops_before(chunk):
            after = [outward[chunk - LAG]] if chunk >= LAG else []
            if chunk > pair_at and (chunk - pair_at) % 2 == 0:
                after += slabs[(chunk - pair_at) // 2 :][:1]
            moving = summed(moving, across[chunk], after)
        outward[chunk] = lax.ppermute(moving, "row", OUTWARD)

    sums(groups[0])
    leave(0)
    cross(1)
    enter(3)
    sums(groups[1])
    cross(2)
    enter(4)
    for chunk in range(1, count):
        leave(chunk)
        cross(chunk + LAG)
        if chunk > 1 and chunk in groups:
            sums(groups[chunk])
        enter(chunk + 2 * LAG)
    return near, across, outward


def contracted(place, first_at, second_at, slabs, chunks):
    near, across, outward = chunks
    count = len(outward)
    entries = count * CHUNK
    tile = outward[0].shape[1]
    depth = K_BLOCKS * tile
    columns = slabs[0].shape[1]
    row_count = len(slabs)
    steps = ROW_BLOCKS_DEV // ROW_TILE
    col_tile = min(512, columns)
    both = sorted(near)

    def kernel(place_ref, first_ref, second_ref, *refs):
        near_refs = dict(zip(both, refs))
        across_refs = dict(zip(both, refs[len(both) :]))
        outward_refs = refs[2 * len(both) : 2 * len(both) + count]
        slab_refs = refs[2 * len(both) + count : 2 * len(both) + count + row_count]
        out_ref, near_held, far_held, slab_held, left, sems = refs[-6:]
        step = pl.program_id(0)
        me, end = place_ref[0], place_ref[1]

        @pl.when(step == 0)
        def _():
            for part in range(count):
                there = pl.ds(part * CHUNK, CHUNK)

                def from_outward(part=part, there=there):
                    pltpu.make_async_copy(
                        outward_refs[part], far_held.at[there], sems.at[2 * part + 1]
                    ).start()

                if part not in near_refs:
                    from_outward()
                    continue
                pltpu.make_async_copy(
                    near_refs[part], near_held.at[there], sems.at[2 * part]
                ).start()
                pl.when(end == 1)(from_outward)

                @pl.when(end == 0)
                def _(part=part, there=there):
                    pltpu.make_async_copy(
                        across_refs[part], far_held.at[there], sems.at[2 * part + 1]
                    ).start()

            for row in range(row_count):
                offset = lax.rem(row - me + row_count, row_count)
                for which in range(row_count):

                    @pl.when(offset == which)
                    def _(row=row, which=which):
                        pltpu.make_async_copy(
                            slab_refs[which],
                            slab_held.at[pl.ds(row * depth, depth)],
                            sems.at[2 * count + row],
                        ).start()

            near_held[entries] = jnp.zeros((tile, tile), near_held.dtype)
            far_held[entries] = jnp.zeros((tile, tile), far_held.dtype)
            for part in range(count):
                there = pl.ds(part * CHUNK, CHUNK)
                if part in near_refs:
                    pltpu.make_async_copy(
                        near_refs[part], near_held.at[there], sems.at[2 * part]
                    ).wait()
                pltpu.make_async_copy(
                    outward_refs[part], far_held.at[there], sems.at[2 * part + 1]
                ).wait()
            for row in range(row_count):
                pltpu.make_async_copy(
                    slab_refs[0],
                    slab_held.at[pl.ds(row * depth, depth)],
                    sems.at[2 * count + row],
                ).wait()

        def fill(row_block, carry):
            for row in range(row_count):
                for k in range(K_BLOCKS):
                    at = row * POSITIONS + (step * ROW_TILE + row_block) * K_BLOCKS + k
                    one = jnp.minimum(first_ref[at], entries)
                    other = jnp.minimum(second_ref[at], entries)
                    there = (row * K_BLOCKS + k) * tile
                    left[
                        pl.ds(pl.multiple_of(row_block * tile, tile), tile),
                        there : there + tile,
                    ] = near_held[one] + far_held[other]
            return carry

        lax.fori_loop(0, ROW_TILE, fill, 0)
        for column in range(0, columns, col_tile):
            part = slice(column, column + col_tile)
            out_ref[:, part] = jnp.dot(
                left[...], slab_held[:, part], preferred_element_type=jnp.float32
            ).astype(out_ref.dtype)

    anywhere = pl.BlockSpec(memory_space=pl.ANY)
    operands = (place, first_at, second_at)
    operands += tuple(near[part] for part in both) + tuple(across[part] for part in both)
    operands += tuple(outward[part] for part in range(count)) + tuple(slabs)
    return pl.pallas_call(
        kernel,
        out_shape=jax.ShapeDtypeStruct((ROW_BLOCKS_DEV * tile, columns), slabs[0].dtype),
        grid_spec=pltpu.PrefetchScalarGridSpec(
            num_scalar_prefetch=3,
            grid=(steps,),
            in_specs=[anywhere] * (len(operands) - 3),
            out_specs=pl.BlockSpec((ROW_TILE * tile, columns), lambda step, *_: (step, 0)),
            scratch_shapes=[
                pltpu.VMEM((entries + 1, tile, tile), slabs[0].dtype),
                pltpu.VMEM((entries + 1, tile, tile), slabs[0].dtype),
                pltpu.VMEM((row_count * depth, columns), slabs[0].dtype),
                pltpu.VMEM((ROW_TILE * tile, row_count * depth), slabs[0].dtype),
                pltpu.SemaphoreType.DMA((2 * count + row_count,)),
            ],
        ),
        compiler_params=pltpu.CompilerParams(vmem_limit_bytes=CONTRACT_VMEM_BYTES),
        cost_estimate=SMALL,
        name="contract_panels",
    )(*operands)


def on_device_chain(tiles, tile_target, tile_place, density):
    row_count = lax.axis_size("row")
    col_count = lax.axis_size("col")
    devices = row_count * col_count
    tile_count, tile_size = tiles.shape[:2]
    capacity = tile_capacity(tile_count, devices)
    plane_slots = col_count * capacity
    me = lax.axis_index("row")
    column = lax.axis_index("col")
    at_end = ((me == 0) | (me == row_count - 1)).astype(jnp.int32)

    targets = tile_target[:, 0]
    codes = jnp.broadcast_to(targets * POSITIONS + tile_place, (devices, tile_count))
    codes = lax.all_to_all(codes, ("row", "col"), split_axis=0, concat_axis=0, tiled=True)
    order = jnp.arange(tile_count, dtype=jnp.int32)
    slot_of = targets * capacity + ranks_of(targets)
    hits = slot_of[None, :] == jnp.arange(devices * capacity, dtype=jnp.int32)[:, None]
    source = jnp.sum(jnp.where(hits, order[None, :], 0), axis=1)

    def exchanged(chosen):
        return lax.all_to_all(chosen, "col", split_axis=0, concat_axis=0, tiled=True)

    half = row_count // 2
    source = source.reshape(2, half, col_count, capacity)
    source = source.transpose(0, 2, 1, 3).reshape(2, half * plane_slots)

    def sent_half(which):
        return picked(tiles, source[which])

    got = [exchanged(sent_half(0))]
    codes = codes.reshape(row_count, col_count * tile_count)
    code_target = codes // POSITIONS
    code_place = codes % POSITIONS
    by_target = (code_target[:, None, :] == jnp.arange(devices, dtype=jnp.int32)[None, :, None])
    by_place = (code_place[:, None, :] == jnp.arange(POSITIONS, dtype=jnp.int32)[None, :, None])
    held = jnp.einsum(
        "ptn,pqn->ptq",
        by_target.astype(jnp.bfloat16),
        by_place.astype(jnp.bfloat16),
        preferred_element_type=jnp.float32,
    )
    filled = held > 0
    classes = jnp.stack(
        [
            jnp.stack([~filled[a] & ~filled[b] & filled[c], ~filled[a] & filled[b], filled[a]])
            for a, b, c in ((0, 1, 2), (3, 2, 1))
        ]
    ).astype(jnp.int32)
    classes = classes.reshape(2, 3, 2, half, col_count, POSITIONS)
    counts = jnp.sum(classes, axis=(3, 5))
    begin = jnp.maximum(counts[:, 0, 0], ALONE)
    last_first = jnp.maximum(begin + counts[:, 1, 0], ONE_BEFORE)
    over = jnp.maximum(last_first + counts[:, 2, 0] - FIRST_PAIR, 0)
    later = jnp.maximum(counts[:, 0, 1], ALONE) + FIRST_PAIR
    last = jnp.maximum(later + counts[:, 1, 1], FIRST_PAIR + ONE_BEFORE)
    fits = (last_first <= FIRST_PAIR) & (last + over + counts[:, 2, 1] <= LIST_ENTRIES)
    fits = jnp.all(fits)
    zero = jnp.zeros_like(begin)
    starts = jnp.stack(
        [zero, begin, last_first, zero + FIRST_PAIR, later, last + over, last], axis=1
    )
    starts = lax.dynamic_index_in_dim(starts, column, 2, keepdims=False)
    mine = lax.dynamic_index_in_dim(classes, column, 4, keepdims=False)
    mine = mine.reshape(2, 3, 2, half * POSITIONS)
    spot = jnp.arange(half * POSITIONS, dtype=jnp.int32)
    before_it = spot[:, None] < spot[None, :]
    rank = jnp.sum(jnp.where(before_it, mine[..., None], 0), axis=3)
    at = rank + starts[:, :6].reshape(2, 2, 3).transpose(0, 2, 1)[..., None]
    moved = at - FIRST_PAIR + starts[:, 6][:, None, None, None]
    first_pair = jnp.arange(2)[None, None, :, None] == 0
    at = jnp.where(first_pair & (at >= FIRST_PAIR), moved, at)
    listed = jnp.min(jnp.where(mine > 0, at, NOWHERE), axis=1)
    listed = listed.reshape(2, row_count, POSITIONS)
    is_low = me < row_count // 2
    first_at = jnp.where(is_low, listed[0], listed[1])
    second_at = jnp.where(is_low, listed[1], listed[0])

    near_codes = lax.dynamic_index_in_dim(codes, me, 0, keepdims=False)
    near_codes = near_codes.reshape(col_count, tile_count)
    near_targets = near_codes // POSITIONS
    near_slots = (near_targets * capacity + jax.vmap(ranks_of)(near_targets))[:, None, :]
    near_places = (near_codes % POSITIONS)[:, None, :]
    wanted = jnp.arange(row_count, dtype=jnp.int32)[:, None] * col_count + column
    wanted = (wanted * capacity + jnp.arange(capacity, dtype=jnp.int32)[None, :]).reshape(1, -1, 1)
    got_place = jnp.sum(jnp.where(near_slots == wanted, near_places + 1, 0), axis=2) - 1
    got_place = got_place.reshape(col_count, row_count, capacity).transpose(1, 0, 2)
    got_place = got_place.reshape(row_count, plane_slots, 1)
    at_place = got_place == jnp.arange(POSITIONS, dtype=jnp.int32)[None, None, :]

    def entries_of(table):
        entry = jnp.sum(jnp.where(at_place, table[:, None, :] + 1, 0), axis=2) - 1
        entry = jnp.where(got_place[..., 0] < 0, NOWHERE, entry)
        entry = entry.reshape(2, half, col_count, capacity)
        return entry.transpose(0, 2, 1, 3).reshape(-1)

    entry = jnp.stack([entries_of(first_at), entries_of(second_at)])
    slot = jnp.arange(row_count * plane_slots, dtype=jnp.int32)
    one, other = entry[:, :, None], entry[:, None, :]
    ahead = (other < one) | ((other == one) & (slot[None, None, :] < slot[None, :, None]))
    turn = jnp.sum(ahead.astype(jnp.int32), axis=2)
    tile_order = jnp.sum(
        jnp.where(turn[:, None, :] == slot[None, :, None], slot[None, None, :], 0), axis=2
    )
    below = entry[:, :, None] < jnp.arange(LIST_ENTRIES + 1, dtype=jnp.int32)[None, None, :]
    entry_bounds = jnp.einsum(
        "os,lse->loe",
        jnp.ones((8, slot.shape[0]), jnp.bfloat16),
        below.astype(jnp.bfloat16),
        preferred_element_type=jnp.float32,
    )[:, 0].astype(jnp.int32)
    def brought(at):
        since = jnp.where(at < FIRST_PAIR, at, at - FIRST_PAIR)
        return jnp.where((since < ALONE) & (at < LIST_ENTRIES), NOWHERE, at).reshape(-1)

    second_at = jnp.where(at_end == 1, second_at.reshape(-1), brought(second_at))
    first_at = brought(first_at)

    source, tile_order = lax.optimization_barrier((source, tile_order))
    chosen = sent_half(1)

    def through_lists(got, chosen, tiles, tile_target, tile_place, density):
        chosen, got = lax.optimization_barrier((chosen, got))
        got = [got, exchanged(chosen)]
        slabs = [passed_along(density, "col", -offset) for offset in range(STEPS)]
        slabs[0] = density
        groups = {
            0: [(1, 0), (0, 1), (0, 3)],
            1: [(0, 2), (0, 4), (1, 1), (1, 2), (1, 3), (1, 4)],
            3: [(0, 6), (0, 7), (0, 8), (0, 9), (1, 5), (1, 6)],
            5: [(0, 10), (0, 11), (0, 12), (1, 7), (1, 8), (1, 9)],
            7: [(1, 10), (1, 11), (1, 12)],
        }

        def sums_of(group, after):
            parts = 1 if max(chunk for _, chunk in group) * CHUNK < FIRST_PAIR else 2
            return listed_sums(got[:parts], tile_order, entry_bounds, group, after)

        chunks = chain_sums(sums_of, groups, slabs)
        place = jnp.stack([me, at_end]).astype(jnp.int32)
        return contracted(place, first_at, second_at, slabs, chunks)

    def round_the_ring(got, chosen, *args):
        return on_device_ring(*args)

    return lax.cond(
        fits,
        through_lists,
        round_the_ring,
        got[0],
        chosen,
        tiles,
        tile_target,
        tile_place,
        density,
    )


def solution(mesh):
    in_specs = (
        P(("row", "col"), None, None),
        P(("row", "col"), None),
        P(("row", "col")),
        P("col", "row"),
    )
    out_specs = P("col", "row")
    on_device = on_device_chain if mesh.shape["row"] == STEPS else on_device_ring
    return jax.shard_map(
        on_device, mesh=mesh, in_specs=in_specs, out_specs=out_specs, check_vma=False
    )
```

time: 522 us -> 407 us (0.78)
  waiting for transfers between devices: 347 us -> 131 us
  Pallas kernels: 0 us -> 135 us
  starting transfers between devices: 23.5 us -> 107 us
  matrix products: 74.5 us -> 0.66 us
  local copies, waits for them, and re-layouts: 60.5 us -> 22.3 us
    ppermute x6 -> x3, waiting for transfers between devices: 162 us -> 0.01 us  [passed_along(): return lax.ppermute(value, axis, pairs)]
    all_to_all x2 -> x3, waiting for transfers between devices: 185 us -> 36.8 us  [the longest x2 36.2 us: exchanged(): lax.all_to_all(chosen, 'col', split_axis=0, concat_axis=0, tiled=True)]
    pallas_call x0 -> x26, Pallas kernels: none -> 135 us  [the longest x18 44.3 us: added(): pl.pallas_call(kernel, out_shape=jax.ShapeDtypeStruct(one.shape, one.dtyp...]
    ppermute x0 -> x31, waiting for transfers between devices: none -> 94.5 us  [the longest x13 82.8 us: leave(): outward[chunk] = lax.ppermute(moving, 'row', OUTWARD)]
    ppermute x0 -> x31, starting transfers between devices: none -> 86.4 us  [the longest x7 59 us: enter(): inward[chunk] = lax.ppermute(listed[0, chunk], 'row', INWARD)]
    dot_general x5 -> x2, matrix products: 74.5 us -> 0.66 us  [the longest x1 0.43 us: on_device_chain(): jnp.einsum('ptn,pqn->ptq', by_target.astype(jnp.bfloat16), by_place.astyp...]
    unnamed x8, local copies, waits for them, and re-layouts: 24.9 us -> 0.04 us
    cond x0 -> x82, local copies, waits for them, and re-layouts: none -> 18.2 us
  transfers between devices with their start and end apart: 8 -> 37, of which waited for: 5 -> 13; matrix products, arithmetic and copies ran while one was open for 12% -> 2% of each run, Pallas kernels for 0% -> 24%
where the time goes in v2:
time: 407 us; the launch traced here: 405 us
  Pallas kernels  135 us (33%)
  waiting for transfers between devices  131 us (32%)
  starting transfers between devices  107 us (26%)
  local copies, waits for them, and re-layouts  22.3 us (5%)
  other arithmetic  6.33 us (2%)
    ppermute x13, waiting for transfers between devices, leave(): outward[chunk] = lax.ppermute(moving, 'row', OUTWARD)  82.8 us
    ppermute x7, starting transfers between devices, enter(): inward[chunk] = lax.ppermute(listed[0, chunk], 'row', INWARD)  59 us
    pallas_call x18, Pallas kernels, added(): pl.pallas_call(kernel, out_shape=jax.ShapeDtypeStruct(one.shape, one.dtyp...  44.3 us
    pallas_call x5, Pallas kernels, listed_sums(): pl.pallas_call(kernel, out_shape=[jax.ShapeDtypeStruct((CHUNK,) + tile, g...  40.4 us
    pallas_call x1, Pallas kernels, contracted(): pl.pallas_call(kernel, out_shape=jax.ShapeDtypeStruct((ROW_BLOCKS_DEV * t...  39.8 us
    all_to_all x2, waiting for transfers between devices, exchanged(): lax.all_to_all(chosen, 'col', split_axis=0, concat_axis=0, tiled=True)  36.2 us
    cond x82, local copies, waits for them, and re-layouts  18.2 us
    ppermute x13, starting transfers between devices, leave(): outward[chunk] = lax.ppermute(moving, 'row', OUTWARD)  17.1 us
  transfers between devices with their start and end apart: 37, of which 13 were waited for; matrix products, arithmetic and copies ran while one was open for 2% of the time, Pallas kernels for 24%

profile of v2, /device:TPU:0, one launch (start us, length us, event | category | flops | bytes accessed | tf_op | source)
XLA Modules:
  0.0 404.9 jit_solution(5968470314258016804)
XLA Ops:
  2.2 7.3 %all-to-all-start.3 = ((s32[32,1,128]{2,1,0:T(1,128)}), s32[32,1,128]{2,1,0:T(1,128)S(1)}, u32[]{:S(2)}, u32[]{:S(2)}) async-start(s32[32,1,128]{2,1,0:T(1,128)} %broadcast_in_dim.161), calls=%async_computation.3 | async-start | bytes 32768 | tf_op jit(solution)/shard_map/all_to_all | solution.py:379
  10.6 5.3 %pick_tiles.3 = bf16[128,128,128]{2,1,0:T(8,128)(2,1)} custom-call(s32[128]{0:T(128)} %squeeze.58.source_ref, bf16[128,128,128]{2,1,0:T(8,128)(2,1)} %tiles_ref.3), custom_call_target="tpu_custom_call" | custom-call | flops 1000 | bytes 1000 | tf_op jit(solution)/shard_map/pick_tiles/pallas_call | solution.py:94
  16.7 4.6 %all-to-all-start.4 = ((bf16[128,128,128]{2,1,0:T(8,128)(2,1)}), bf16[128,128,128]{2,1,0:T(8,128)(2,1)}, u32[]{:S(2)}, u32[]{:S(2)}) async-start(bf16[128,128,128]{2,1,0:T(8,128)(2,1)} %pick_tiles.3), calls=%async_computation.4 | async-start | bytes 8388608 | tf_op jit(solution)/shard_map/all_to_all | solution.py:386
  27.4 5.3 %pick_tiles.2 = bf16[128,128,128]{2,1,0:T(8,128)(2,1)} custom-call(s32[128]{0:T(128)} %slice_bitcast_fusion.source_ref, bf16[128,128,128]{2,1,0:T(8,128)(2,1)} %tiles_ref.3), custom_call_target="tpu_custom_call" | custom-call | flops 1000 | bytes 1000 | tf_op jit(solution)/shard_map/pick_tiles/pallas_call | solution.py:94
  34.1 36.2 %all-to-all-done.4 = bf16[128,128,128]{2,1,0:T(8,128)(2,1)} async-done(((bf16[128,128,128]{2,1,0:T(8,128)(2,1)}), bf16[128,128,128]{2,1,0:T(8,128)(2,1)}, u32[]{:S(2)}, u32[]{:S(2)}) %all-to-all-start.4) | async-done | bytes 4194336 | tf_op jit(solution)/shard_map/all_to_all | solution.py:386
  70.3 334.3 %conditional.1 = (bf16[3072,2048]{1,0:T(8,128)(2,1)}) conditional(s32[]{:T(128)} %convert_element_type.46, (s32[128,1]{0,1:T(1,128)S(1)}, s32[128]{0:T(128)S(1)}, bf16[128,128,128]{2,1,0:T(8,128)(2,1)}, bf16[512,2048]{1,0:T(8,128)(2,1)}) %tuple.61, (s32[]{:T(128)}, s32[]{:T(128)}, pred[]{:T(512)}, s32[1,2,2,96]{3,2,1,0:T(2,128)S(1)}, ...), branch_computations={%region_12.16_spmd, %region_16.17_spmd} | conditional | flops 26606317568 | bytes 355532864 | solution.py:510
  70.3 4.6 %all-to-all-start = ((bf16[128,128,128]{2,1,0:T(8,128)(2,1)}), bf16[128,128,128]{2,1,0:T(8,128)(2,1)}, u32[]{:S(2)}, u32[]{:S(2)}) async-start(bf16[128,128,128]{2,1,0:T(8,128)(2,1)} %get-tuple-element.111), calls=%async_computation | async-start | bytes 8388608 | tf_op jit(solution)/shard_map/cond/branch_1_fun/all_to_all | solution.py:386
  75.5 5.9 %sum_tiles.5 = (bf16[24,128,128]{2,1,0:T(8,128)(2,1)}, bf16[24,128,128]{2,1,0:T(8,128)(2,1)}, bf16[24,128,128]{2,1,0:T(8,128)(2,1)}) custom-call(s32[2,256]{1,0:T(2,128)S(1)} %get-tuple-element.99.order_ref, s32[2,313]{1,0:T(2,128)} %fusion.bounds_ref, bf16[128,128,128]{2,1,0:T(8,128)(2,1)} %get-tuple-element.103.refs_0_), custom_call_target="tpu_custom_call" | custom-call | flops 1000 | bytes 1000 | tf_op jit(solution)/shard_map/cond/branch_1_fun/sum_tiles/pallas_call | solution.py:150
  82.2 6.1 %collective-permute-start = (bf16[24,128,128]{2,1,0:T(8,128)(2,1)}, bf16[24,128,128]{2,1,0:T(8,128)(2,1)S(1)}, u32[]{:S(2)}, u32[]{:S(2)}) collective-permute-start(bf16[24,128,128]{2,1,0:T(8,128)(2,1)} %get-tuple-element.107.one_ref), channel_id=1, source_target_pairs={{0,8},{24,16},{1,9},{25,17},{2,10},{26,18},{3,11},{27,19},{4,12},{... | collective-permute-start | bytes 2359304 | tf_op jit(solution)/shard_map/cond/branch_1_fun/ppermute | solution.py:211
  89.6 8.3 %sum_tiles.6 = (bf16[24,128,128]{2,1,0:T(8,128)(2,1)}, bf16[24,128,128]{2,1,0:T(8,128)(2,1)}, bf16[24,128,128]{2,1,0:T(8,128)(2,1)}, bf16[24,128,128]{2,1,0:T(8,...) custom-call(s32[2,256]{1,0:T(2,128)S(1)} %get-tuple-element.99.order_ref, ...), custom_call_target="tpu_custom_call" | custom-call | flops 1000 | bytes 1000 | tf_op jit(solution)/shard_map/cond/branch_1_fun/sum_tiles/pallas_call | solution.py:150
  98.7 6.5 %collective-permute-start.2 = (bf16[24,128,128]{2,1,0:T(8,128)(2,1)}, bf16[24,128,128]{2,1,0:T(8,128)(2,1)S(1)}, u32[]{:S(2)}, u32[]{:S(2)}) collective-permute-start(bf16[24,128,128]{2,1,0:T(8,128)(2,1)} %get-tuple-element.109.one_ref), channel_id=1, source_target_pairs={{0,8},{24,16},{1,9},{25,17},{2,10},{26,18},{3,11},{27,19},{4,12},{... | collective-permute-start | bytes 2359304 | tf_op jit(solution)/shard_map/cond/branch_1_fun/ppermute | solution.py:211
  117.6 4.8 %collective-permute-done.2.other_ref = bf16[24,128,128]{2,1,0:T(8,128)(2,1)S(1)} collective-permute-done((bf16[24,128,128]{2,1,0:T(8,128)(2,1)}, bf16[24,128,128]{2,1,0:T(8,128)(2,1)S(1)}, u32[]{:S(2)}, u32[]{:S(2)}) %collective-permute-start.2) | collective-permute-done | bytes 786464 | tf_op jit(solution)/shard_map/cond/branch_1_fun/ppermute | solution.py:211
  134.1 9.8 %sum_tiles.7 = (bf16[24,128,128]{2,1,0:T(8,128)(2,1)}, bf16[24,128,128]{2,1,0:T(8,128)(2,1)}, bf16[24,128,128]{2,1,0:T(8,128)(2,1)}, bf16[24,128,128]{2,1,0:T(8,...) custom-call(s32[2,256]{1,0:T(2,128)S(1)} %get-tuple-element.99.order_ref, ...), custom_call_target="tpu_custom_call" | custom-call | flops 1000 | bytes 1000 | tf_op jit(solution)/shard_map/cond/branch_1_fun/sum_tiles/pallas_call | solution.py:150
  143.9 6.2 %collective-permute-done.10.refs_1_.refs_24_ = bf16[24,128,128]{2,1,0:T(8,128)(2,1)} collective-permute-done((bf16[24,128,128]{2,1,0:T(8,128)(2,1)S(1)}, bf16[24,128,128]{2,1,0:T(8,128)(2,1)}, u32[]{:S(2)}, u32[]{:S(2)}) %collective-permute-start.10) | collective-permute-done | bytes 786464 | tf_op jit(solution)/shard_map/cond/branch_1_fun/ppermute | solution.py:227
  154.6 10.9 %collective-permute-start.7 = (bf16[24,128,128]{2,1,0:T(8,128)(2,1)}, bf16[24,128,128]{2,1,0:T(8,128)(2,1)}, u32[]{:S(2)}, u32[]{:S(2)}) collective-permute-start(bf16[24,128,128]{2,1,0:T(8,128)(2,1)} %get-tuple-element.115.one_ref), channel_id=1, source_target_pairs={{0,8},{24,16},{1,9},{25,17},{2,10},{26,18},{3,11},{27,19},{4,12},{... | collective-permute-start | bytes 2359304 | tf_op jit(solution)/shard_map/cond/branch_1_fun/ppermute | solution.py:211
  166.9 11.0 %collective-permute-done.11.refs_1_.refs_26_ = bf16[24,128,128]{2,1,0:T(8,128)(2,1)S(1)} collective-permute-done((bf16[24,128,128]{2,1,0:T(8,128)(2,1)}, bf16[24,128,128]{2,1,0:T(8,128)(2,1)S(1)}, u32[]{:S(2)}, u32[]{:S(2)}) %collective-permute-start.11) | collective-permute-done | bytes 786464 | tf_op jit(solution)/shard_map/cond/branch_1_fun/ppermute | solution.py:227
  177.9 2.8 collective-permute-start.22
  180.7 9.4 %sum_tiles.8 = (bf16[24,128,128]{2,1,0:T(8,128)(2,1)}, bf16[24,128,128]{2,1,0:T(8,128)(2,1)}, bf16[24,128,128]{2,1,0:T(8,128)(2,1)}, bf16[24,128,128]{2,1,0:T(8,...) custom-call(s32[2,256]{1,0:T(2,128)S(1)} %get-tuple-element.99.order_ref, ...), custom_call_target="tpu_custom_call" | custom-call | flops 1000 | bytes 1000 | tf_op jit(solution)/shard_map/cond/branch_1_fun/sum_tiles/pallas_call | solution.py:150
  191.6 2.5 add_tiles.24.refs_0_
  194.2 4.2 %collective-permute-start.12 = (bf16[24,128,128]{2,1,0:T(8,128)(2,1)}, bf16[24,128,128]{2,1,0:T(8,128)(2,1)}, u32[]{:S(2)}, u32[]{:S(2)}) collective-permute-start(bf16[24,128,128]{2,1,0:T(8,128)(2,1)} %get-tuple-element.119.one_ref), channel_id=1, source_target_pairs={{0,8},{24,16},{1,9},{25,17},{2,10},{26,18},{3,11},{27,19},{4,12},{... | collective-permute-start | bytes 2359304 | tf_op jit(solution)/shard_map/cond/branch_1_fun/ppermute | solution.py:211
  202.9 11.9 %collective-permute-start.16 = (bf16[24,128,128]{2,1,0:T(8,128)(2,1)S(1)}, bf16[24,128,128]{2,1,0:T(8,128)(2,1)}, u32[]{:S(2)}, u32[]{:S(2)}) collective-permute-start(bf16[24,128,128]{2,1,0:T(8,128)(2,1)S(1)} %copy-done.21), channel_id=1, source_target_pairs={{0,8},{24,16},{1,9},{25,17},{2,10},{26,18},{3,11},{27,19},{4,12},{... | collective-permute-start | bytes 2359304 | tf_op jit(solution)/shard_map/cond/branch_1_fun/ppermute | solution.py:211
  222.7 7.0 %sum_tiles.9 = (bf16[24,128,128]{2,1,0:T(8,128)(2,1)}, bf16[24,128,128]{2,1,0:T(8,128)(2,1)}, bf16[24,128,128]{2,1,0:T(8,128)(2,1)}) custom-call(s32[2,256]{1,0:T(2,128)S(1)} %get-tuple-element.99.order_ref, s32[2,313]{1,0:T(2,128)} %fusion.bounds_ref, bf16[128,128,128]{2,1,0:T(8,128)(2,1)} %get-tuple-element.103.refs_0_, ...), custom_call_target="tpu_custom_call" | custom-call | flops 1000 | bytes 1000 | tf_op jit(solution)/shard_map/cond/branch_1_fun/sum_tiles/pallas_call | solution.py:150
  229.7 2.5 add_tiles.28.refs_0_
  232.2 11.2 %collective-permute-start.19 = (bf16[24,128,128]{2,1,0:T(8,128)(2,1)}, bf16[24,128,128]{2,1,0:T(8,128)(2,1)}, u32[]{:S(2)}, u32[]{:S(2)}) collective-permute-start(bf16[24,128,128]{2,1,0:T(8,128)(2,1)} %get-tuple-element.125.one_ref), channel_id=1, source_target_pairs={{0,8},{24,16},{1,9},{25,17},{2,10},{26,18},{3,11},{27,19},{4,12},{... | collective-permute-start | bytes 2359304 | tf_op jit(solution)/shard_map/cond/branch_1_fun/ppermute | solution.py:211
  247.9 8.1 %collective-permute-start.23 = (bf16[24,128,128]{2,1,0:T(8,128)(2,1)S(1)}, bf16[24,128,128]{2,1,0:T(8,128)(2,1)}, u32[]{:S(2)}, u32[]{:S(2)}) collective-permute-start(bf16[24,128,128]{2,1,0:T(8,128)(2,1)S(1)} %copy-done.40), channel_id=1, source_target_pairs={{0,8},{24,16},{1,9},{25,17},{2,10},{26,18},{3,11},{27,19},{4,12},{... | collective-permute-start | bytes 2359304 | tf_op jit(solution)/shard_map/cond/branch_1_fun/ppermute | solution.py:211
  264.4 3.7 collective-permute-done.25.refs_1_.refs_30_
  272.4 4.6 %collective-permute-done.23.other_ref = bf16[24,128,128]{2,1,0:T(8,128)(2,1)} collective-permute-done((bf16[24,128,128]{2,1,0:T(8,128)(2,1)S(1)}, bf16[24,128,128]{2,1,0:T(8,128)(2,1)}, u32[]{:S(2)}, u32[]{:S(2)}) %collective-permute-start.23) | collective-permute-done | bytes 786464 | tf_op jit(solution)/shard_map/cond/branch_1_fun/ppermute | solution.py:211
  289.2 15.9 %collective-permute-done.30.refs_1_.refs_32_ = bf16[24,128,128]{2,1,0:T(8,128)(2,1)S(1)} collective-permute-done((bf16[24,128,128]{2,1,0:T(8,128)(2,1)S(1)}, bf16[24,128,128]{2,1,0:T(8,128)(2,1)S(1)}, u32[]{:S(2)}, u32[]{:S(2)}) %collective-permute-start.30) | collective-permute-done | bytes 786464 | tf_op jit(solution)/shard_map/cond/branch_1_fun/ppermute | solution.py:227
  310.1 12.1 %collective-permute-done.28.refs_25_ = bf16[24,128,128]{2,1,0:T(8,128)(2,1)} collective-permute-done((bf16[24,128,128]{2,1,0:T(8,128)(2,1)}, bf16[24,128,128]{2,1,0:T(8,128)(2,1)}, u32[]{:S(2)}, u32[]{:S(2)}) %collective-permute-start.28) | collective-permute-done | bytes 786464 | tf_op jit(solution)/shard_map/cond/branch_1_fun/ppermute | solution.py:227
  322.1 16.9 %collective-permute-done.32.refs_33_ = bf16[24,128,128]{2,1,0:T(8,128)(2,1)} collective-permute-done((bf16[24,128,128]{2,1,0:T(8,128)(2,1)}, bf16[24,128,128]{2,1,0:T(8,128)(2,1)}, u32[]{:S(2)}, u32[]{:S(2)}) %collective-permute-start.32) | collective-permute-done | bytes 786464 | tf_op jit(solution)/shard_map/cond/branch_1_fun/ppermute | solution.py:227
  339.0 15.6 %collective-permute-done.33.refs_34_ = bf16[24,128,128]{2,1,0:T(8,128)(2,1)} collective-permute-done((bf16[24,128,128]{2,1,0:T(8,128)(2,1)}, bf16[24,128,128]{2,1,0:T(8,128)(2,1)}, u32[]{:S(2)}, u32[]{:S(2)}) %collective-permute-start.33) | collective-permute-done | bytes 786464 | tf_op jit(solution)/shard_map/cond/branch_1_fun/ppermute | solution.py:227
  364.8 39.8 %contract_panels.1 = bf16[3072,2048]{1,0:T(8,128)(2,1)} custom-call(s32[2]{0:T(128)S(1)} %pad_add_fusion.place_ref, s32[384]{0:T(512)S(1)} %get-tuple-element.200.first_ref, s32[384]{0:T(512)S(1)} %get-tuple-element.199.second_ref, bf16[24,128,128]{2,1,0:T(8,128)(2,1)S(1)} %copy-done.14, bf16[24,128,128]{2,1,0:T(8,128)(2,1)S(1)} %copy-done.9, ...), custom_call_target="tpu_custom_call" | custom-call | flops 1000 | bytes 1000 | tf_op jit(solution)/shard_map/cond/branch_1_fun/contract_panels/pallas_call | solution.py:344
  (234 shorter events, 102.1 us)
Async XLA Ops:
  16.7 53.7 %all-to-all-start.4 = ((bf16[128,128,128]{2,1,0:T(8,128)(2,1)}), bf16[128,128,128]{2,1,0:T(8,128)(2,1)}, u32[]{:S(2)}, u32[]{:S(2)}) async-start(bf16[128,128,128]{2,1,0:T(8,128)(2,1)} %pick_tiles.3), calls=%async_computation.4 | async-start | bytes 8388608 | tf_op jit(solution)/shard_map/all_to_all | solution.py:386
  70.3 63.7 %all-to-all-start = ((bf16[128,128,128]{2,1,0:T(8,128)(2,1)}), bf16[128,128,128]{2,1,0:T(8,128)(2,1)}, u32[]{:S(2)}, u32[]{:S(2)}) async-start(bf16[128,128,128]{2,1,0:T(8,128)(2,1)} %get-tuple-element.111), calls=%async_computation | async-start | bytes 8388608 | tf_op jit(solution)/shard_map/cond/branch_1_fun/all_to_all | solution.py:386
  81.5 23.7 %collective-permute-start.1 = (bf16[24,128,128]{2,1,0:T(8,128)(2,1)}, bf16[24,128,128]{2,1,0:T(8,128)(2,1)S(1)}, u32[]{:S(2)}, u32[]{:S(2)}) collective-permute-start(bf16[24,128,128]{2,1,0:T(8,128)(2,1)} %get-tuple-element.104.refs_0_), channel_id=1, source_target_pairs={{8,16},{16,8},{9,17},{17,9},{10,18},{18,10},{11,19},{19,11},{12,20... | collective-permute-start | bytes 2359304 | tf_op jit(solution)/shard_map/cond/branch_1_fun/ppermute | solution.py:218
  82.2 27.7 %collective-permute-start = (bf16[24,128,128]{2,1,0:T(8,128)(2,1)}, bf16[24,128,128]{2,1,0:T(8,128)(2,1)S(1)}, u32[]{:S(2)}, u32[]{:S(2)}) collective-permute-start(bf16[24,128,128]{2,1,0:T(8,128)(2,1)} %get-tuple-element.107.one_ref), channel_id=1, source_target_pairs={{0,8},{24,16},{1,9},{25,17},{2,10},{26,18},{3,11},{27,19},{4,12},{... | collective-permute-start | bytes 2359304 | tf_op jit(solution)/shard_map/cond/branch_1_fun/ppermute | solution.py:211
  88.3 25.7 %collective-permute-start.4 = (bf16[24,128,128]{2,1,0:T(8,128)(2,1)}, bf16[24,128,128]{2,1,0:T(8,128)(2,1)S(1)}, u32[]{:S(2)}, u32[]{:S(2)}) collective-permute-start(bf16[24,128,128]{2,1,0:T(8,128)(2,1)} %get-tuple-element.105.refs_1_), channel_id=1, source_target_pairs={{8,0},{16,24},{9,1},{17,25},{10,2},{18,26},{11,3},{19,27},{12,4},{... | collective-permute-start | bytes 2359304 | tf_op jit(solution)/shard_map/cond/branch_1_fun/ppermute | solution.py:227
  98.7 23.8 %collective-permute-start.2 = (bf16[24,128,128]{2,1,0:T(8,128)(2,1)}, bf16[24,128,128]{2,1,0:T(8,128)(2,1)S(1)}, u32[]{:S(2)}, u32[]{:S(2)}) collective-permute-start(bf16[24,128,128]{2,1,0:T(8,128)(2,1)} %get-tuple-element.109.one_ref), channel_id=1, source_target_pairs={{0,8},{24,16},{1,9},{25,17},{2,10},{26,18},{3,11},{27,19},{4,12},{... | collective-permute-start | bytes 2359304 | tf_op jit(solution)/shard_map/cond/branch_1_fun/ppermute | solution.py:211
  108.6 21.9 %collective-permute-start.6 = (bf16[24,128,128]{2,1,0:T(8,128)(2,1)}, bf16[24,128,128]{2,1,0:T(8,128)(2,1)S(1)}, u32[]{:S(2)}, u32[]{:S(2)}) collective-permute-start(bf16[24,128,128]{2,1,0:T(8,128)(2,1)} %add_tiles.18.refs_0_), channel_id=1, source_target_pairs={{8,0},{16,24},{9,1},{17,25},{10,2},{18,26},{11,3},{19,27},{12,4},{... | collective-permute-start | bytes 2359304 | tf_op jit(solution)/shard_map/cond/branch_1_fun/ppermute | solution.py:227
  113.3 17.2 %collective-permute-start.5 = (bf16[24,128,128]{2,1,0:T(8,128)(2,1)}, bf16[24,128,128]{2,1,0:T(8,128)(2,1)S(1)}, u32[]{:S(2)}, u32[]{:S(2)}) collective-permute-start(bf16[24,128,128]{2,1,0:T(8,128)(2,1)} %add_tiles.19.refs_0_.refs_2_), channel_id=1, source_target_pairs={{8,16},{16,8},{9,17},{17,9},{10,18},{18,10},{11,19},{19,11},{12,20... | collective-permute-start | bytes 2359304 | tf_op jit(solution)/shard_map/cond/branch_1_fun/ppermute | solution.py:218
  125.8 18.1 %collective-permute-start.9 = (bf16[24,128,128]{2,1,0:T(8,128)(2,1)}, bf16[24,128,128]{2,1,0:T(8,128)(2,1)}, u32[]{:S(2)}, u32[]{:S(2)}) collective-permute-start(bf16[24,128,128]{2,1,0:T(8,128)(2,1)} %add_tiles.21.refs_0_.refs_3_), channel_id=1, source_target_pairs={{8,16},{16,8},{9,17},{17,9},{10,18},{18,10},{11,19},{19,11},{12,20... | collective-permute-start | bytes 2359304 | tf_op jit(solution)/shard_map/cond/branch_1_fun/ppermute | solution.py:218
  127.3 22.8 %collective-permute-start.10 = (bf16[24,128,128]{2,1,0:T(8,128)(2,1)S(1)}, bf16[24,128,128]{2,1,0:T(8,128)(2,1)}, u32[]{:S(2)}, u32[]{:S(2)}) collective-permute-start(bf16[24,128,128]{2,1,0:T(8,128)(2,1)S(1)} %copy-done.25), channel_id=1, source_target_pairs={{8,0},{16,24},{9,1},{17,25},{10,2},{18,26},{11,3},{19,27},{12,4},{... | collective-permute-start | bytes 2359304 | tf_op jit(solution)/shard_map/cond/branch_1_fun/ppermute | solution.py:227
  128.6 72.2 %collective-permute-start.15 = (bf16[512,2048]{1,0:T(8,128)(2,1)}, bf16[512,2048]{1,0:T(8,128)(2,1)S(1)}, u32[]{:S(2)}, u32[]{:S(2)}) collective-permute-start(bf16[512,2048]{1,0:T(8,128)(2,1)} %get-tuple-element.122.refs_35_), channel_id=1, source_target_pairs={{0,7},{1,0},{2,1},{3,2},{4,3},{5,4},{6,5},{7,6},{8,15},{9,8},{10,9... | collective-permute-start | bytes 6291464 | tf_op jit(solution)/shard_map/cond/branch_1_fun/ppermute | solution.py:33
  152.6 25.3 %collective-permute-start.11 = (bf16[24,128,128]{2,1,0:T(8,128)(2,1)}, bf16[24,128,128]{2,1,0:T(8,128)(2,1)S(1)}, u32[]{:S(2)}, u32[]{:S(2)}) collective-permute-start(bf16[24,128,128]{2,1,0:T(8,128)(2,1)} %add_tiles.23.refs_2_), channel_id=1, source_target_pairs={{8,0},{16,24},{9,1},{17,25},{10,2},{18,26},{11,3},{19,27},{12,4},{... | collective-permute-start | bytes 2359304 | tf_op jit(solution)/shard_map/cond/branch_1_fun/ppermute | solution.py:227
  153.9 36.1 %collective-permute-start.8 = (bf16[24,128,128]{2,1,0:T(8,128)(2,1)S(1)}, bf16[24,128,128]{2,1,0:T(8,128)(2,1)S(1)}, u32[]{:S(2)}, u32[]{:S(2)}) collective-permute-start(bf16[24,128,128]{2,1,0:T(8,128)(2,1)S(1)} %copy-done.12), channel_id=1, source_target_pairs={{8,16},{16,8},{9,17},{17,9},{10,18},{18,10},{11,19},{19,11},{12,20... | collective-permute-start | bytes 2359304 | tf_op jit(solution)/shard_map/cond/branch_1_fun/ppermute | solution.py:218
  154.6 39.6 %collective-permute-start.7 = (bf16[24,128,128]{2,1,0:T(8,128)(2,1)}, bf16[24,128,128]{2,1,0:T(8,128)(2,1)}, u32[]{:S(2)}, u32[]{:S(2)}) collective-permute-start(bf16[24,128,128]{2,1,0:T(8,128)(2,1)} %get-tuple-element.115.one_ref), channel_id=1, source_target_pairs={{0,8},{24,16},{1,9},{25,17},{2,10},{26,18},{3,11},{27,19},{4,12},{... | collective-permute-start | bytes 2359304 | tf_op jit(solution)/shard_map/cond/branch_1_fun/ppermute | solution.py:211
  165.5 36.0 %collective-permute-start.14 = (bf16[24,128,128]{2,1,0:T(8,128)(2,1)}, bf16[24,128,128]{2,1,0:T(8,128)(2,1)}, u32[]{:S(2)}, u32[]{:S(2)}) collective-permute-start(bf16[24,128,128]{2,1,0:T(8,128)(2,1)} %get-tuple-element.121), channel_id=1, source_target_pairs={{8,0},{16,24},{9,1},{17,25},{10,2},{18,26},{11,3},{19,27},{12,4},{... | collective-permute-start | bytes 2359304 | tf_op jit(solution)/shard_map/cond/branch_1_fun/ppermute | solution.py:227
  177.9 67.9 %collective-permute-start.22 = (bf16[512,2048]{1,0:T(8,128)(2,1)}, bf16[512,2048]{1,0:T(8,128)(2,1)S(1)}, u32[]{:S(2)}, u32[]{:S(2)}) collective-permute-start(bf16[512,2048]{1,0:T(8,128)(2,1)} %get-tuple-element.122.refs_35_), channel_id=1, source_target_pairs={{0,6},{1,7},{2,0},{3,1},{4,2},{5,3},{6,4},{7,5},{8,14},{9,15},{10,... | collective-permute-start | bytes 6291464 | tf_op jit(solution)/shard_map/cond/branch_1_fun/ppermute | solution.py:33
  194.2 23.0 %collective-permute-start.12 = (bf16[24,128,128]{2,1,0:T(8,128)(2,1)}, bf16[24,128,128]{2,1,0:T(8,128)(2,1)}, u32[]{:S(2)}, u32[]{:S(2)}) collective-permute-start(bf16[24,128,128]{2,1,0:T(8,128)(2,1)} %get-tuple-element.119.one_ref), channel_id=1, source_target_pairs={{0,8},{24,16},{1,9},{25,17},{2,10},{26,18},{3,11},{27,19},{4,12},{... | collective-permute-start | bytes 2359304 | tf_op jit(solution)/shard_map/cond/branch_1_fun/ppermute | solution.py:211
  200.8 20.4 %collective-permute-start.17 = (bf16[24,128,128]{2,1,0:T(8,128)(2,1)}, bf16[24,128,128]{2,1,0:T(8,128)(2,1)S(1)}, u32[]{:S(2)}, u32[]{:S(2)}) collective-permute-start(bf16[24,128,128]{2,1,0:T(8,128)(2,1)} %add_tiles.25.refs_0_.refs_6_), channel_id=1, source_target_pairs={{8,16},{16,8},{9,17},{17,9},{10,18},{18,10},{11,19},{19,11},{12,20... | collective-permute-start | bytes 2359304 | tf_op jit(solution)/shard_map/cond/branch_1_fun/ppermute | solution.py:218
  201.6 21.0 %collective-permute-start.18 = (bf16[24,128,128]{2,1,0:T(8,128)(2,1)S(1)}, bf16[24,128,128]{2,1,0:T(8,128)(2,1)}, u32[]{:S(2)}, u32[]{:S(2)}) collective-permute-start(bf16[24,128,128]{2,1,0:T(8,128)(2,1)S(1)} %copy-done.23), channel_id=1, source_target_pairs={{8,0},{16,24},{9,1},{17,25},{10,2},{18,26},{11,3},{19,27},{12,4},{... | collective-permute-start | bytes 2359304 | tf_op jit(solution)/shard_map/cond/branch_1_fun/ppermute | solution.py:227
  202.9 29.3 %collective-permute-start.16 = (bf16[24,128,128]{2,1,0:T(8,128)(2,1)S(1)}, bf16[24,128,128]{2,1,0:T(8,128)(2,1)}, u32[]{:S(2)}, u32[]{:S(2)}) collective-permute-start(bf16[24,128,128]{2,1,0:T(8,128)(2,1)S(1)} %copy-done.21), channel_id=1, source_target_pairs={{0,8},{24,16},{1,9},{25,17},{2,10},{26,18},{3,11},{27,19},{4,12},{... | collective-permute-start | bytes 2359304 | tf_op jit(solution)/shard_map/cond/branch_1_fun/ppermute | solution.py:211
  219.7 27.4 %collective-permute-start.20 = (bf16[24,128,128]{2,1,0:T(8,128)(2,1)}, bf16[24,128,128]{2,1,0:T(8,128)(2,1)}, u32[]{:S(2)}, u32[]{:S(2)}) collective-permute-start(bf16[24,128,128]{2,1,0:T(8,128)(2,1)} %add_tiles.27.refs_2_.refs_7_), channel_id=1, source_target_pairs={{8,16},{16,8},{9,17},{17,9},{10,18},{18,10},{11,19},{19,11},{12,20... | collective-permute-start | bytes 2359304 | tf_op jit(solution)/shard_map/cond/branch_1_fun/ppermute | solution.py:218
  221.3 26.6 %collective-permute-start.21 = (bf16[24,128,128]{2,1,0:T(8,128)(2,1)S(1)}, bf16[24,128,128]{2,1,0:T(8,128)(2,1)}, u32[]{:S(2)}, u32[]{:S(2)}) collective-permute-start(bf16[24,128,128]{2,1,0:T(8,128)(2,1)S(1)} %copy-done.22), channel_id=1, source_target_pairs={{8,0},{16,24},{9,1},{17,25},{10,2},{18,26},{11,3},{19,27},{12,4},{... | collective-permute-start | bytes 2359304 | tf_op jit(solution)/shard_map/cond/branch_1_fun/ppermute | solution.py:227
  222.6 58.9 %collective-permute-start.31 = (bf16[512,2048]{1,0:T(8,128)(2,1)}, bf16[512,2048]{1,0:T(8,128)(2,1)S(1)}, u32[]{:S(2)}, u32[]{:S(2)}) collective-permute-start(bf16[512,2048]{1,0:T(8,128)(2,1)} %get-tuple-element.122.refs_35_), channel_id=1, source_target_pairs={{0,5},{1,6},{2,7},{3,0},{4,1},{5,2},{6,3},{7,4},{8,13},{9,14},{10,... | collective-permute-start | bytes 6291464 | tf_op jit(solution)/shard_map/cond/branch_1_fun/ppermute | solution.py:33
  232.2 28.5 %collective-permute-start.19 = (bf16[24,128,128]{2,1,0:T(8,128)(2,1)}, bf16[24,128,128]{2,1,0:T(8,128)(2,1)}, u32[]{:S(2)}, u32[]{:S(2)}) collective-permute-start(bf16[24,128,128]{2,1,0:T(8,128)(2,1)} %get-tuple-element.125.one_ref), channel_id=1, source_target_pairs={{0,8},{24,16},{1,9},{25,17},{2,10},{26,18},{3,11},{27,19},{4,12},{... | collective-permute-start | bytes 2359304 | tf_op jit(solution)/shard_map/cond/branch_1_fun/ppermute | solution.py:211
  245.9 22.3 %collective-permute-start.25 = (bf16[24,128,128]{2,1,0:T(8,128)(2,1)S(1)}, bf16[24,128,128]{2,1,0:T(8,128)(2,1)S(1)}, u32[]{:S(2)}, u32[]{:S(2)}) collective-permute-start(bf16[24,128,128]{2,1,0:T(8,128)(2,1)S(1)} %copy-done.24), channel_id=1, source_target_pairs={{8,0},{16,24},{9,1},{17,25},{10,2},{18,26},{11,3},{19,27},{12,4},{... | collective-permute-start | bytes 2359304 | tf_op jit(solution)/shard_map/cond/branch_1_fun/ppermute | solution.py:227
  247.2 21.7 %collective-permute-start.24 = (bf16[24,128,128]{2,1,0:T(8,128)(2,1)}, bf16[24,128,128]{2,1,0:T(8,128)(2,1)S(1)}, u32[]{:S(2)}, u32[]{:S(2)}) collective-permute-start(bf16[24,128,128]{2,1,0:T(8,128)(2,1)} %add_tiles.29.refs_0_.refs_8_), channel_id=1, source_target_pairs={{8,16},{16,8},{9,17},{17,9},{10,18},{18,10},{11,19},{19,11},{12,20... | collective-permute-start | bytes 2359304 | tf_op jit(solution)/shard_map/cond/branch_1_fun/ppermute | solution.py:218
  247.9 29.1 %collective-permute-start.23 = (bf16[24,128,128]{2,1,0:T(8,128)(2,1)S(1)}, bf16[24,128,128]{2,1,0:T(8,128)(2,1)}, u32[]{:S(2)}, u32[]{:S(2)}) collective-permute-start(bf16[24,128,128]{2,1,0:T(8,128)(2,1)S(1)} %copy-done.40), channel_id=1, source_target_pairs={{0,8},{24,16},{1,9},{25,17},{2,10},{26,18},{3,11},{27,19},{4,12},{... | collective-permute-start | bytes 2359304 | tf_op jit(solution)/shard_map/cond/branch_1_fun/ppermute | solution.py:211
  260.7 23.6 %collective-permute-start.29 = (bf16[24,128,128]{2,1,0:T(8,128)(2,1)}, bf16[24,128,128]{2,1,0:T(8,128)(2,1)S(1)}, u32[]{:S(2)}, u32[]{:S(2)}) collective-permute-start(bf16[24,128,128]{2,1,0:T(8,128)(2,1)} %add_tiles.30.refs_0_), channel_id=1, source_target_pairs={{8,0},{16,24},{9,1},{17,25},{10,2},{18,26},{11,3},{19,27},{12,4},{... | collective-permute-start | bytes 2359304 | tf_op jit(solution)/shard_map/cond/branch_1_fun/ppermute | solution.py:227
  280.2 24.9 %collective-permute-start.30 = (bf16[24,128,128]{2,1,0:T(8,128)(2,1)S(1)}, bf16[24,128,128]{2,1,0:T(8,128)(2,1)S(1)}, u32[]{:S(2)}, u32[]{:S(2)}) collective-permute-start(bf16[24,128,128]{2,1,0:T(8,128)(2,1)S(1)} %copy-done.26), channel_id=1, source_target_pairs={{8,0},{16,24},{9,1},{17,25},{10,2},{18,26},{11,3},{19,27},{12,4},{... | collective-permute-start | bytes 2359304 | tf_op jit(solution)/shard_map/cond/branch_1_fun/ppermute | solution.py:227
  281.5 40.6 %collective-permute-start.28 = (bf16[24,128,128]{2,1,0:T(8,128)(2,1)}, bf16[24,128,128]{2,1,0:T(8,128)(2,1)}, u32[]{:S(2)}, u32[]{:S(2)}) collective-permute-start(bf16[24,128,128]{2,1,0:T(8,128)(2,1)} %add_tiles.22.refs_2_), channel_id=1, source_target_pairs={{8,0},{16,24},{9,1},{17,25},{10,2},{18,26},{11,3},{19,27},{12,4},{... | collective-permute-start | bytes 2359304 | tf_op jit(solution)/shard_map/cond/branch_1_fun/ppermute | solution.py:227
  287.6 51.3 %collective-permute-start.32 = (bf16[24,128,128]{2,1,0:T(8,128)(2,1)}, bf16[24,128,128]{2,1,0:T(8,128)(2,1)}, u32[]{:S(2)}, u32[]{:S(2)}) collective-permute-start(bf16[24,128,128]{2,1,0:T(8,128)(2,1)} %add_tiles.34.refs_0_), channel_id=1, source_target_pairs={{8,0},{16,24},{9,1},{17,25},{10,2},{18,26},{11,3},{19,27},{12,4},{... | collective-permute-start | bytes 2359304 | tf_op jit(solution)/shard_map/cond/branch_1_fun/ppermute | solution.py:227
  308.5 46.1 %collective-permute-start.33 = (bf16[24,128,128]{2,1,0:T(8,128)(2,1)}, bf16[24,128,128]{2,1,0:T(8,128)(2,1)}, u32[]{:S(2)}, u32[]{:S(2)}) collective-permute-start(bf16[24,128,128]{2,1,0:T(8,128)(2,1)} %add_tiles.35), channel_id=1, source_target_pairs={{8,0},{16,24},{9,1},{17,25},{10,2},{18,26},{11,3},{19,27},{12,4},{... | collective-permute-start | bytes 2359304 | tf_op jit(solution)/shard_map/cond/branch_1_fun/ppermute | solution.py:227
  (48 other events, 615.3 us)

commit v3 on v2

--- a/solution.py
+++ b/solution.py
@@ -20,10 +20,11 @@
 CHUNK = 24
 ALONE, ONE_BEFORE, FIRST_PAIR, LAST_PAIR = 24, 72, 120, 192
 LIST_ENTRIES = FIRST_PAIR + LAST_PAIR
+FIRST_DONE = 240
 NOWHERE = 1 << 15
 ROW_TILE = 4
-SUM_VMEM_BYTES = 56 * 1024 * 1024
-CONTRACT_VMEM_BYTES = 44 * 1024 * 1024
+SUM_VMEM_BYTES = 24 * 1024 * 1024
+CONTRACT_VMEM_BYTES = 56 * 1024 * 1024
 SMALL = pl.CostEstimate(flops=1000, bytes_accessed=1000, transcendentals=0)
 
 
@@ -242,14 +243,18 @@
     return near, across, outward
 
 
-def contracted(place, first_at, second_at, slabs, chunks):
-    near, across, outward = chunks
-    count = len(outward)
+def contracted(place, first_at, second_at, slabs, chunks, rows, span, before, out_dtype):
+    low, high = span
+    near, across, outward = (
+        {at - low: part[at] for at in range(low, high) if at in part} for part in chunks
+    )
+    count = high - low
     entries = count * CHUNK
     tile = outward[0].shape[1]
     depth = K_BLOCKS * tile
     columns = slabs[0].shape[1]
     row_count = len(slabs)
+    panels = len(rows)
     steps = ROW_BLOCKS_DEV // ROW_TILE
     col_tile = min(512, columns)
     both = sorted(near)
@@ -260,6 +265,7 @@
         outward_refs = refs[2 * len(both) : 2 * len(both) + count]
         slab_refs = refs[2 * len(both) + count : 2 * len(both) + count + row_count]
         out_ref, near_held, far_held, slab_held, left, sems = refs[-6:]
+        before_ref = refs[-7]
         step = pl.program_id(0)
         me, end = place_ref[0], place_ref[1]
 
@@ -287,16 +293,16 @@
                         across_refs[part], far_held.at[there], sems.at[2 * part + 1]
                     ).start()
 
-            for row in range(row_count):
+            for panel, row in enumerate(rows):
                 offset = lax.rem(row - me + row_count, row_count)
                 for which in range(row_count):
 
                     @pl.when(offset == which)
-                    def _(row=row, which=which):
+                    def _(panel=panel, which=which):
                         pltpu.make_async_copy(
                             slab_refs[which],
-                            slab_held.at[pl.ds(row * depth, depth)],
-                            sems.at[2 * count + row],
+                            slab_held.at[pl.ds(panel * depth, depth)],
+                            sems.at[2 * count + panel],
                         ).start()
 
             near_held[entries] = jnp.zeros((tile, tile), near_held.dtype)
@@ -310,20 +316,20 @@
                 pltpu.make_async_copy(
                     outward_refs[part], far_held.at[there], sems.at[2 * part + 1]
                 ).wait()
-            for row in range(row_count):
+            for panel in range(panels):
                 pltpu.make_async_copy(
                     slab_refs[0],
-                    slab_held.at[pl.ds(row * depth, depth)],
-                    sems.at[2 * count + row],
+                    slab_held.at[pl.ds(panel * depth, depth)],
+                    sems.at[2 * count + panel],
                 ).wait()
 
         def fill(row_block, carry):
-            for row in range(row_count):
+            for panel, row in enumerate(rows):
                 for k in range(K_BLOCKS):
                     at = row * POSITIONS + (step * ROW_TILE + row_block) * K_BLOCKS + k
-                    one = jnp.minimum(first_ref[at], entries)
-                    other = jnp.minimum(second_ref[at], entries)
-                    there = (row * K_BLOCKS + k) * tile
+                    one = jnp.minimum(first_ref[at] - low * CHUNK, entries)
+                    other = jnp.minimum(second_ref[at] - low * CHUNK, entries)
+                    there = (panel * K_BLOCKS + k) * tile
                     left[
                         pl.ds(pl.multiple_of(row_block * tile, tile), tile),
                         there : there + tile,
@@ -333,34 +339,37 @@
         lax.fori_loop(0, ROW_TILE, fill, 0)
         for column in range(0, columns, col_tile):
             part = slice(column, column + col_tile)
-            out_ref[:, part] = jnp.dot(
-                left[...], slab_held[:, part], preferred_element_type=jnp.float32
-            ).astype(out_ref.dtype)
+            product = jnp.dot(left[...], slab_held[:, part], preferred_element_type=jnp.float32)
+            if before is not None:
+                product = product + before_ref[:, part]
+            out_ref[:, part] = product.astype(out_ref.dtype)
 
     anywhere = pl.BlockSpec(memory_space=pl.ANY)
+    blocked = pl.BlockSpec((ROW_TILE * tile, columns), lambda step, *_: (step, 0))
     operands = (place, first_at, second_at)
     operands += tuple(near[part] for part in both) + tuple(across[part] for part in both)
     operands += tuple(outward[part] for part in range(count)) + tuple(slabs)
+    extra = () if before is None else (before,)
     return pl.pallas_call(
         kernel,
-        out_shape=jax.ShapeDtypeStruct((ROW_BLOCKS_DEV * tile, columns), slabs[0].dtype),
+        out_shape=jax.ShapeDtypeStruct((ROW_BLOCKS_DEV * tile, columns), out_dtype),
         grid_spec=pltpu.PrefetchScalarGridSpec(
             num_scalar_prefetch=3,
             grid=(steps,),
-            in_specs=[anywhere] * (len(operands) - 3),
-            out_specs=pl.BlockSpec((ROW_TILE * tile, columns), lambda step, *_: (step, 0)),
+            in_specs=[anywhere] * (len(operands) - 3) + [blocked] * len(extra),
+            out_specs=blocked,
             scratch_shapes=[
                 pltpu.VMEM((entries + 1, tile, tile), slabs[0].dtype),
                 pltpu.VMEM((entries + 1, tile, tile), slabs[0].dtype),
-                pltpu.VMEM((row_count * depth, columns), slabs[0].dtype),
-                pltpu.VMEM((ROW_TILE * tile, row_count * depth), slabs[0].dtype),
-                pltpu.SemaphoreType.DMA((2 * count + row_count,)),
+                pltpu.VMEM((panels * depth, columns), slabs[0].dtype),
+                pltpu.VMEM((ROW_TILE * tile, panels * depth), slabs[0].dtype),
+                pltpu.SemaphoreType.DMA((2 * count + panels,)),
             ],
         ),
         compiler_params=pltpu.CompilerParams(vmem_limit_bytes=CONTRACT_VMEM_BYTES),
         cost_estimate=SMALL,
         name="contract_panels",
-    )(*operands)
+    )(*operands, *extra)
 
 
 def on_device_chain(tiles, tile_target, tile_place, density):
@@ -419,7 +428,7 @@
     later = jnp.maximum(counts[:, 0, 1], ALONE) + FIRST_PAIR
     last = jnp.maximum(later + counts[:, 1, 1], FIRST_PAIR + ONE_BEFORE)
     fits = (last_first <= FIRST_PAIR) & (last + over + counts[:, 2, 1] <= LIST_ENTRIES)
-    fits = jnp.all(fits)
+    fits = jnp.all(fits & (last + over <= FIRST_DONE))
     zero = jnp.zeros_like(begin)
     starts = jnp.stack(
         [zero, begin, last_first, zero + FIRST_PAIR, later, last + over, last], axis=1
@@ -492,8 +501,8 @@
             0: [(1, 0), (0, 1), (0, 3)],
             1: [(0, 2), (0, 4), (1, 1), (1, 2), (1, 3), (1, 4)],
             3: [(0, 6), (0, 7), (0, 8), (0, 9), (1, 5), (1, 6)],
-            5: [(0, 10), (0, 11), (0, 12), (1, 7), (1, 8), (1, 9)],
-            7: [(1, 10), (1, 11), (1, 12)],
+            6: [(0, 10), (0, 11), (0, 12), (1, 7), (1, 8), (1, 9)],
+            8: [(1, 10), (1, 11), (1, 12)],
         }
 
         def sums_of(group, after):
@@ -502,7 +511,11 @@
 
         chunks = chain_sums(sums_of, groups, slabs)
         place = jnp.stack([me, at_end]).astype(jnp.int32)
-        return contracted(place, first_at, second_at, slabs, chunks)
+        common = (place, first_at, second_at, slabs, chunks)
+        early, late = FIRST_DONE // CHUNK, FIRST_PAIR // CHUNK
+        total = contracted(*common, range(half), (0, early), None, jnp.float32)
+        end = LIST_ENTRIES // CHUNK
+        return contracted(*common, range(half, row_count), (late, end), total, density.dtype)
 
     def round_the_ring(got, chosen, *args):
         return on_device_ring(*args)

time: 407 us -> 361 us (0.89)
  Pallas kernels: 135 us -> 99 us
  waiting for transfers between devices: 131 us -> 156 us
  starting transfers between devices: 107 us -> 86.4 us
  local copies, waits for them, and re-layouts: 22.3 us -> 8.83 us
    pallas_call x18, Pallas kernels: 44.3 us -> 7.36 us  [added(): pl.pallas_call(kernel, out_shape=jax.ShapeDtypeStruct(one.shape, one.dtyp...]
    ppermute x7, starting transfers between devices: 59 us -> 41 us  [enter(): inward[chunk] = lax.ppermute(listed[0, chunk], 'row', INWARD)]
    cond x82 -> x74, local copies, waits for them, and re-layouts: 18.2 us -> 3.74 us
    ppermute x13, waiting for transfers between devices: 82.8 us -> 96.5 us  [leave(): outward[chunk] = lax.ppermute(moving, 'row', OUTWARD)]
    pallas_call x1 -> x2, Pallas kernels: 39.8 us -> 52.8 us  [contracted(): pl.pallas_call(kernel, out_shape=jax.ShapeDtypeStruct((ROW_BLOCKS_DEV * t...]
    ppermute x7, waiting for transfers between devices: 11.6 us -> 21.7 us  [enter(): inward[chunk] = lax.ppermute(listed[0, chunk], 'row', INWARD)]
    pallas_call x5, Pallas kernels: 40.4 us -> 30.6 us  [listed_sums(): pl.pallas_call(kernel, out_shape=[jax.ShapeDtypeStruct((CHUNK,) + tile, g...]
  transfers between devices with their start and end apart: 37 -> 37, of which waited for: 13 -> 18; matrix products, arithmetic and copies ran while one was open for 2% -> 2% of each run, Pallas kernels for 24% -> 20%
where the time goes in v3:
time: 361 us; the launch traced here: 360 us
  waiting for transfers between devices  156 us (43%)
  Pallas kernels  99 us (27%)
  starting transfers between devices  86.4 us (24%)
  local copies, waits for them, and re-layouts  8.83 us (2%)
  other arithmetic  7.08 us (2%)
    ppermute x13, waiting for transfers between devices, leave(): outward[chunk] = lax.ppermute(moving, 'row', OUTWARD)  96.5 us
    pallas_call x2, Pallas kernels, contracted(): pl.pallas_call(kernel, out_shape=jax.ShapeDtypeStruct((ROW_BLOCKS_DEV * t...  52.8 us
    ppermute x7, starting transfers between devices, enter(): inward[chunk] = lax.ppermute(listed[0, chunk], 'row', INWARD)  41 us
    all_to_all x2, waiting for transfers between devices, exchanged(): lax.all_to_all(chosen, 'col', split_axis=0, concat_axis=0, tiled=True)  36.6 us
    pallas_call x5, Pallas kernels, listed_sums(): pl.pallas_call(kernel, out_shape=[jax.ShapeDtypeStruct((CHUNK,) + tile, g...  30.6 us
    ppermute x7, waiting for transfers between devices, enter(): inward[chunk] = lax.ppermute(listed[0, chunk], 'row', INWARD)  21.7 us
    ppermute x13, starting transfers between devices, leave(): outward[chunk] = lax.ppermute(moving, 'row', OUTWARD)  16.8 us
    all_to_all x2, starting transfers between devices, exchanged(): lax.all_to_all(chosen, 'col', split_axis=0, concat_axis=0, tiled=True)  9.13 us
  transfers between devices with their start and end apart: 37, of which 18 were waited for; matrix products, arithmetic and copies ran while one was open for 2% of the time, Pallas kernels for 20%

profile of v3, /device:TPU:0, one launch (start us, length us, event | category | flops | bytes accessed | tf_op | source)
XLA Modules:
  0.0 360.3 jit_solution(9430636334861529332)
XLA Ops:
  2.2 7.3 %all-to-all-start.3 = ((s32[32,1,128]{2,1,0:T(1,128)}), s32[32,1,128]{2,1,0:T(1,128)S(1)}, u32[]{:S(2)}, u32[]{:S(2)}) async-start(s32[32,1,128]{2,1,0:T(1,128)} %broadcast_in_dim.161), calls=%async_computation.3 | async-start | bytes 32768 | tf_op jit(solution)/shard_map/all_to_all | solution.py:388
  16.6 4.6 %all-to-all-start.4 = ((bf16[128,128,128]{2,1,0:T(8,128)(2,1)}), bf16[128,128,128]{2,1,0:T(8,128)(2,1)}, u32[]{:S(2)}, u32[]{:S(2)}) async-start(bf16[128,128,128]{2,1,0:T(8,128)(2,1)} %copy-done.3), calls=%async_computation.4 | async-start | bytes 8388608 | tf_op jit(solution)/shard_map/all_to_all | solution.py:395
  27.0 5.1 %pick_tiles.2 = bf16[128,128,128]{2,1,0:T(8,128)(2,1)} custom-call(s32[128]{0:T(128)S(1)} %slice_bitcast_fusion.source_ref, bf16[128,128,128]{2,1,0:T(8,128)(2,1)} %tiles_ref.3), custom_call_target="tpu_custom_call" | custom-call | flops 1000 | bytes 1000 | tf_op jit(solution)/shard_map/pick_tiles/pallas_call | solution.py:95
  33.7 36.6 %all-to-all-done.4 = bf16[128,128,128]{2,1,0:T(8,128)(2,1)} async-done(((bf16[128,128,128]{2,1,0:T(8,128)(2,1)}), bf16[128,128,128]{2,1,0:T(8,128)(2,1)}, u32[]{:S(2)}, u32[]{:S(2)}) %all-to-all-start.4) | async-done | bytes 4194336 | tf_op jit(solution)/shard_map/all_to_all | solution.py:395
  70.3 289.8 %conditional.1 = (bf16[3072,2048]{1,0:T(8,128)(2,1)}) conditional(s32[]{:T(128)} %convert_element_type.46, (s32[128,1]{0,1:T(1,128)S(1)}, s32[128]{0:T(128)S(1)}, bf16[128,128,128]{2,1,0:T(8,128)(2,1)}, bf16[512,2048]{1,0:T(8,128)(2,1)}) %tuple.61, (s32[]{:T(128)}, s32[]{:T(128)}, pred[]{:T(512)}, s32[1,2,2,96]{3,2,1,0:T(2,128)S(1)}, ...), branch_computations={%region_12.16_spmd, %region_16.17_spmd} | conditional | flops 26606317568 | bytes 347144256 | solution.py:523
  70.4 4.6 %all-to-all-start = ((bf16[128,128,128]{2,1,0:T(8,128)(2,1)}), bf16[128,128,128]{2,1,0:T(8,128)(2,1)}, u32[]{:S(2)}, u32[]{:S(2)}) async-start(bf16[128,128,128]{2,1,0:T(8,128)(2,1)} %get-tuple-element.104), calls=%async_computation | async-start | bytes 8388608 | tf_op jit(solution)/shard_map/cond/branch_1_fun/all_to_all | solution.py:395
  75.0 4.4 %sum_tiles.5 = (bf16[24,128,128]{2,1,0:T(8,128)(2,1)S(1)}, bf16[24,128,128]{2,1,0:T(8,128)(2,1)S(1)}, bf16[24,128,128]{2,1,0:T(8,128)(2,1)S(1)}) custom-call(s32[2,256]{1,0:T(2,128)S(1)} %get-tuple-element.99.order_ref, s32[2,313]{1,0:T(2,128)S(1)} %fusion.bounds_ref, bf16[128,128,128]{2,1,0:T(8,128)(2,1)} %get-tuple-element.103.refs_0_), custom_call_target="tpu_custom_call" | custom-call | flops 1000 | bytes 1000 | tf_op jit(solution)/shard_map/cond/branch_1_fun/sum_tiles/pallas_call | solution.py:151
  80.1 5.4 %collective-permute-start = (bf16[24,128,128]{2,1,0:T(8,128)(2,1)S(1)}, bf16[24,128,128]{2,1,0:T(8,128)(2,1)S(1)}, u32[]{:S(2)}, u32[]{:S(2)}) collective-permute-start(bf16[24,128,128]{2,1,0:T(8,128)(2,1)S(1)} %get-tuple-element.107.one_ref), channel_id=1, source_target_pairs={{0,8},{24,16},{1,9},{25,17},{2,10},{26,18},{3,11},{27,19},{4,12},{... | collective-permute-start | bytes 2359304 | tf_op jit(solution)/shard_map/cond/branch_1_fun/ppermute | solution.py:212
  86.8 6.0 %sum_tiles.6 = (bf16[24,128,128]{2,1,0:T(8,128)(2,1)S(1)}, bf16[24,128,128]{2,1,0:T(8,128)(2,1)S(1)}, bf16[24,128,128]{2,1,0:T(8,128)(2,1)S(1)}, bf16[24,128,128...) custom-call(s32[2,256]{1,0:T(2,128)S(1)} %get-tuple-element.99.order_ref, ...), custom_call_target="tpu_custom_call" | custom-call | flops 1000 | bytes 1000 | tf_op jit(solution)/shard_map/cond/branch_1_fun/sum_tiles/pallas_call | solution.py:151
  94.4 6.5 %collective-permute-start.3 = (bf16[24,128,128]{2,1,0:T(8,128)(2,1)S(1)}, bf16[24,128,128]{2,1,0:T(8,128)(2,1)S(1)}, u32[]{:S(2)}, u32[]{:S(2)}) collective-permute-start(bf16[24,128,128]{2,1,0:T(8,128)(2,1)S(1)} %get-tuple-element.111.one_ref), channel_id=1, source_target_pairs={{0,8},{24,16},{1,9},{25,17},{2,10},{26,18},{3,11},{27,19},{4,12},{... | collective-permute-start | bytes 2359304 | tf_op jit(solution)/shard_map/cond/branch_1_fun/ppermute | solution.py:212
  104.2 3.5 collective-permute-done.5.refs_1_.refs_16_
  109.0 10.5 %collective-permute-done.3.other_ref = bf16[24,128,128]{2,1,0:T(8,128)(2,1)S(1)} collective-permute-done((bf16[24,128,128]{2,1,0:T(8,128)(2,1)S(1)}, bf16[24,128,128]{2,1,0:T(8,128)(2,1)S(1)}, u32[]{:S(2)}, u32[]{:S(2)}) %collective-permute-start.3) | collective-permute-done | bytes 786464 | tf_op jit(solution)/shard_map/cond/branch_1_fun/ppermute | solution.py:212
  126.6 7.3 %sum_tiles.7 = (bf16[24,128,128]{2,1,0:T(8,128)(2,1)S(1)}, bf16[24,128,128]{2,1,0:T(8,128)(2,1)S(1)}, bf16[24,128,128]{2,1,0:T(8,128)(2,1)S(1)}, bf16[24,128,128...) custom-call(s32[2,256]{1,0:T(2,128)S(1)} %get-tuple-element.99.order_ref, ...), custom_call_target="tpu_custom_call" | custom-call | flops 1000 | bytes 1000 | tf_op jit(solution)/shard_map/cond/branch_1_fun/sum_tiles/pallas_call | solution.py:151
  134.0 9.5 %collective-permute-done.10.refs_1_.refs_18_ = bf16[24,128,128]{2,1,0:T(8,128)(2,1)} collective-permute-done((bf16[24,128,128]{2,1,0:T(8,128)(2,1)}, bf16[24,128,128]{2,1,0:T(8,128)(2,1)}, u32[]{:S(2)}, u32[]{:S(2)}) %collective-permute-start.10) | collective-permute-done | bytes 786464 | tf_op jit(solution)/shard_map/cond/branch_1_fun/ppermute | solution.py:228
  146.8 13.9 %collective-permute-start.7 = (bf16[24,128,128]{2,1,0:T(8,128)(2,1)S(1)}, bf16[24,128,128]{2,1,0:T(8,128)(2,1)S(1)}, u32[]{:S(2)}, u32[]{:S(2)}) collective-permute-start(bf16[24,128,128]{2,1,0:T(8,128)(2,1)S(1)} %get-tuple-element.115.one_ref), channel_id=1, source_target_pairs={{0,8},{24,16},{1,9},{25,17},{2,10},{26,18},{3,11},{27,19},{4,12},{... | collective-permute-start | bytes 2359304 | tf_op jit(solution)/shard_map/cond/branch_1_fun/ppermute | solution.py:212
  162.0 11.7 %collective-permute-done.11.refs_1_.refs_20_ = bf16[24,128,128]{2,1,0:T(8,128)(2,1)S(1)} collective-permute-done((bf16[24,128,128]{2,1,0:T(8,128)(2,1)S(1)}, bf16[24,128,128]{2,1,0:T(8,128)(2,1)S(1)}, u32[]{:S(2)}, u32[]{:S(2)}) %collective-permute-start.11) | collective-permute-done | bytes 786464 | tf_op jit(solution)/shard_map/cond/branch_1_fun/ppermute | solution.py:228
  177.2 4.9 %collective-permute-start.12 = (bf16[24,128,128]{2,1,0:T(8,128)(2,1)S(1)}, bf16[24,128,128]{2,1,0:T(8,128)(2,1)S(1)}, u32[]{:S(2)}, u32[]{:S(2)}) collective-permute-start(bf16[24,128,128]{2,1,0:T(8,128)(2,1)S(1)} %get-tuple-element.118.one_ref), channel_id=1, source_target_pairs={{0,8},{24,16},{1,9},{25,17},{2,10},{26,18},{3,11},{27,19},{4,12},{... | collective-permute-start | bytes 2359304 | tf_op jit(solution)/shard_map/cond/branch_1_fun/ppermute | solution.py:212
  183.1 6.7 %collective-permute-done.14.refs_1_.refs_21_.refs_14_ = bf16[24,128,128]{2,1,0:T(8,128)(2,1)S(1)} collective-permute-done((bf16[24,128,128]{2,1,0:T(8,128)(2,1)S(1)}, bf16[24,128,128]{2,1,0:T(8,128)(2,1)S(1)}, u32[]{:S(2)}, u32[]{:S(2)}) %collective-permute-start.14) | collective-permute-done | bytes 786464 | tf_op jit(solution)/shard_map/cond/branch_1_fun/ppermute | solution.py:228
  191.1 7.5 %sum_tiles.8 = (bf16[24,128,128]{2,1,0:T(8,128)(2,1)S(1)}, bf16[24,128,128]{2,1,0:T(8,128)(2,1)S(1)}, bf16[24,128,128]{2,1,0:T(8,128)(2,1)S(1)}, bf16[24,128,128...) custom-call(s32[2,256]{1,0:T(2,128)S(1)} %get-tuple-element.99.order_ref, ...), custom_call_target="tpu_custom_call" | custom-call | flops 1000 | bytes 1000 | tf_op jit(solution)/shard_map/cond/branch_1_fun/sum_tiles/pallas_call | solution.py:151
  198.6 4.4 %collective-permute-start.16 = (bf16[24,128,128]{2,1,0:T(8,128)(2,1)S(1)}, bf16[24,128,128]{2,1,0:T(8,128)(2,1)S(1)}, u32[]{:S(2)}, u32[]{:S(2)}) collective-permute-start(bf16[24,128,128]{2,1,0:T(8,128)(2,1)S(1)} %get-tuple-element.120.refs_0_.one_ref), channel_id=1, source_target_pairs={{0,8},{24,16},{1,9},{25,17},{2,10},{26,18},{3,11},{27,19},{4,12},{... | collective-permute-start | bytes 2359304 | tf_op jit(solution)/shard_map/cond/branch_1_fun/ppermute | solution.py:212
  205.5 5.0 %collective-permute-done.18.refs_1_.refs_22_.refs_15_ = bf16[24,128,128]{2,1,0:T(8,128)(2,1)S(1)} collective-permute-done((bf16[24,128,128]{2,1,0:T(8,128)(2,1)S(1)}, bf16[24,128,128]{2,1,0:T(8,128)(2,1)S(1)}, u32[]{:S(2)}, u32[]{:S(2)}) %collective-permute-start.18) | collective-permute-done | bytes 786464 | tf_op jit(solution)/shard_map/cond/branch_1_fun/ppermute | solution.py:228
  210.6 7.9 %collective-permute-done.16.other_ref = bf16[24,128,128]{2,1,0:T(8,128)(2,1)S(1)} collective-permute-done((bf16[24,128,128]{2,1,0:T(8,128)(2,1)S(1)}, bf16[24,128,128]{2,1,0:T(8,128)(2,1)S(1)}, u32[]{:S(2)}, u32[]{:S(2)}) %collective-permute-start.16) | collective-permute-done | bytes 786464 | tf_op jit(solution)/shard_map/cond/branch_1_fun/ppermute | solution.py:212
  218.6 4.4 %collective-permute-start.19 = (bf16[24,128,128]{2,1,0:T(8,128)(2,1)S(1)}, bf16[24,128,128]{2,1,0:T(8,128)(2,1)S(1)}, u32[]{:S(2)}, u32[]{:S(2)}) collective-permute-start(bf16[24,128,128]{2,1,0:T(8,128)(2,1)S(1)} %get-tuple-element.124.one_ref), channel_id=1, source_target_pairs={{0,8},{24,16},{1,9},{25,17},{2,10},{26,18},{3,11},{27,19},{4,12},{... | collective-permute-start | bytes 2359304 | tf_op jit(solution)/shard_map/cond/branch_1_fun/ppermute | solution.py:212
  225.3 10.3 %collective-permute-done.21.refs_1_.refs_23_.refs_16_ = bf16[24,128,128]{2,1,0:T(8,128)(2,1)S(1)} collective-permute-done((bf16[24,128,128]{2,1,0:T(8,128)(2,1)S(1)}, bf16[24,128,128]{2,1,0:T(8,128)(2,1)S(1)}, u32[]{:S(2)}, u32[]{:S(2)}) %collective-permute-start.21) | collective-permute-done | bytes 786464 | tf_op jit(solution)/shard_map/cond/branch_1_fun/ppermute | solution.py:228
  237.1 5.5 %sum_tiles.9 = (bf16[24,128,128]{2,1,0:T(8,128)(2,1)S(1)}, bf16[24,128,128]{2,1,0:T(8,128)(2,1)S(1)}, bf16[24,128,128]{2,1,0:T(8,128)(2,1)S(1)}) custom-call(s32[2,256]{1,0:T(2,128)S(1)} %get-tuple-element.99.order_ref, s32[2,313]{1,0:T(2,128)S(1)} %fusion.bounds_ref, bf16[128,128,128]{2,1,0:T(8,128)(2,1)} %get-tuple-element.103.refs_0_, ...), custom_call_target="tpu_custom_call" | custom-call | flops 1000 | bytes 1000 | tf_op jit(solution)/shard_map/cond/branch_1_fun/sum_tiles/pallas_call | solution.py:151
  244.4 7.4 %collective-permute-done.25.refs_1_.refs_24_.refs_17_ = bf16[24,128,128]{2,1,0:T(8,128)(2,1)S(1)} collective-permute-done((bf16[24,128,128]{2,1,0:T(8,128)(2,1)S(1)}, bf16[24,128,128]{2,1,0:T(8,128)(2,1)S(1)}, u32[]{:S(2)}, u32[]{:S(2)}) %collective-permute-start.25) | collective-permute-done | bytes 786464 | tf_op jit(solution)/shard_map/cond/branch_1_fun/ppermute | solution.py:228
  258.7 9.6 %collective-permute-done.28.refs_1_.refs_25_.refs_18_ = bf16[24,128,128]{2,1,0:T(8,128)(2,1)S(1)} collective-permute-done((bf16[24,128,128]{2,1,0:T(8,128)(2,1)S(1)}, bf16[24,128,128]{2,1,0:T(8,128)(2,1)S(1)}, u32[]{:S(2)}, u32[]{:S(2)}) %collective-permute-start.28) | collective-permute-done | bytes 786464 | tf_op jit(solution)/shard_map/cond/branch_1_fun/ppermute | solution.py:228
  269.8 15.3 %collective-permute-done.29.refs_1_.refs_19_ = bf16[24,128,128]{2,1,0:T(8,128)(2,1)S(1)} collective-permute-done((bf16[24,128,128]{2,1,0:T(8,128)(2,1)S(1)}, bf16[24,128,128]{2,1,0:T(8,128)(2,1)S(1)}, u32[]{:S(2)}, u32[]{:S(2)}) %collective-permute-start.29) | collective-permute-done | bytes 786464 | tf_op jit(solution)/shard_map/cond/branch_1_fun/ppermute | solution.py:228
  289.0 13.1 %collective-permute-done.33.refs_19_ = bf16[24,128,128]{2,1,0:T(8,128)(2,1)} collective-permute-done((bf16[24,128,128]{2,1,0:T(8,128)(2,1)}, bf16[24,128,128]{2,1,0:T(8,128)(2,1)}, u32[]{:S(2)}, u32[]{:S(2)}) %collective-permute-start.33) | collective-permute-done | bytes 786464 | tf_op jit(solution)/shard_map/cond/branch_1_fun/ppermute | solution.py:228
  302.1 25.5 %contract_panels.2.refs_26_ = f32[3072,2048]{1,0:T(8,128)} custom-call(s32[2]{0:T(128)} %pad_add_fusion.place_ref, s32[384]{0:T(512)} %get-tuple-element.200.first_ref, s32[384]{0:T(512)} %get-tuple-element.199.second_ref, bf16[24,128,128]{2,1,0:T(8,128)(2,1)} %copy-done.35, bf16[24,128,128]{2,1,0:T(8,128)(2,1)} %copy-done.27, ...), custom_call_target="tpu_custom_call" | custom-call | flops 1000 | bytes 1000 | tf_op jit(solution)/shard_map/cond/branch_1_fun/contract_panels/pallas_call | solution.py:353
  327.6 4.3 %collective-permute-done.32.refs_21_ = bf16[24,128,128]{2,1,0:T(8,128)(2,1)S(1)} collective-permute-done((bf16[24,128,128]{2,1,0:T(8,128)(2,1)}, bf16[24,128,128]{2,1,0:T(8,128)(2,1)S(1)}, u32[]{:S(2)}, u32[]{:S(2)}) %collective-permute-start.32) | collective-permute-done | bytes 786464 | tf_op jit(solution)/shard_map/cond/branch_1_fun/ppermute | solution.py:228
  332.8 27.3 %contract_panels.3 = bf16[3072,2048]{1,0:T(8,128)(2,1)} custom-call(s32[2]{0:T(128)} %pad_add_fusion.place_ref, s32[384]{0:T(512)} %get-tuple-element.200.first_ref, s32[384]{0:T(512)} %get-tuple-element.199.second_ref, bf16[24,128,128]{2,1,0:T(8,128)(2,1)} %copy-done.9, bf16[24,128,128]{2,1,0:T(8,128)(2,1)} %copy-done.25, bf16[24,128,128]{2,1,0:T(8,128)(2,1)} %copy-done.4, ...), custom_call_target="tpu_custom_call" | custom-call | flops 1000 | bytes 1000 | tf_op jit(solution)/shard_map/cond/branch_1_fun/contract_panels/pallas_call | solution.py:353
  (229 shorter events, 62.1 us)
Async XLA Ops:
  16.6 53.7 %all-to-all-start.4 = ((bf16[128,128,128]{2,1,0:T(8,128)(2,1)}), bf16[128,128,128]{2,1,0:T(8,128)(2,1)}, u32[]{:S(2)}, u32[]{:S(2)}) async-start(bf16[128,128,128]{2,1,0:T(8,128)(2,1)} %copy-done.3), calls=%async_computation.4 | async-start | bytes 8388608 | tf_op jit(solution)/shard_map/all_to_all | solution.py:395
  70.4 56.2 %all-to-all-start = ((bf16[128,128,128]{2,1,0:T(8,128)(2,1)}), bf16[128,128,128]{2,1,0:T(8,128)(2,1)}, u32[]{:S(2)}, u32[]{:S(2)}) async-start(bf16[128,128,128]{2,1,0:T(8,128)(2,1)} %get-tuple-element.104), calls=%async_computation | async-start | bytes 8388608 | tf_op jit(solution)/shard_map/cond/branch_1_fun/all_to_all | solution.py:395
  79.3 21.5 %collective-permute-start.1 = (bf16[24,128,128]{2,1,0:T(8,128)(2,1)S(1)}, bf16[24,128,128]{2,1,0:T(8,128)(2,1)S(1)}, u32[]{:S(2)}, u32[]{:S(2)}) collective-permute-start(bf16[24,128,128]{2,1,0:T(8,128)(2,1)S(1)} %get-tuple-element.109.refs_0_), channel_id=1, source_target_pairs={{8,16},{16,8},{9,17},{17,9},{10,18},{18,10},{11,19},{19,11},{12,20... | collective-permute-start | bytes 2359304 | tf_op jit(solution)/shard_map/cond/branch_1_fun/ppermute | solution.py:219
  80.1 23.2 %collective-permute-start = (bf16[24,128,128]{2,1,0:T(8,128)(2,1)S(1)}, bf16[24,128,128]{2,1,0:T(8,128)(2,1)S(1)}, u32[]{:S(2)}, u32[]{:S(2)}) collective-permute-start(bf16[24,128,128]{2,1,0:T(8,128)(2,1)S(1)} %get-tuple-element.107.one_ref), channel_id=1, source_target_pairs={{0,8},{24,16},{1,9},{25,17},{2,10},{26,18},{3,11},{27,19},{4,12},{... | collective-permute-start | bytes 2359304 | tf_op jit(solution)/shard_map/cond/branch_1_fun/ppermute | solution.py:212
  85.5 22.3 %collective-permute-start.5 = (bf16[24,128,128]{2,1,0:T(8,128)(2,1)S(1)}, bf16[24,128,128]{2,1,0:T(8,128)(2,1)S(1)}, u32[]{:S(2)}, u32[]{:S(2)}) collective-permute-start(bf16[24,128,128]{2,1,0:T(8,128)(2,1)S(1)} %get-tuple-element.105.refs_1_), channel_id=1, source_target_pairs={{8,0},{16,24},{9,1},{17,25},{10,2},{18,26},{11,3},{19,27},{12,4},{... | collective-permute-start | bytes 2359304 | tf_op jit(solution)/shard_map/cond/branch_1_fun/ppermute | solution.py:228
  94.4 25.2 %collective-permute-start.3 = (bf16[24,128,128]{2,1,0:T(8,128)(2,1)S(1)}, bf16[24,128,128]{2,1,0:T(8,128)(2,1)S(1)}, u32[]{:S(2)}, u32[]{:S(2)}) collective-permute-start(bf16[24,128,128]{2,1,0:T(8,128)(2,1)S(1)} %get-tuple-element.111.one_ref), channel_id=1, source_target_pairs={{0,8},{24,16},{1,9},{25,17},{2,10},{26,18},{3,11},{27,19},{4,12},{... | collective-permute-start | bytes 2359304 | tf_op jit(solution)/shard_map/cond/branch_1_fun/ppermute | solution.py:212
  101.1 22.6 %collective-permute-start.6 = (bf16[24,128,128]{2,1,0:T(8,128)(2,1)S(1)}, bf16[24,128,128]{2,1,0:T(8,128)(2,1)S(1)}, u32[]{:S(2)}, u32[]{:S(2)}) collective-permute-start(bf16[24,128,128]{2,1,0:T(8,128)(2,1)S(1)} %add_tiles.18.refs_0_), channel_id=1, source_target_pairs={{8,0},{16,24},{9,1},{17,25},{10,2},{18,26},{11,3},{19,27},{12,4},{... | collective-permute-start | bytes 2359304 | tf_op jit(solution)/shard_map/cond/branch_1_fun/ppermute | solution.py:228
  103.5 20.2 %collective-permute-start.2 = (bf16[24,128,128]{2,1,0:T(8,128)(2,1)S(1)}, bf16[24,128,128]{2,1,0:T(8,128)(2,1)S(1)}, u32[]{:S(2)}, u32[]{:S(2)}) collective-permute-start(bf16[24,128,128]{2,1,0:T(8,128)(2,1)S(1)} %add_tiles.19.refs_0_.refs_2_), channel_id=1, source_target_pairs={{8,16},{16,8},{9,17},{17,9},{10,18},{18,10},{11,19},{19,11},{12,20... | collective-permute-start | bytes 2359304 | tf_op jit(solution)/shard_map/cond/branch_1_fun/ppermute | solution.py:219
  121.3 22.1 %collective-permute-start.10 = (bf16[24,128,128]{2,1,0:T(8,128)(2,1)}, bf16[24,128,128]{2,1,0:T(8,128)(2,1)}, u32[]{:S(2)}, u32[]{:S(2)}) collective-permute-start(bf16[24,128,128]{2,1,0:T(8,128)(2,1)} %add_tiles.20.refs_0_), channel_id=1, source_target_pairs={{8,0},{16,24},{9,1},{17,25},{10,2},{18,26},{11,3},{19,27},{12,4},{... | collective-permute-start | bytes 2359304 | tf_op jit(solution)/shard_map/cond/branch_1_fun/ppermute | solution.py:228
  122.6 59.7 %collective-permute-start.15 = (bf16[512,2048]{1,0:T(8,128)(2,1)}, bf16[512,2048]{1,0:T(8,128)(2,1)S(1)}, u32[]{:S(2)}, u32[]{:S(2)}) collective-permute-start(bf16[512,2048]{1,0:T(8,128)(2,1)} %get-tuple-element.122.refs_26_.refs_22_), channel_id=1, source_target_pairs={{0,7},{1,0},{2,1},{3,2},{4,3},{5,4},{6,5},{7,6},{8,15},{9,8},{10,9... | collective-permute-start | bytes 6291464 | tf_op jit(solution)/shard_map/cond/branch_1_fun/ppermute | solution.py:34
  144.8 29.0 %collective-permute-start.11 = (bf16[24,128,128]{2,1,0:T(8,128)(2,1)S(1)}, bf16[24,128,128]{2,1,0:T(8,128)(2,1)S(1)}, u32[]{:S(2)}, u32[]{:S(2)}) collective-permute-start(bf16[24,128,128]{2,1,0:T(8,128)(2,1)S(1)} %add_tiles.23.refs_0_), channel_id=1, source_target_pairs={{8,0},{16,24},{9,1},{17,25},{10,2},{18,26},{11,3},{19,27},{12,4},{... | collective-permute-start | bytes 2359304 | tf_op jit(solution)/shard_map/cond/branch_1_fun/ppermute | solution.py:228
  146.1 30.1 %collective-permute-start.8 = (bf16[24,128,128]{2,1,0:T(8,128)(2,1)S(1)}, bf16[24,128,128]{2,1,0:T(8,128)(2,1)S(1)}, u32[]{:S(2)}, u32[]{:S(2)}) collective-permute-start(bf16[24,128,128]{2,1,0:T(8,128)(2,1)S(1)} %get-tuple-element.113.refs_0_.refs_4_), channel_id=1, source_target_pairs={{8,16},{16,8},{9,17},{17,9},{10,18},{18,10},{11,19},{19,11},{12,20... | collective-permute-start | bytes 2359304 | tf_op jit(solution)/shard_map/cond/branch_1_fun/ppermute | solution.py:219
  146.8 30.4 %collective-permute-start.7 = (bf16[24,128,128]{2,1,0:T(8,128)(2,1)S(1)}, bf16[24,128,128]{2,1,0:T(8,128)(2,1)S(1)}, u32[]{:S(2)}, u32[]{:S(2)}) collective-permute-start(bf16[24,128,128]{2,1,0:T(8,128)(2,1)S(1)} %get-tuple-element.115.one_ref), channel_id=1, source_target_pairs={{0,8},{24,16},{1,9},{25,17},{2,10},{26,18},{3,11},{27,19},{4,12},{... | collective-permute-start | bytes 2359304 | tf_op jit(solution)/shard_map/cond/branch_1_fun/ppermute | solution.py:212
  160.7 29.1 %collective-permute-start.14 = (bf16[24,128,128]{2,1,0:T(8,128)(2,1)S(1)}, bf16[24,128,128]{2,1,0:T(8,128)(2,1)S(1)}, u32[]{:S(2)}, u32[]{:S(2)}) collective-permute-start(bf16[24,128,128]{2,1,0:T(8,128)(2,1)S(1)} %get-tuple-element.121), channel_id=1, source_target_pairs={{8,0},{16,24},{9,1},{17,25},{10,2},{18,26},{11,3},{19,27},{12,4},{... | collective-permute-start | bytes 2359304 | tf_op jit(solution)/shard_map/cond/branch_1_fun/ppermute | solution.py:228
  173.8 49.5 %collective-permute-start.22 = (bf16[512,2048]{1,0:T(8,128)(2,1)}, bf16[512,2048]{1,0:T(8,128)(2,1)S(1)}, u32[]{:S(2)}, u32[]{:S(2)}) collective-permute-start(bf16[512,2048]{1,0:T(8,128)(2,1)} %get-tuple-element.122.refs_26_.refs_22_), channel_id=1, source_target_pairs={{0,6},{1,7},{2,0},{3,1},{4,2},{5,3},{6,4},{7,5},{8,14},{9,15},{10,... | collective-permute-start | bytes 6291464 | tf_op jit(solution)/shard_map/cond/branch_1_fun/ppermute | solution.py:34
  176.2 22.4 %collective-permute-start.13 = (bf16[24,128,128]{2,1,0:T(8,128)(2,1)S(1)}, bf16[24,128,128]{2,1,0:T(8,128)(2,1)S(1)}, u32[]{:S(2)}, u32[]{:S(2)}) collective-permute-start(bf16[24,128,128]{2,1,0:T(8,128)(2,1)S(1)} %get-tuple-element.114.refs_5_.refs_1_), channel_id=1, source_target_pairs={{8,16},{16,8},{9,17},{17,9},{10,18},{18,10},{11,19},{19,11},{12,20... | collective-permute-start | bytes 2359304 | tf_op jit(solution)/shard_map/cond/branch_1_fun/ppermute | solution.py:219
  177.2 26.0 %collective-permute-start.12 = (bf16[24,128,128]{2,1,0:T(8,128)(2,1)S(1)}, bf16[24,128,128]{2,1,0:T(8,128)(2,1)S(1)}, u32[]{:S(2)}, u32[]{:S(2)}) collective-permute-start(bf16[24,128,128]{2,1,0:T(8,128)(2,1)S(1)} %get-tuple-element.118.one_ref), channel_id=1, source_target_pairs={{0,8},{24,16},{1,9},{25,17},{2,10},{26,18},{3,11},{27,19},{4,12},{... | collective-permute-start | bytes 2359304 | tf_op jit(solution)/shard_map/cond/branch_1_fun/ppermute | solution.py:212
  182.4 21.8 %collective-permute-start.17 = (bf16[24,128,128]{2,1,0:T(8,128)(2,1)S(1)}, bf16[24,128,128]{2,1,0:T(8,128)(2,1)S(1)}, u32[]{:S(2)}, u32[]{:S(2)}) collective-permute-start(bf16[24,128,128]{2,1,0:T(8,128)(2,1)S(1)} %add_tiles.25.refs_2_.refs_6_), channel_id=1, source_target_pairs={{8,16},{16,8},{9,17},{17,9},{10,18},{18,10},{11,19},{19,11},{12,20... | collective-permute-start | bytes 2359304 | tf_op jit(solution)/shard_map/cond/branch_1_fun/ppermute | solution.py:219
  189.8 20.6 %collective-permute-start.18 = (bf16[24,128,128]{2,1,0:T(8,128)(2,1)S(1)}, bf16[24,128,128]{2,1,0:T(8,128)(2,1)S(1)}, u32[]{:S(2)}, u32[]{:S(2)}) collective-permute-start(bf16[24,128,128]{2,1,0:T(8,128)(2,1)S(1)} %add_tiles.24.refs_0_), channel_id=1, source_target_pairs={{8,0},{16,24},{9,1},{17,25},{10,2},{18,26},{11,3},{19,27},{12,4},{... | collective-permute-start | bytes 2359304 | tf_op jit(solution)/shard_map/cond/branch_1_fun/ppermute | solution.py:228
  198.6 20.0 %collective-permute-start.16 = (bf16[24,128,128]{2,1,0:T(8,128)(2,1)S(1)}, bf16[24,128,128]{2,1,0:T(8,128)(2,1)S(1)}, u32[]{:S(2)}, u32[]{:S(2)}) collective-permute-start(bf16[24,128,128]{2,1,0:T(8,128)(2,1)S(1)} %get-tuple-element.120.refs_0_.one_ref), channel_id=1, source_target_pairs={{0,8},{24,16},{1,9},{25,17},{2,10},{26,18},{3,11},{27,19},{4,12},{... | collective-permute-start | bytes 2359304 | tf_op jit(solution)/shard_map/cond/branch_1_fun/ppermute | solution.py:212
  203.4 21.1 %collective-permute-start.20 = (bf16[24,128,128]{2,1,0:T(8,128)(2,1)S(1)}, bf16[24,128,128]{2,1,0:T(8,128)(2,1)S(1)}, u32[]{:S(2)}, u32[]{:S(2)}) collective-permute-start(bf16[24,128,128]{2,1,0:T(8,128)(2,1)S(1)} %add_tiles.27.refs_0_.refs_7_.refs_3_), channel_id=1, source_target_pairs={{8,16},{16,8},{9,17},{17,9},{10,18},{18,10},{11,19},{19,11},{12,20... | collective-permute-start | bytes 2359304 | tf_op jit(solution)/shard_map/cond/branch_1_fun/ppermute | solution.py:219
  204.2 31.4 %collective-permute-start.21 = (bf16[24,128,128]{2,1,0:T(8,128)(2,1)S(1)}, bf16[24,128,128]{2,1,0:T(8,128)(2,1)S(1)}, u32[]{:S(2)}, u32[]{:S(2)}) collective-permute-start(bf16[24,128,128]{2,1,0:T(8,128)(2,1)S(1)} %add_tiles.26.refs_0_), channel_id=1, source_target_pairs={{8,0},{16,24},{9,1},{17,25},{10,2},{18,26},{11,3},{19,27},{12,4},{... | collective-permute-start | bytes 2359304 | tf_op jit(solution)/shard_map/cond/branch_1_fun/ppermute | solution.py:228
  210.4 46.9 %collective-permute-start.30 = (bf16[512,2048]{1,0:T(8,128)(2,1)}, bf16[512,2048]{1,0:T(8,128)(2,1)S(1)}, u32[]{:S(2)}, u32[]{:S(2)}) collective-permute-start(bf16[512,2048]{1,0:T(8,128)(2,1)} %get-tuple-element.122.refs_26_.refs_22_), channel_id=1, source_target_pairs={{0,5},{1,6},{2,7},{3,0},{4,1},{5,2},{6,3},{7,4},{8,13},{9,14},{10,... | collective-permute-start | bytes 6291464 | tf_op jit(solution)/shard_map/cond/branch_1_fun/ppermute | solution.py:34
  218.6 24.3 %collective-permute-start.19 = (bf16[24,128,128]{2,1,0:T(8,128)(2,1)S(1)}, bf16[24,128,128]{2,1,0:T(8,128)(2,1)S(1)}, u32[]{:S(2)}, u32[]{:S(2)}) collective-permute-start(bf16[24,128,128]{2,1,0:T(8,128)(2,1)S(1)} %get-tuple-element.124.one_ref), channel_id=1, source_target_pairs={{0,8},{24,16},{1,9},{25,17},{2,10},{26,18},{3,11},{27,19},{4,12},{... | collective-permute-start | bytes 2359304 | tf_op jit(solution)/shard_map/cond/branch_1_fun/ppermute | solution.py:212
  223.2 28.6 %collective-permute-start.25 = (bf16[24,128,128]{2,1,0:T(8,128)(2,1)S(1)}, bf16[24,128,128]{2,1,0:T(8,128)(2,1)S(1)}, u32[]{:S(2)}, u32[]{:S(2)}) collective-permute-start(bf16[24,128,128]{2,1,0:T(8,128)(2,1)S(1)} %add_tiles.28.refs_0_), channel_id=1, source_target_pairs={{8,0},{16,24},{9,1},{17,25},{10,2},{18,26},{11,3},{19,27},{12,4},{... | collective-permute-start | bytes 2359304 | tf_op jit(solution)/shard_map/cond/branch_1_fun/ppermute | solution.py:228
  224.6 28.0 %collective-permute-start.24 = (bf16[24,128,128]{2,1,0:T(8,128)(2,1)S(1)}, bf16[24,128,128]{2,1,0:T(8,128)(2,1)S(1)}, u32[]{:S(2)}, u32[]{:S(2)}) collective-permute-start(bf16[24,128,128]{2,1,0:T(8,128)(2,1)S(1)} %add_tiles.29.refs_2_.refs_4_), channel_id=1, source_target_pairs={{8,16},{16,8},{9,17},{17,9},{10,18},{18,10},{11,19},{19,11},{12,20... | collective-permute-start | bytes 2359304 | tf_op jit(solution)/shard_map/cond/branch_1_fun/ppermute | solution.py:219
  235.6 19.5 %collective-permute-start.23 = (bf16[24,128,128]{2,1,0:T(8,128)(2,1)S(1)}, bf16[24,128,128]{2,1,0:T(8,128)(2,1)S(1)}, u32[]{:S(2)}, u32[]{:S(2)}) collective-permute-start(bf16[24,128,128]{2,1,0:T(8,128)(2,1)S(1)} %get-tuple-element.127.one_ref), channel_id=1, source_target_pairs={{0,8},{24,16},{1,9},{25,17},{2,10},{26,18},{3,11},{27,19},{4,12},{... | collective-permute-start | bytes 2359304 | tf_op jit(solution)/shard_map/cond/branch_1_fun/ppermute | solution.py:212
  242.9 25.4 %collective-permute-start.28 = (bf16[24,128,128]{2,1,0:T(8,128)(2,1)S(1)}, bf16[24,128,128]{2,1,0:T(8,128)(2,1)S(1)}, u32[]{:S(2)}, u32[]{:S(2)}) collective-permute-start(bf16[24,128,128]{2,1,0:T(8,128)(2,1)S(1)} %add_tiles.30.refs_0_), channel_id=1, source_target_pairs={{8,0},{16,24},{9,1},{17,25},{10,2},{18,26},{11,3},{19,27},{12,4},{... | collective-permute-start | bytes 2359304 | tf_op jit(solution)/shard_map/cond/branch_1_fun/ppermute | solution.py:228
  256.0 29.1 %collective-permute-start.29 = (bf16[24,128,128]{2,1,0:T(8,128)(2,1)S(1)}, bf16[24,128,128]{2,1,0:T(8,128)(2,1)S(1)}, u32[]{:S(2)}, u32[]{:S(2)}) collective-permute-start(bf16[24,128,128]{2,1,0:T(8,128)(2,1)S(1)} %add_tiles.32.refs_0_), channel_id=1, source_target_pairs={{8,0},{16,24},{9,1},{17,25},{10,2},{18,26},{11,3},{19,27},{12,4},{... | collective-permute-start | bytes 2359304 | tf_op jit(solution)/shard_map/cond/branch_1_fun/ppermute | solution.py:228
  257.4 44.8 %collective-permute-start.33 = (bf16[24,128,128]{2,1,0:T(8,128)(2,1)}, bf16[24,128,128]{2,1,0:T(8,128)(2,1)}, u32[]{:S(2)}, u32[]{:S(2)}) collective-permute-start(bf16[24,128,128]{2,1,0:T(8,128)(2,1)} %add_tiles.22.refs_2_), channel_id=1, source_target_pairs={{8,0},{16,24},{9,1},{17,25},{10,2},{18,26},{11,3},{19,27},{12,4},{... | collective-permute-start | bytes 2359304 | tf_op jit(solution)/shard_map/cond/branch_1_fun/ppermute | solution.py:228
  268.5 59.1 %collective-permute-start.31 = (bf16[24,128,128]{2,1,0:T(8,128)(2,1)S(1)}, bf16[24,128,128]{2,1,0:T(8,128)(2,1)S(1)}, u32[]{:S(2)}, u32[]{:S(2)}) collective-permute-start(bf16[24,128,128]{2,1,0:T(8,128)(2,1)S(1)} %add_tiles.34.refs_0_), channel_id=1, source_target_pairs={{8,0},{16,24},{9,1},{17,25},{10,2},{18,26},{11,3},{19,27},{12,4},{... | collective-permute-start | bytes 2359304 | tf_op jit(solution)/shard_map/cond/branch_1_fun/ppermute | solution.py:228
  286.3 45.6 %collective-permute-start.32 = (bf16[24,128,128]{2,1,0:T(8,128)(2,1)}, bf16[24,128,128]{2,1,0:T(8,128)(2,1)S(1)}, u32[]{:S(2)}, u32[]{:S(2)}) collective-permute-start(bf16[24,128,128]{2,1,0:T(8,128)(2,1)} %add_tiles.35), channel_id=1, source_target_pairs={{8,0},{16,24},{9,1},{17,25},{10,2},{18,26},{11,3},{19,27},{12,4},{... | collective-permute-start | bytes 2359304 | tf_op jit(solution)/shard_map/cond/branch_1_fun/ppermute | solution.py:228
  (45 other events, 688.9 us)

commit v4 on v3

--- a/solution.py
+++ b/solution.py
@@ -20,7 +20,7 @@
 CHUNK = 24
 ALONE, ONE_BEFORE, FIRST_PAIR, LAST_PAIR = 24, 72, 120, 192
 LIST_ENTRIES = FIRST_PAIR + LAST_PAIR
-FIRST_DONE = 240
+FIRST_DONE = 264
 NOWHERE = 1 << 15
 ROW_TILE = 4
 SUM_VMEM_BYTES = 24 * 1024 * 1024

time: 361 us -> 361 us (level)
  transfers between devices with their start and end apart: 37 -> 37, of which waited for: 18 -> 17; matrix products, arithmetic and copies ran while one was open for 2% -> 2% of each run, Pallas kernels for 20% -> 20%
where the time goes in v4:
time: 361 us; the launch traced here: 360 us
  waiting for transfers between devices  155 us (43%)
  Pallas kernels  99.2 us (27%)
  starting transfers between devices  86.9 us (24%)
  local copies, waits for them, and re-layouts  8.83 us (2%)
  other arithmetic  7.08 us (2%)
    ppermute x13, waiting for transfers between devices, leave(): outward[chunk] = lax.ppermute(moving, 'row', OUTWARD)  94.3 us
    pallas_call x2, Pallas kernels, contracted(): pl.pallas_call(kernel, out_shape=jax.ShapeDtypeStruct((ROW_BLOCKS_DEV * t...  53.3 us
    ppermute x7, starting transfers between devices, enter(): inward[chunk] = lax.ppermute(listed[0, chunk], 'row', INWARD)  41.3 us
    all_to_all x2, waiting for transfers between devices, exchanged(): lax.all_to_all(chosen, 'col', split_axis=0, concat_axis=0, tiled=True)  36.6 us
    pallas_call x5, Pallas kernels, listed_sums(): pl.pallas_call(kernel, out_shape=[jax.ShapeDtypeStruct((CHUNK,) + tile, g...  30.3 us
    ppermute x7, waiting for transfers between devices, enter(): inward[chunk] = lax.ppermute(listed[0, chunk], 'row', INWARD)  22.7 us
    ppermute x13, starting transfers between devices, leave(): outward[chunk] = lax.ppermute(moving, 'row', OUTWARD)  16.8 us
    all_to_all x2, starting transfers between devices, exchanged(): lax.all_to_all(chosen, 'col', split_axis=0, concat_axis=0, tiled=True)  9.13 us
  transfers between devices with their start and end apart: 37, of which 17 were waited for; matrix products, arithmetic and copies ran while one was open for 2% of the time, Pallas kernels for 20%

profile of v4, /device:TPU:0, one launch (start us, length us, event | category | flops | bytes accessed | tf_op | source)
XLA Modules:
  0.0 359.7 jit_solution(3013577261577449582)
XLA Ops:
  2.2 7.3 %all-to-all-start.3 = ((s32[32,1,128]{2,1,0:T(1,128)}), s32[32,1,128]{2,1,0:T(1,128)S(1)}, u32[]{:S(2)}, u32[]{:S(2)}) async-start(s32[32,1,128]{2,1,0:T(1,128)} %broadcast_in_dim.161), calls=%async_computation.3 | async-start | bytes 32768 | tf_op jit(solution)/shard_map/all_to_all | solution.py:388
  16.6 4.6 %all-to-all-start.4 = ((bf16[128,128,128]{2,1,0:T(8,128)(2,1)}), bf16[128,128,128]{2,1,0:T(8,128)(2,1)}, u32[]{:S(2)}, u32[]{:S(2)}) async-start(bf16[128,128,128]{2,1,0:T(8,128)(2,1)} %copy-done.3), calls=%async_computation.4 | async-start | bytes 8388608 | tf_op jit(solution)/shard_map/all_to_all | solution.py:395
  27.0 5.1 %pick_tiles.2 = bf16[128,128,128]{2,1,0:T(8,128)(2,1)} custom-call(s32[128]{0:T(128)S(1)} %slice_bitcast_fusion.source_ref, bf16[128,128,128]{2,1,0:T(8,128)(2,1)} %tiles_ref.3), custom_call_target="tpu_custom_call" | custom-call | flops 1000 | bytes 1000 | tf_op jit(solution)/shard_map/pick_tiles/pallas_call | solution.py:95
  33.7 36.6 %all-to-all-done.4 = bf16[128,128,128]{2,1,0:T(8,128)(2,1)} async-done(((bf16[128,128,128]{2,1,0:T(8,128)(2,1)}), bf16[128,128,128]{2,1,0:T(8,128)(2,1)}, u32[]{:S(2)}, u32[]{:S(2)}) %all-to-all-start.4) | async-done | bytes 4194336 | tf_op jit(solution)/shard_map/all_to_all | solution.py:395
  70.3 289.2 %conditional.1 = (bf16[3072,2048]{1,0:T(8,128)(2,1)}) conditional(s32[]{:T(128)} %convert_element_type.46, (s32[128,1]{0,1:T(1,128)S(1)}, s32[128]{0:T(128)S(1)}, bf16[128,128,128]{2,1,0:T(8,128)(2,1)}, bf16[512,2048]{1,0:T(8,128)(2,1)}) %tuple.61, (s32[]{:T(128)}, s32[]{:T(128)}, pred[]{:T(512)}, s32[1,2,2,96]{3,2,1,0:T(2,128)S(1)}, ...), branch_computations={%region_12.16_spmd, %region_16.17_spmd} | conditional | flops 26606317568 | bytes 347144256 | solution.py:523
  70.4 4.6 %all-to-all-start = ((bf16[128,128,128]{2,1,0:T(8,128)(2,1)}), bf16[128,128,128]{2,1,0:T(8,128)(2,1)}, u32[]{:S(2)}, u32[]{:S(2)}) async-start(bf16[128,128,128]{2,1,0:T(8,128)(2,1)} %get-tuple-element.104), calls=%async_computation | async-start | bytes 8388608 | tf_op jit(solution)/shard_map/cond/branch_1_fun/all_to_all | solution.py:395
  75.0 4.4 %sum_tiles.5 = (bf16[24,128,128]{2,1,0:T(8,128)(2,1)S(1)}, bf16[24,128,128]{2,1,0:T(8,128)(2,1)S(1)}, bf16[24,128,128]{2,1,0:T(8,128)(2,1)S(1)}) custom-call(s32[2,256]{1,0:T(2,128)S(1)} %get-tuple-element.99.order_ref, s32[2,313]{1,0:T(2,128)S(1)} %fusion.bounds_ref, bf16[128,128,128]{2,1,0:T(8,128)(2,1)} %get-tuple-element.103.refs_0_), custom_call_target="tpu_custom_call" | custom-call | flops 1000 | bytes 1000 | tf_op jit(solution)/shard_map/cond/branch_1_fun/sum_tiles/pallas_call | solution.py:151
  80.1 5.4 %collective-permute-start = (bf16[24,128,128]{2,1,0:T(8,128)(2,1)S(1)}, bf16[24,128,128]{2,1,0:T(8,128)(2,1)S(1)}, u32[]{:S(2)}, u32[]{:S(2)}) collective-permute-start(bf16[24,128,128]{2,1,0:T(8,128)(2,1)S(1)} %get-tuple-element.107.one_ref), channel_id=1, source_target_pairs={{0,8},{24,16},{1,9},{25,17},{2,10},{26,18},{3,11},{27,19},{4,12},{... | collective-permute-start | bytes 2359304 | tf_op jit(solution)/shard_map/cond/branch_1_fun/ppermute | solution.py:212
  86.8 5.6 %sum_tiles.6 = (bf16[24,128,128]{2,1,0:T(8,128)(2,1)S(1)}, bf16[24,128,128]{2,1,0:T(8,128)(2,1)S(1)}, bf16[24,128,128]{2,1,0:T(8,128)(2,1)S(1)}, bf16[24,128,128...) custom-call(s32[2,256]{1,0:T(2,128)S(1)} %get-tuple-element.99.order_ref, ...), custom_call_target="tpu_custom_call" | custom-call | flops 1000 | bytes 1000 | tf_op jit(solution)/shard_map/cond/branch_1_fun/sum_tiles/pallas_call | solution.py:151
  94.1 6.5 %collective-permute-start.3 = (bf16[24,128,128]{2,1,0:T(8,128)(2,1)S(1)}, bf16[24,128,128]{2,1,0:T(8,128)(2,1)S(1)}, u32[]{:S(2)}, u32[]{:S(2)}) collective-permute-start(bf16[24,128,128]{2,1,0:T(8,128)(2,1)S(1)} %get-tuple-element.111.one_ref), channel_id=1, source_target_pairs={{0,8},{24,16},{1,9},{25,17},{2,10},{26,18},{3,11},{27,19},{4,12},{... | collective-permute-start | bytes 2359304 | tf_op jit(solution)/shard_map/cond/branch_1_fun/ppermute | solution.py:212
  104.3 3.5 collective-permute-done.5.refs_1_.refs_18_
  109.1 10.4 %collective-permute-done.3.other_ref = bf16[24,128,128]{2,1,0:T(8,128)(2,1)S(1)} collective-permute-done((bf16[24,128,128]{2,1,0:T(8,128)(2,1)S(1)}, bf16[24,128,128]{2,1,0:T(8,128)(2,1)S(1)}, u32[]{:S(2)}, u32[]{:S(2)}) %collective-permute-start.3) | collective-permute-done | bytes 786464 | tf_op jit(solution)/shard_map/cond/branch_1_fun/ppermute | solution.py:212
  126.6 7.5 %sum_tiles.7 = (bf16[24,128,128]{2,1,0:T(8,128)(2,1)S(1)}, bf16[24,128,128]{2,1,0:T(8,128)(2,1)S(1)}, bf16[24,128,128]{2,1,0:T(8,128)(2,1)S(1)}, bf16[24,128,128...) custom-call(s32[2,256]{1,0:T(2,128)S(1)} %get-tuple-element.99.order_ref, ...), custom_call_target="tpu_custom_call" | custom-call | flops 1000 | bytes 1000 | tf_op jit(solution)/shard_map/cond/branch_1_fun/sum_tiles/pallas_call | solution.py:151
  134.2 9.0 %collective-permute-done.10.refs_1_.refs_20_ = bf16[24,128,128]{2,1,0:T(8,128)(2,1)} collective-permute-done((bf16[24,128,128]{2,1,0:T(8,128)(2,1)}, bf16[24,128,128]{2,1,0:T(8,128)(2,1)}, u32[]{:S(2)}, u32[]{:S(2)}) %collective-permute-start.10) | collective-permute-done | bytes 786464 | tf_op jit(solution)/shard_map/cond/branch_1_fun/ppermute | solution.py:228
  146.5 14.2 %collective-permute-start.7 = (bf16[24,128,128]{2,1,0:T(8,128)(2,1)S(1)}, bf16[24,128,128]{2,1,0:T(8,128)(2,1)S(1)}, u32[]{:S(2)}, u32[]{:S(2)}) collective-permute-start(bf16[24,128,128]{2,1,0:T(8,128)(2,1)S(1)} %get-tuple-element.115.one_ref), channel_id=1, source_target_pairs={{0,8},{24,16},{1,9},{25,17},{2,10},{26,18},{3,11},{27,19},{4,12},{... | collective-permute-start | bytes 2359304 | tf_op jit(solution)/shard_map/cond/branch_1_fun/ppermute | solution.py:212
  162.0 11.7 %collective-permute-done.11.refs_1_.refs_22_ = bf16[24,128,128]{2,1,0:T(8,128)(2,1)S(1)} collective-permute-done((bf16[24,128,128]{2,1,0:T(8,128)(2,1)S(1)}, bf16[24,128,128]{2,1,0:T(8,128)(2,1)S(1)}, u32[]{:S(2)}, u32[]{:S(2)}) %collective-permute-start.11) | collective-permute-done | bytes 786464 | tf_op jit(solution)/shard_map/cond/branch_1_fun/ppermute | solution.py:228
  177.1 4.8 %collective-permute-start.12 = (bf16[24,128,128]{2,1,0:T(8,128)(2,1)S(1)}, bf16[24,128,128]{2,1,0:T(8,128)(2,1)S(1)}, u32[]{:S(2)}, u32[]{:S(2)}) collective-permute-start(bf16[24,128,128]{2,1,0:T(8,128)(2,1)S(1)} %get-tuple-element.118.one_ref), channel_id=1, source_target_pairs={{0,8},{24,16},{1,9},{25,17},{2,10},{26,18},{3,11},{27,19},{4,12},{... | collective-permute-start | bytes 2359304 | tf_op jit(solution)/shard_map/cond/branch_1_fun/ppermute | solution.py:212
  182.9 6.6 %collective-permute-done.14.refs_1_.refs_23_.refs_14_ = bf16[24,128,128]{2,1,0:T(8,128)(2,1)S(1)} collective-permute-done((bf16[24,128,128]{2,1,0:T(8,128)(2,1)S(1)}, bf16[24,128,128]{2,1,0:T(8,128)(2,1)S(1)}, u32[]{:S(2)}, u32[]{:S(2)}) %collective-permute-start.14) | collective-permute-done | bytes 786464 | tf_op jit(solution)/shard_map/cond/branch_1_fun/ppermute | solution.py:228
  190.8 7.4 %sum_tiles.8 = (bf16[24,128,128]{2,1,0:T(8,128)(2,1)S(1)}, bf16[24,128,128]{2,1,0:T(8,128)(2,1)S(1)}, bf16[24,128,128]{2,1,0:T(8,128)(2,1)S(1)}, bf16[24,128,128...) custom-call(s32[2,256]{1,0:T(2,128)S(1)} %get-tuple-element.99.order_ref, ...), custom_call_target="tpu_custom_call" | custom-call | flops 1000 | bytes 1000 | tf_op jit(solution)/shard_map/cond/branch_1_fun/sum_tiles/pallas_call | solution.py:151
  198.2 4.5 %collective-permute-start.16 = (bf16[24,128,128]{2,1,0:T(8,128)(2,1)S(1)}, bf16[24,128,128]{2,1,0:T(8,128)(2,1)S(1)}, u32[]{:S(2)}, u32[]{:S(2)}) collective-permute-start(bf16[24,128,128]{2,1,0:T(8,128)(2,1)S(1)} %get-tuple-element.120.refs_0_.one_ref), channel_id=1, source_target_pairs={{0,8},{24,16},{1,9},{25,17},{2,10},{26,18},{3,11},{27,19},{4,12},{... | collective-permute-start | bytes 2359304 | tf_op jit(solution)/shard_map/cond/branch_1_fun/ppermute | solution.py:212
  205.2 4.8 %collective-permute-done.18.refs_1_.refs_24_.refs_15_ = bf16[24,128,128]{2,1,0:T(8,128)(2,1)S(1)} collective-permute-done((bf16[24,128,128]{2,1,0:T(8,128)(2,1)S(1)}, bf16[24,128,128]{2,1,0:T(8,128)(2,1)S(1)}, u32[]{:S(2)}, u32[]{:S(2)}) %collective-permute-start.18) | collective-permute-done | bytes 786464 | tf_op jit(solution)/shard_map/cond/branch_1_fun/ppermute | solution.py:228
  210.2 8.0 %collective-permute-done.16.other_ref = bf16[24,128,128]{2,1,0:T(8,128)(2,1)S(1)} collective-permute-done((bf16[24,128,128]{2,1,0:T(8,128)(2,1)S(1)}, bf16[24,128,128]{2,1,0:T(8,128)(2,1)S(1)}, u32[]{:S(2)}, u32[]{:S(2)}) %collective-permute-start.16) | collective-permute-done | bytes 786464 | tf_op jit(solution)/shard_map/cond/branch_1_fun/ppermute | solution.py:212
  218.1 4.4 %collective-permute-start.19 = (bf16[24,128,128]{2,1,0:T(8,128)(2,1)S(1)}, bf16[24,128,128]{2,1,0:T(8,128)(2,1)S(1)}, u32[]{:S(2)}, u32[]{:S(2)}) collective-permute-start(bf16[24,128,128]{2,1,0:T(8,128)(2,1)S(1)} %get-tuple-element.124.one_ref), channel_id=1, source_target_pairs={{0,8},{24,16},{1,9},{25,17},{2,10},{26,18},{3,11},{27,19},{4,12},{... | collective-permute-start | bytes 2359304 | tf_op jit(solution)/shard_map/cond/branch_1_fun/ppermute | solution.py:212
  224.9 9.8 %collective-permute-done.21.refs_1_.refs_25_.refs_16_ = bf16[24,128,128]{2,1,0:T(8,128)(2,1)S(1)} collective-permute-done((bf16[24,128,128]{2,1,0:T(8,128)(2,1)S(1)}, bf16[24,128,128]{2,1,0:T(8,128)(2,1)S(1)}, u32[]{:S(2)}, u32[]{:S(2)}) %collective-permute-start.21) | collective-permute-done | bytes 786464 | tf_op jit(solution)/shard_map/cond/branch_1_fun/ppermute | solution.py:228
  236.1 5.5 %sum_tiles.9 = (bf16[24,128,128]{2,1,0:T(8,128)(2,1)S(1)}, bf16[24,128,128]{2,1,0:T(8,128)(2,1)S(1)}, bf16[24,128,128]{2,1,0:T(8,128)(2,1)S(1)}) custom-call(s32[2,256]{1,0:T(2,128)S(1)} %get-tuple-element.99.order_ref, s32[2,313]{1,0:T(2,128)S(1)} %fusion.bounds_ref, bf16[128,128,128]{2,1,0:T(8,128)(2,1)} %get-tuple-element.103.refs_0_, ...), custom_call_target="tpu_custom_call" | custom-call | flops 1000 | bytes 1000 | tf_op jit(solution)/shard_map/cond/branch_1_fun/sum_tiles/pallas_call | solution.py:151
  243.3 7.6 %collective-permute-done.25.refs_1_.refs_26_.refs_17_ = bf16[24,128,128]{2,1,0:T(8,128)(2,1)S(1)} collective-permute-done((bf16[24,128,128]{2,1,0:T(8,128)(2,1)S(1)}, bf16[24,128,128]{2,1,0:T(8,128)(2,1)S(1)}, u32[]{:S(2)}, u32[]{:S(2)}) %collective-permute-start.25) | collective-permute-done | bytes 786464 | tf_op jit(solution)/shard_map/cond/branch_1_fun/ppermute | solution.py:228
  258.6 7.9 %collective-permute-done.28.refs_1_.refs_27_.refs_18_ = bf16[24,128,128]{2,1,0:T(8,128)(2,1)S(1)} collective-permute-done((bf16[24,128,128]{2,1,0:T(8,128)(2,1)S(1)}, bf16[24,128,128]{2,1,0:T(8,128)(2,1)S(1)}, u32[]{:S(2)}, u32[]{:S(2)}) %collective-permute-start.28) | collective-permute-done | bytes 786464 | tf_op jit(solution)/shard_map/cond/branch_1_fun/ppermute | solution.py:228
  268.1 15.3 %collective-permute-done.29.refs_1_.refs_28_.refs_19_ = bf16[24,128,128]{2,1,0:T(8,128)(2,1)S(1)} collective-permute-done((bf16[24,128,128]{2,1,0:T(8,128)(2,1)S(1)}, bf16[24,128,128]{2,1,0:T(8,128)(2,1)S(1)}, u32[]{:S(2)}, u32[]{:S(2)}) %collective-permute-start.29) | collective-permute-done | bytes 786464 | tf_op jit(solution)/shard_map/cond/branch_1_fun/ppermute | solution.py:228
  287.3 13.1 %collective-permute-done.33.refs_21_ = bf16[24,128,128]{2,1,0:T(8,128)(2,1)} collective-permute-done((bf16[24,128,128]{2,1,0:T(8,128)(2,1)}, bf16[24,128,128]{2,1,0:T(8,128)(2,1)}, u32[]{:S(2)}, u32[]{:S(2)}) %collective-permute-start.33) | collective-permute-done | bytes 786464 | tf_op jit(solution)/shard_map/cond/branch_1_fun/ppermute | solution.py:228
  300.4 26.0 %contract_panels.2.refs_26_ = f32[3072,2048]{1,0:T(8,128)} custom-call(s32[2]{0:T(128)} %pad_add_fusion.place_ref, s32[384]{0:T(512)} %get-tuple-element.200.first_ref, s32[384]{0:T(512)} %get-tuple-element.199.second_ref, bf16[24,128,128]{2,1,0:T(8,128)(2,1)} %copy-done.35, bf16[24,128,128]{2,1,0:T(8,128)(2,1)} %copy-done.27, ...), custom_call_target="tpu_custom_call" | custom-call | flops 1000 | bytes 1000 | tf_op jit(solution)/shard_map/cond/branch_1_fun/contract_panels/pallas_call | solution.py:353
  326.3 5.0 %collective-permute-done.32.refs_21_ = bf16[24,128,128]{2,1,0:T(8,128)(2,1)S(1)} collective-permute-done((bf16[24,128,128]{2,1,0:T(8,128)(2,1)}, bf16[24,128,128]{2,1,0:T(8,128)(2,1)S(1)}, u32[]{:S(2)}, u32[]{:S(2)}) %collective-permute-start.32) | collective-permute-done | bytes 786464 | tf_op jit(solution)/shard_map/cond/branch_1_fun/ppermute | solution.py:228
  332.2 27.3 %contract_panels.3 = bf16[3072,2048]{1,0:T(8,128)(2,1)} custom-call(s32[2]{0:T(128)} %pad_add_fusion.place_ref, s32[384]{0:T(512)} %get-tuple-element.200.first_ref, s32[384]{0:T(512)} %get-tuple-element.199.second_ref, bf16[24,128,128]{2,1,0:T(8,128)(2,1)} %copy-done.9, bf16[24,128,128]{2,1,0:T(8,128)(2,1)} %copy-done.25, bf16[24,128,128]{2,1,0:T(8,128)(2,1)} %copy-done.4, ...), custom_call_target="tpu_custom_call" | custom-call | flops 1000 | bytes 1000 | tf_op jit(solution)/shard_map/cond/branch_1_fun/contract_panels/pallas_call | solution.py:353
  (229 shorter events, 63.4 us)
Async XLA Ops:
  16.6 53.7 %all-to-all-start.4 = ((bf16[128,128,128]{2,1,0:T(8,128)(2,1)}), bf16[128,128,128]{2,1,0:T(8,128)(2,1)}, u32[]{:S(2)}, u32[]{:S(2)}) async-start(bf16[128,128,128]{2,1,0:T(8,128)(2,1)} %copy-done.3), calls=%async_computation.4 | async-start | bytes 8388608 | tf_op jit(solution)/shard_map/all_to_all | solution.py:395
  70.4 56.3 %all-to-all-start = ((bf16[128,128,128]{2,1,0:T(8,128)(2,1)}), bf16[128,128,128]{2,1,0:T(8,128)(2,1)}, u32[]{:S(2)}, u32[]{:S(2)}) async-start(bf16[128,128,128]{2,1,0:T(8,128)(2,1)} %get-tuple-element.104), calls=%async_computation | async-start | bytes 8388608 | tf_op jit(solution)/shard_map/cond/branch_1_fun/all_to_all | solution.py:395
  79.3 21.3 %collective-permute-start.1 = (bf16[24,128,128]{2,1,0:T(8,128)(2,1)S(1)}, bf16[24,128,128]{2,1,0:T(8,128)(2,1)S(1)}, u32[]{:S(2)}, u32[]{:S(2)}) collective-permute-start(bf16[24,128,128]{2,1,0:T(8,128)(2,1)S(1)} %get-tuple-element.109.refs_0_), channel_id=1, source_target_pairs={{8,16},{16,8},{9,17},{17,9},{10,18},{18,10},{11,19},{19,11},{12,20... | collective-permute-start | bytes 2359304 | tf_op jit(solution)/shard_map/cond/branch_1_fun/ppermute | solution.py:219
  80.1 23.3 %collective-permute-start = (bf16[24,128,128]{2,1,0:T(8,128)(2,1)S(1)}, bf16[24,128,128]{2,1,0:T(8,128)(2,1)S(1)}, u32[]{:S(2)}, u32[]{:S(2)}) collective-permute-start(bf16[24,128,128]{2,1,0:T(8,128)(2,1)S(1)} %get-tuple-element.107.one_ref), channel_id=1, source_target_pairs={{0,8},{24,16},{1,9},{25,17},{2,10},{26,18},{3,11},{27,19},{4,12},{... | collective-permute-start | bytes 2359304 | tf_op jit(solution)/shard_map/cond/branch_1_fun/ppermute | solution.py:212
  85.5 22.3 %collective-permute-start.5 = (bf16[24,128,128]{2,1,0:T(8,128)(2,1)S(1)}, bf16[24,128,128]{2,1,0:T(8,128)(2,1)S(1)}, u32[]{:S(2)}, u32[]{:S(2)}) collective-permute-start(bf16[24,128,128]{2,1,0:T(8,128)(2,1)S(1)} %get-tuple-element.105.refs_1_), channel_id=1, source_target_pairs={{8,0},{16,24},{9,1},{17,25},{10,2},{18,26},{11,3},{19,27},{12,4},{... | collective-permute-start | bytes 2359304 | tf_op jit(solution)/shard_map/cond/branch_1_fun/ppermute | solution.py:228
  94.1 25.4 %collective-permute-start.3 = (bf16[24,128,128]{2,1,0:T(8,128)(2,1)S(1)}, bf16[24,128,128]{2,1,0:T(8,128)(2,1)S(1)}, u32[]{:S(2)}, u32[]{:S(2)}) collective-permute-start(bf16[24,128,128]{2,1,0:T(8,128)(2,1)S(1)} %get-tuple-element.111.one_ref), channel_id=1, source_target_pairs={{0,8},{24,16},{1,9},{25,17},{2,10},{26,18},{3,11},{27,19},{4,12},{... | collective-permute-start | bytes 2359304 | tf_op jit(solution)/shard_map/cond/branch_1_fun/ppermute | solution.py:212
  100.8 23.0 %collective-permute-start.6 = (bf16[24,128,128]{2,1,0:T(8,128)(2,1)S(1)}, bf16[24,128,128]{2,1,0:T(8,128)(2,1)S(1)}, u32[]{:S(2)}, u32[]{:S(2)}) collective-permute-start(bf16[24,128,128]{2,1,0:T(8,128)(2,1)S(1)} %add_tiles.18.refs_0_), channel_id=1, source_target_pairs={{8,0},{16,24},{9,1},{17,25},{10,2},{18,26},{11,3},{19,27},{12,4},{... | collective-permute-start | bytes 2359304 | tf_op jit(solution)/shard_map/cond/branch_1_fun/ppermute | solution.py:228
  103.5 20.2 %collective-permute-start.2 = (bf16[24,128,128]{2,1,0:T(8,128)(2,1)S(1)}, bf16[24,128,128]{2,1,0:T(8,128)(2,1)S(1)}, u32[]{:S(2)}, u32[]{:S(2)}) collective-permute-start(bf16[24,128,128]{2,1,0:T(8,128)(2,1)S(1)} %add_tiles.19.refs_0_.refs_2_), channel_id=1, source_target_pairs={{8,16},{16,8},{9,17},{17,9},{10,18},{18,10},{11,19},{19,11},{12,20... | collective-permute-start | bytes 2359304 | tf_op jit(solution)/shard_map/cond/branch_1_fun/ppermute | solution.py:219
  121.2 21.9 %collective-permute-start.10 = (bf16[24,128,128]{2,1,0:T(8,128)(2,1)}, bf16[24,128,128]{2,1,0:T(8,128)(2,1)}, u32[]{:S(2)}, u32[]{:S(2)}) collective-permute-start(bf16[24,128,128]{2,1,0:T(8,128)(2,1)} %add_tiles.20.refs_0_), channel_id=1, source_target_pairs={{8,0},{16,24},{9,1},{17,25},{10,2},{18,26},{11,3},{19,27},{12,4},{... | collective-permute-start | bytes 2359304 | tf_op jit(solution)/shard_map/cond/branch_1_fun/ppermute | solution.py:228
  122.5 59.6 %collective-permute-start.15 = (bf16[512,2048]{1,0:T(8,128)(2,1)}, bf16[512,2048]{1,0:T(8,128)(2,1)S(1)}, u32[]{:S(2)}, u32[]{:S(2)}) collective-permute-start(bf16[512,2048]{1,0:T(8,128)(2,1)} %get-tuple-element.122.refs_29_.refs_22_), channel_id=1, source_target_pairs={{0,7},{1,0},{2,1},{3,2},{4,3},{5,4},{6,5},{7,6},{8,15},{9,8},{10,9... | collective-permute-start | bytes 6291464 | tf_op jit(solution)/shard_map/cond/branch_1_fun/ppermute | solution.py:34
  144.5 29.2 %collective-permute-start.11 = (bf16[24,128,128]{2,1,0:T(8,128)(2,1)S(1)}, bf16[24,128,128]{2,1,0:T(8,128)(2,1)S(1)}, u32[]{:S(2)}, u32[]{:S(2)}) collective-permute-start(bf16[24,128,128]{2,1,0:T(8,128)(2,1)S(1)} %add_tiles.23.refs_0_), channel_id=1, source_target_pairs={{8,0},{16,24},{9,1},{17,25},{10,2},{18,26},{11,3},{19,27},{12,4},{... | collective-permute-start | bytes 2359304 | tf_op jit(solution)/shard_map/cond/branch_1_fun/ppermute | solution.py:228
  145.8 30.4 %collective-permute-start.8 = (bf16[24,128,128]{2,1,0:T(8,128)(2,1)S(1)}, bf16[24,128,128]{2,1,0:T(8,128)(2,1)S(1)}, u32[]{:S(2)}, u32[]{:S(2)}) collective-permute-start(bf16[24,128,128]{2,1,0:T(8,128)(2,1)S(1)} %get-tuple-element.113.refs_0_.refs_4_), channel_id=1, source_target_pairs={{8,16},{16,8},{9,17},{17,9},{10,18},{18,10},{11,19},{19,11},{12,20... | collective-permute-start | bytes 2359304 | tf_op jit(solution)/shard_map/cond/branch_1_fun/ppermute | solution.py:219
  146.5 30.6 %collective-permute-start.7 = (bf16[24,128,128]{2,1,0:T(8,128)(2,1)S(1)}, bf16[24,128,128]{2,1,0:T(8,128)(2,1)S(1)}, u32[]{:S(2)}, u32[]{:S(2)}) collective-permute-start(bf16[24,128,128]{2,1,0:T(8,128)(2,1)S(1)} %get-tuple-element.115.one_ref), channel_id=1, source_target_pairs={{0,8},{24,16},{1,9},{25,17},{2,10},{26,18},{3,11},{27,19},{4,12},{... | collective-permute-start | bytes 2359304 | tf_op jit(solution)/shard_map/cond/branch_1_fun/ppermute | solution.py:212
  160.7 28.8 %collective-permute-start.14 = (bf16[24,128,128]{2,1,0:T(8,128)(2,1)S(1)}, bf16[24,128,128]{2,1,0:T(8,128)(2,1)S(1)}, u32[]{:S(2)}, u32[]{:S(2)}) collective-permute-start(bf16[24,128,128]{2,1,0:T(8,128)(2,1)S(1)} %get-tuple-element.121), channel_id=1, source_target_pairs={{8,0},{16,24},{9,1},{17,25},{10,2},{18,26},{11,3},{19,27},{12,4},{... | collective-permute-start | bytes 2359304 | tf_op jit(solution)/shard_map/cond/branch_1_fun/ppermute | solution.py:228
  173.6 49.2 %collective-permute-start.22 = (bf16[512,2048]{1,0:T(8,128)(2,1)}, bf16[512,2048]{1,0:T(8,128)(2,1)S(1)}, u32[]{:S(2)}, u32[]{:S(2)}) collective-permute-start(bf16[512,2048]{1,0:T(8,128)(2,1)} %get-tuple-element.122.refs_29_.refs_22_), channel_id=1, source_target_pairs={{0,6},{1,7},{2,0},{3,1},{4,2},{5,3},{6,4},{7,5},{8,14},{9,15},{10,... | collective-permute-start | bytes 6291464 | tf_op jit(solution)/shard_map/cond/branch_1_fun/ppermute | solution.py:34
  176.2 22.0 %collective-permute-start.13 = (bf16[24,128,128]{2,1,0:T(8,128)(2,1)S(1)}, bf16[24,128,128]{2,1,0:T(8,128)(2,1)S(1)}, u32[]{:S(2)}, u32[]{:S(2)}) collective-permute-start(bf16[24,128,128]{2,1,0:T(8,128)(2,1)S(1)} %get-tuple-element.114.refs_5_.refs_1_), channel_id=1, source_target_pairs={{8,16},{16,8},{9,17},{17,9},{10,18},{18,10},{11,19},{19,11},{12,20... | collective-permute-start | bytes 2359304 | tf_op jit(solution)/shard_map/cond/branch_1_fun/ppermute | solution.py:219
  177.1 25.8 %collective-permute-start.12 = (bf16[24,128,128]{2,1,0:T(8,128)(2,1)S(1)}, bf16[24,128,128]{2,1,0:T(8,128)(2,1)S(1)}, u32[]{:S(2)}, u32[]{:S(2)}) collective-permute-start(bf16[24,128,128]{2,1,0:T(8,128)(2,1)S(1)} %get-tuple-element.118.one_ref), channel_id=1, source_target_pairs={{0,8},{24,16},{1,9},{25,17},{2,10},{26,18},{3,11},{27,19},{4,12},{... | collective-permute-start | bytes 2359304 | tf_op jit(solution)/shard_map/cond/branch_1_fun/ppermute | solution.py:212
  182.2 21.7 %collective-permute-start.17 = (bf16[24,128,128]{2,1,0:T(8,128)(2,1)S(1)}, bf16[24,128,128]{2,1,0:T(8,128)(2,1)S(1)}, u32[]{:S(2)}, u32[]{:S(2)}) collective-permute-start(bf16[24,128,128]{2,1,0:T(8,128)(2,1)S(1)} %add_tiles.25.refs_2_.refs_6_), channel_id=1, source_target_pairs={{8,16},{16,8},{9,17},{17,9},{10,18},{18,10},{11,19},{19,11},{12,20... | collective-permute-start | bytes 2359304 | tf_op jit(solution)/shard_map/cond/branch_1_fun/ppermute | solution.py:219
  189.5 20.5 %collective-permute-start.18 = (bf16[24,128,128]{2,1,0:T(8,128)(2,1)S(1)}, bf16[24,128,128]{2,1,0:T(8,128)(2,1)S(1)}, u32[]{:S(2)}, u32[]{:S(2)}) collective-permute-start(bf16[24,128,128]{2,1,0:T(8,128)(2,1)S(1)} %add_tiles.24.refs_0_), channel_id=1, source_target_pairs={{8,0},{16,24},{9,1},{17,25},{10,2},{18,26},{11,3},{19,27},{12,4},{... | collective-permute-start | bytes 2359304 | tf_op jit(solution)/shard_map/cond/branch_1_fun/ppermute | solution.py:228
  198.2 19.9 %collective-permute-start.16 = (bf16[24,128,128]{2,1,0:T(8,128)(2,1)S(1)}, bf16[24,128,128]{2,1,0:T(8,128)(2,1)S(1)}, u32[]{:S(2)}, u32[]{:S(2)}) collective-permute-start(bf16[24,128,128]{2,1,0:T(8,128)(2,1)S(1)} %get-tuple-element.120.refs_0_.one_ref), channel_id=1, source_target_pairs={{0,8},{24,16},{1,9},{25,17},{2,10},{26,18},{3,11},{27,19},{4,12},{... | collective-permute-start | bytes 2359304 | tf_op jit(solution)/shard_map/cond/branch_1_fun/ppermute | solution.py:212
  203.1 21.0 %collective-permute-start.20 = (bf16[24,128,128]{2,1,0:T(8,128)(2,1)S(1)}, bf16[24,128,128]{2,1,0:T(8,128)(2,1)S(1)}, u32[]{:S(2)}, u32[]{:S(2)}) collective-permute-start(bf16[24,128,128]{2,1,0:T(8,128)(2,1)S(1)} %add_tiles.27.refs_0_.refs_7_.refs_3_), channel_id=1, source_target_pairs={{8,16},{16,8},{9,17},{17,9},{10,18},{18,10},{11,19},{19,11},{12,20... | collective-permute-start | bytes 2359304 | tf_op jit(solution)/shard_map/cond/branch_1_fun/ppermute | solution.py:219
  203.9 30.7 %collective-permute-start.21 = (bf16[24,128,128]{2,1,0:T(8,128)(2,1)S(1)}, bf16[24,128,128]{2,1,0:T(8,128)(2,1)S(1)}, u32[]{:S(2)}, u32[]{:S(2)}) collective-permute-start(bf16[24,128,128]{2,1,0:T(8,128)(2,1)S(1)} %add_tiles.26.refs_0_), channel_id=1, source_target_pairs={{8,0},{16,24},{9,1},{17,25},{10,2},{18,26},{11,3},{19,27},{12,4},{... | collective-permute-start | bytes 2359304 | tf_op jit(solution)/shard_map/cond/branch_1_fun/ppermute | solution.py:228
  210.0 47.3 %collective-permute-start.30 = (bf16[512,2048]{1,0:T(8,128)(2,1)}, bf16[512,2048]{1,0:T(8,128)(2,1)S(1)}, u32[]{:S(2)}, u32[]{:S(2)}) collective-permute-start(bf16[512,2048]{1,0:T(8,128)(2,1)} %get-tuple-element.122.refs_29_.refs_22_), channel_id=1, source_target_pairs={{0,5},{1,6},{2,7},{3,0},{4,1},{5,2},{6,3},{7,4},{8,13},{9,14},{10,... | collective-permute-start | bytes 6291464 | tf_op jit(solution)/shard_map/cond/branch_1_fun/ppermute | solution.py:34
  218.1 23.7 %collective-permute-start.19 = (bf16[24,128,128]{2,1,0:T(8,128)(2,1)S(1)}, bf16[24,128,128]{2,1,0:T(8,128)(2,1)S(1)}, u32[]{:S(2)}, u32[]{:S(2)}) collective-permute-start(bf16[24,128,128]{2,1,0:T(8,128)(2,1)S(1)} %get-tuple-element.124.one_ref), channel_id=1, source_target_pairs={{0,8},{24,16},{1,9},{25,17},{2,10},{26,18},{3,11},{27,19},{4,12},{... | collective-permute-start | bytes 2359304 | tf_op jit(solution)/shard_map/cond/branch_1_fun/ppermute | solution.py:212
  222.8 28.1 %collective-permute-start.25 = (bf16[24,128,128]{2,1,0:T(8,128)(2,1)S(1)}, bf16[24,128,128]{2,1,0:T(8,128)(2,1)S(1)}, u32[]{:S(2)}, u32[]{:S(2)}) collective-permute-start(bf16[24,128,128]{2,1,0:T(8,128)(2,1)S(1)} %add_tiles.28.refs_0_), channel_id=1, source_target_pairs={{8,0},{16,24},{9,1},{17,25},{10,2},{18,26},{11,3},{19,27},{12,4},{... | collective-permute-start | bytes 2359304 | tf_op jit(solution)/shard_map/cond/branch_1_fun/ppermute | solution.py:228
  224.1 27.5 %collective-permute-start.24 = (bf16[24,128,128]{2,1,0:T(8,128)(2,1)S(1)}, bf16[24,128,128]{2,1,0:T(8,128)(2,1)S(1)}, u32[]{:S(2)}, u32[]{:S(2)}) collective-permute-start(bf16[24,128,128]{2,1,0:T(8,128)(2,1)S(1)} %add_tiles.29.refs_2_.refs_8_.refs_4_), channel_id=1, source_target_pairs={{8,16},{16,8},{9,17},{17,9},{10,18},{18,10},{11,19},{19,11},{12,20... | collective-permute-start | bytes 2359304 | tf_op jit(solution)/shard_map/cond/branch_1_fun/ppermute | solution.py:219
  234.6 20.4 %collective-permute-start.23 = (bf16[24,128,128]{2,1,0:T(8,128)(2,1)S(1)}, bf16[24,128,128]{2,1,0:T(8,128)(2,1)S(1)}, u32[]{:S(2)}, u32[]{:S(2)}) collective-permute-start(bf16[24,128,128]{2,1,0:T(8,128)(2,1)S(1)} %get-tuple-element.127.one_ref), channel_id=1, source_target_pairs={{0,8},{24,16},{1,9},{25,17},{2,10},{26,18},{3,11},{27,19},{4,12},{... | collective-permute-start | bytes 2359304 | tf_op jit(solution)/shard_map/cond/branch_1_fun/ppermute | solution.py:212
  241.8 24.7 %collective-permute-start.28 = (bf16[24,128,128]{2,1,0:T(8,128)(2,1)S(1)}, bf16[24,128,128]{2,1,0:T(8,128)(2,1)S(1)}, u32[]{:S(2)}, u32[]{:S(2)}) collective-permute-start(bf16[24,128,128]{2,1,0:T(8,128)(2,1)S(1)} %add_tiles.30.refs_0_), channel_id=1, source_target_pairs={{8,0},{16,24},{9,1},{17,25},{10,2},{18,26},{11,3},{19,27},{12,4},{... | collective-permute-start | bytes 2359304 | tf_op jit(solution)/shard_map/cond/branch_1_fun/ppermute | solution.py:228
  256.0 27.4 %collective-permute-start.29 = (bf16[24,128,128]{2,1,0:T(8,128)(2,1)S(1)}, bf16[24,128,128]{2,1,0:T(8,128)(2,1)S(1)}, u32[]{:S(2)}, u32[]{:S(2)}) collective-permute-start(bf16[24,128,128]{2,1,0:T(8,128)(2,1)S(1)} %add_tiles.32.refs_0_), channel_id=1, source_target_pairs={{8,0},{16,24},{9,1},{17,25},{10,2},{18,26},{11,3},{19,27},{12,4},{... | collective-permute-start | bytes 2359304 | tf_op jit(solution)/shard_map/cond/branch_1_fun/ppermute | solution.py:228
  257.3 43.1 %collective-permute-start.33 = (bf16[24,128,128]{2,1,0:T(8,128)(2,1)}, bf16[24,128,128]{2,1,0:T(8,128)(2,1)}, u32[]{:S(2)}, u32[]{:S(2)}) collective-permute-start(bf16[24,128,128]{2,1,0:T(8,128)(2,1)} %add_tiles.22.refs_2_), channel_id=1, source_target_pairs={{8,0},{16,24},{9,1},{17,25},{10,2},{18,26},{11,3},{19,27},{12,4},{... | collective-permute-start | bytes 2359304 | tf_op jit(solution)/shard_map/cond/branch_1_fun/ppermute | solution.py:228
  266.7 59.6 %collective-permute-start.31 = (bf16[24,128,128]{2,1,0:T(8,128)(2,1)S(1)}, bf16[24,128,128]{2,1,0:T(8,128)(2,1)S(1)}, u32[]{:S(2)}, u32[]{:S(2)}) collective-permute-start(bf16[24,128,128]{2,1,0:T(8,128)(2,1)S(1)} %add_tiles.34.refs_0_), channel_id=1, source_target_pairs={{8,0},{16,24},{9,1},{17,25},{10,2},{18,26},{11,3},{19,27},{12,4},{... | collective-permute-start | bytes 2359304 | tf_op jit(solution)/shard_map/cond/branch_1_fun/ppermute | solution.py:228
  284.5 46.8 %collective-permute-start.32 = (bf16[24,128,128]{2,1,0:T(8,128)(2,1)}, bf16[24,128,128]{2,1,0:T(8,128)(2,1)S(1)}, u32[]{:S(2)}, u32[]{:S(2)}) collective-permute-start(bf16[24,128,128]{2,1,0:T(8,128)(2,1)} %add_tiles.35), channel_id=1, source_target_pairs={{8,0},{16,24},{9,1},{17,25},{10,2},{18,26},{11,3},{19,27},{12,4},{... | collective-permute-start | bytes 2359304 | tf_op jit(solution)/shard_map/cond/branch_1_fun/ppermute | solution.py:228
  (45 other events, 674.7 us)

commit v5 on v4

--- a/solution.py
+++ b/solution.py
@@ -23,7 +23,7 @@
 FIRST_DONE = 264
 NOWHERE = 1 << 15
 ROW_TILE = 4
-SUM_VMEM_BYTES = 24 * 1024 * 1024
+SUM_VMEM_BYTES = 18 * 1024 * 1024
 CONTRACT_VMEM_BYTES = 56 * 1024 * 1024
 SMALL = pl.CostEstimate(flops=1000, bytes_accessed=1000, transcendentals=0)
 
@@ -256,7 +256,7 @@
     row_count = len(slabs)
     panels = len(rows)
     steps = ROW_BLOCKS_DEV // ROW_TILE
-    col_tile = min(512, columns)
+    col_tile = min(1024, columns)
     both = sorted(near)
 
     def kernel(place_ref, first_ref, second_ref, *refs):

time: 361 us -> 361 us (level)
  no operation moved by 1% of the time
where the time goes in v5:
time: 361 us; the launch traced here: 359 us
  waiting for transfers between devices  155 us (43%)
  Pallas kernels  99.4 us (28%)
  starting transfers between devices  86.6 us (24%)
  local copies, waits for them, and re-layouts  8.83 us (2%)
  other arithmetic  7.08 us (2%)
    ppermute x13, waiting for transfers between devices, leave(): outward[chunk] = lax.ppermute(moving, 'row', OUTWARD)  95.2 us
    pallas_call x2, Pallas kernels, contracted(): pl.pallas_call(kernel, out_shape=jax.ShapeDtypeStruct((ROW_BLOCKS_DEV * t...  53.2 us
    ppermute x7, starting transfers between devices, enter(): inward[chunk] = lax.ppermute(listed[0, chunk], 'row', INWARD)  41.3 us
    all_to_all x2, waiting for transfers between devices, exchanged(): lax.all_to_all(chosen, 'col', split_axis=0, concat_axis=0, tiled=True)  36.6 us
    pallas_call x5, Pallas kernels, listed_sums(): pl.pallas_call(kernel, out_shape=[jax.ShapeDtypeStruct((CHUNK,) + tile, g...  30.6 us
    ppermute x7, waiting for transfers between devices, enter(): inward[chunk] = lax.ppermute(listed[0, chunk], 'row', INWARD)  21.6 us
    ppermute x13, starting transfers between devices, leave(): outward[chunk] = lax.ppermute(moving, 'row', OUTWARD)  16.8 us
    all_to_all x2, starting transfers between devices, exchanged(): lax.all_to_all(chosen, 'col', split_axis=0, concat_axis=0, tiled=True)  9.13 us
  transfers between devices with their start and end apart: 37, of which 17 were waited for; matrix products, arithmetic and copies ran while one was open for 2% of the time, Pallas kernels for 20%

profile of v5, /device:TPU:0, one launch (start us, length us, event | category | flops | bytes accessed | tf_op | source)
XLA Modules:
  0.0 359.4 jit_solution(1661994728513083753)
XLA Ops:
  2.2 7.3 %all-to-all-start.3 = ((s32[32,1,128]{2,1,0:T(1,128)}), s32[32,1,128]{2,1,0:T(1,128)S(1)}, u32[]{:S(2)}, u32[]{:S(2)}) async-start(s32[32,1,128]{2,1,0:T(1,128)} %broadcast_in_dim.161), calls=%async_computation.3 | async-start | bytes 32768 | tf_op jit(solution)/shard_map/all_to_all | solution.py:388
  16.6 4.6 %all-to-all-start.4 = ((bf16[128,128,128]{2,1,0:T(8,128)(2,1)}), bf16[128,128,128]{2,1,0:T(8,128)(2,1)}, u32[]{:S(2)}, u32[]{:S(2)}) async-start(bf16[128,128,128]{2,1,0:T(8,128)(2,1)} %copy-done.3), calls=%async_computation.4 | async-start | bytes 8388608 | tf_op jit(solution)/shard_map/all_to_all | solution.py:395
  27.0 5.1 %pick_tiles.2 = bf16[128,128,128]{2,1,0:T(8,128)(2,1)} custom-call(s32[128]{0:T(128)S(1)} %slice_bitcast_fusion.source_ref, bf16[128,128,128]{2,1,0:T(8,128)(2,1)} %tiles_ref.3), custom_call_target="tpu_custom_call" | custom-call | flops 1000 | bytes 1000 | tf_op jit(solution)/shard_map/pick_tiles/pallas_call | solution.py:95
  33.7 36.6 %all-to-all-done.4 = bf16[128,128,128]{2,1,0:T(8,128)(2,1)} async-done(((bf16[128,128,128]{2,1,0:T(8,128)(2,1)}), bf16[128,128,128]{2,1,0:T(8,128)(2,1)}, u32[]{:S(2)}, u32[]{:S(2)}) %all-to-all-start.4) | async-done | bytes 4194336 | tf_op jit(solution)/shard_map/all_to_all | solution.py:395
  70.3 288.9 %conditional.1 = (bf16[3072,2048]{1,0:T(8,128)(2,1)}) conditional(s32[]{:T(128)} %convert_element_type.46, (s32[128,1]{0,1:T(1,128)S(1)}, s32[128]{0:T(128)S(1)}, bf16[128,128,128]{2,1,0:T(8,128)(2,1)}, bf16[512,2048]{1,0:T(8,128)(2,1)}) %tuple.61, (s32[]{:T(128)}, s32[]{:T(128)}, pred[]{:T(512)}, s32[1,2,2,96]{3,2,1,0:T(2,128)S(1)}, ...), branch_computations={%region_12.16_spmd, %region_16.17_spmd} | conditional | flops 26606317568 | bytes 347144256 | solution.py:523
  70.4 4.6 %all-to-all-start = ((bf16[128,128,128]{2,1,0:T(8,128)(2,1)}), bf16[128,128,128]{2,1,0:T(8,128)(2,1)}, u32[]{:S(2)}, u32[]{:S(2)}) async-start(bf16[128,128,128]{2,1,0:T(8,128)(2,1)} %get-tuple-element.104), calls=%async_computation | async-start | bytes 8388608 | tf_op jit(solution)/shard_map/cond/branch_1_fun/all_to_all | solution.py:395
  75.0 4.6 %sum_tiles.5 = (bf16[24,128,128]{2,1,0:T(8,128)(2,1)S(1)}, bf16[24,128,128]{2,1,0:T(8,128)(2,1)S(1)}, bf16[24,128,128]{2,1,0:T(8,128)(2,1)S(1)}) custom-call(s32[2,256]{1,0:T(2,128)S(1)} %get-tuple-element.99.order_ref, s32[2,313]{1,0:T(2,128)S(1)} %fusion.bounds_ref, bf16[128,128,128]{2,1,0:T(8,128)(2,1)} %get-tuple-element.103.refs_0_), custom_call_target="tpu_custom_call" | custom-call | flops 1000 | bytes 1000 | tf_op jit(solution)/shard_map/cond/branch_1_fun/sum_tiles/pallas_call | solution.py:151
  80.3 5.4 %collective-permute-start = (bf16[24,128,128]{2,1,0:T(8,128)(2,1)S(1)}, bf16[24,128,128]{2,1,0:T(8,128)(2,1)S(1)}, u32[]{:S(2)}, u32[]{:S(2)}) collective-permute-start(bf16[24,128,128]{2,1,0:T(8,128)(2,1)S(1)} %get-tuple-element.107.one_ref), channel_id=1, source_target_pairs={{0,8},{24,16},{1,9},{25,17},{2,10},{26,18},{3,11},{27,19},{4,12},{... | collective-permute-start | bytes 2359304 | tf_op jit(solution)/shard_map/cond/branch_1_fun/ppermute | solution.py:212
  87.0 6.3 %sum_tiles.6 = (bf16[24,128,128]{2,1,0:T(8,128)(2,1)S(1)}, bf16[24,128,128]{2,1,0:T(8,128)(2,1)S(1)}, bf16[24,128,128]{2,1,0:T(8,128)(2,1)S(1)}, bf16[24,128,128...) custom-call(s32[2,256]{1,0:T(2,128)S(1)} %get-tuple-element.99.order_ref, ...), custom_call_target="tpu_custom_call" | custom-call | flops 1000 | bytes 1000 | tf_op jit(solution)/shard_map/cond/branch_1_fun/sum_tiles/pallas_call | solution.py:151
  94.9 6.8 %collective-permute-start.3 = (bf16[24,128,128]{2,1,0:T(8,128)(2,1)S(1)}, bf16[24,128,128]{2,1,0:T(8,128)(2,1)S(1)}, u32[]{:S(2)}, u32[]{:S(2)}) collective-permute-start(bf16[24,128,128]{2,1,0:T(8,128)(2,1)S(1)} %get-tuple-element.111.one_ref), channel_id=1, source_target_pairs={{0,8},{24,16},{1,9},{25,17},{2,10},{26,18},{3,11},{27,19},{4,12},{... | collective-permute-start | bytes 2359304 | tf_op jit(solution)/shard_map/cond/branch_1_fun/ppermute | solution.py:212
  104.4 3.5 collective-permute-done.5.refs_1_.refs_18_
  109.2 10.2 %collective-permute-done.3.other_ref = bf16[24,128,128]{2,1,0:T(8,128)(2,1)S(1)} collective-permute-done((bf16[24,128,128]{2,1,0:T(8,128)(2,1)S(1)}, bf16[24,128,128]{2,1,0:T(8,128)(2,1)S(1)}, u32[]{:S(2)}, u32[]{:S(2)}) %collective-permute-start.3) | collective-permute-done | bytes 786464 | tf_op jit(solution)/shard_map/cond/branch_1_fun/ppermute | solution.py:212
  126.5 7.3 %sum_tiles.7 = (bf16[24,128,128]{2,1,0:T(8,128)(2,1)S(1)}, bf16[24,128,128]{2,1,0:T(8,128)(2,1)S(1)}, bf16[24,128,128]{2,1,0:T(8,128)(2,1)S(1)}, bf16[24,128,128...) custom-call(s32[2,256]{1,0:T(2,128)S(1)} %get-tuple-element.99.order_ref, ...), custom_call_target="tpu_custom_call" | custom-call | flops 1000 | bytes 1000 | tf_op jit(solution)/shard_map/cond/branch_1_fun/sum_tiles/pallas_call | solution.py:151
  133.9 9.3 %collective-permute-done.10.refs_1_.refs_20_ = bf16[24,128,128]{2,1,0:T(8,128)(2,1)} collective-permute-done((bf16[24,128,128]{2,1,0:T(8,128)(2,1)}, bf16[24,128,128]{2,1,0:T(8,128)(2,1)}, u32[]{:S(2)}, u32[]{:S(2)}) %collective-permute-start.10) | collective-permute-done | bytes 786464 | tf_op jit(solution)/shard_map/cond/branch_1_fun/ppermute | solution.py:228
  146.5 14.2 %collective-permute-start.7 = (bf16[24,128,128]{2,1,0:T(8,128)(2,1)S(1)}, bf16[24,128,128]{2,1,0:T(8,128)(2,1)S(1)}, u32[]{:S(2)}, u32[]{:S(2)}) collective-permute-start(bf16[24,128,128]{2,1,0:T(8,128)(2,1)S(1)} %get-tuple-element.115.one_ref), channel_id=1, source_target_pairs={{0,8},{24,16},{1,9},{25,17},{2,10},{26,18},{3,11},{27,19},{4,12},{... | collective-permute-start | bytes 2359304 | tf_op jit(solution)/shard_map/cond/branch_1_fun/ppermute | solution.py:212
  162.0 11.8 %collective-permute-done.11.refs_1_.refs_22_ = bf16[24,128,128]{2,1,0:T(8,128)(2,1)S(1)} collective-permute-done((bf16[24,128,128]{2,1,0:T(8,128)(2,1)S(1)}, bf16[24,128,128]{2,1,0:T(8,128)(2,1)S(1)}, u32[]{:S(2)}, u32[]{:S(2)}) %collective-permute-start.11) | collective-permute-done | bytes 786464 | tf_op jit(solution)/shard_map/cond/branch_1_fun/ppermute | solution.py:228
  177.1 4.7 %collective-permute-start.12 = (bf16[24,128,128]{2,1,0:T(8,128)(2,1)S(1)}, bf16[24,128,128]{2,1,0:T(8,128)(2,1)S(1)}, u32[]{:S(2)}, u32[]{:S(2)}) collective-permute-start(bf16[24,128,128]{2,1,0:T(8,128)(2,1)S(1)} %get-tuple-element.118.one_ref), channel_id=1, source_target_pairs={{0,8},{24,16},{1,9},{25,17},{2,10},{26,18},{3,11},{27,19},{4,12},{... | collective-permute-start | bytes 2359304 | tf_op jit(solution)/shard_map/cond/branch_1_fun/ppermute | solution.py:212
  182.8 6.8 %collective-permute-done.14.refs_1_.refs_23_.refs_14_ = bf16[24,128,128]{2,1,0:T(8,128)(2,1)S(1)} collective-permute-done((bf16[24,128,128]{2,1,0:T(8,128)(2,1)S(1)}, bf16[24,128,128]{2,1,0:T(8,128)(2,1)S(1)}, u32[]{:S(2)}, u32[]{:S(2)}) %collective-permute-start.14) | collective-permute-done | bytes 786464 | tf_op jit(solution)/shard_map/cond/branch_1_fun/ppermute | solution.py:228
  190.8 7.0 %sum_tiles.8 = (bf16[24,128,128]{2,1,0:T(8,128)(2,1)S(1)}, bf16[24,128,128]{2,1,0:T(8,128)(2,1)S(1)}, bf16[24,128,128]{2,1,0:T(8,128)(2,1)S(1)}, bf16[24,128,128...) custom-call(s32[2,256]{1,0:T(2,128)S(1)} %get-tuple-element.99.order_ref, ...), custom_call_target="tpu_custom_call" | custom-call | flops 1000 | bytes 1000 | tf_op jit(solution)/shard_map/cond/branch_1_fun/sum_tiles/pallas_call | solution.py:151
  197.9 4.4 %collective-permute-start.16 = (bf16[24,128,128]{2,1,0:T(8,128)(2,1)S(1)}, bf16[24,128,128]{2,1,0:T(8,128)(2,1)S(1)}, u32[]{:S(2)}, u32[]{:S(2)}) collective-permute-start(bf16[24,128,128]{2,1,0:T(8,128)(2,1)S(1)} %get-tuple-element.120.refs_0_.one_ref), channel_id=1, source_target_pairs={{0,8},{24,16},{1,9},{25,17},{2,10},{26,18},{3,11},{27,19},{4,12},{... | collective-permute-start | bytes 2359304 | tf_op jit(solution)/shard_map/cond/branch_1_fun/ppermute | solution.py:212
  204.8 5.1 %collective-permute-done.18.refs_1_.refs_24_.refs_15_ = bf16[24,128,128]{2,1,0:T(8,128)(2,1)S(1)} collective-permute-done((bf16[24,128,128]{2,1,0:T(8,128)(2,1)S(1)}, bf16[24,128,128]{2,1,0:T(8,128)(2,1)S(1)}, u32[]{:S(2)}, u32[]{:S(2)}) %collective-permute-start.18) | collective-permute-done | bytes 786464 | tf_op jit(solution)/shard_map/cond/branch_1_fun/ppermute | solution.py:228
  210.0 7.9 %collective-permute-done.16.other_ref = bf16[24,128,128]{2,1,0:T(8,128)(2,1)S(1)} collective-permute-done((bf16[24,128,128]{2,1,0:T(8,128)(2,1)S(1)}, bf16[24,128,128]{2,1,0:T(8,128)(2,1)S(1)}, u32[]{:S(2)}, u32[]{:S(2)}) %collective-permute-start.16) | collective-permute-done | bytes 786464 | tf_op jit(solution)/shard_map/cond/branch_1_fun/ppermute | solution.py:212
  217.9 4.4 %collective-permute-start.19 = (bf16[24,128,128]{2,1,0:T(8,128)(2,1)S(1)}, bf16[24,128,128]{2,1,0:T(8,128)(2,1)S(1)}, u32[]{:S(2)}, u32[]{:S(2)}) collective-permute-start(bf16[24,128,128]{2,1,0:T(8,128)(2,1)S(1)} %get-tuple-element.124.one_ref), channel_id=1, source_target_pairs={{0,8},{24,16},{1,9},{25,17},{2,10},{26,18},{3,11},{27,19},{4,12},{... | collective-permute-start | bytes 2359304 | tf_op jit(solution)/shard_map/cond/branch_1_fun/ppermute | solution.py:212
  224.7 9.4 %collective-permute-done.21.refs_1_.refs_25_.refs_16_ = bf16[24,128,128]{2,1,0:T(8,128)(2,1)S(1)} collective-permute-done((bf16[24,128,128]{2,1,0:T(8,128)(2,1)S(1)}, bf16[24,128,128]{2,1,0:T(8,128)(2,1)S(1)}, u32[]{:S(2)}, u32[]{:S(2)}) %collective-permute-start.21) | collective-permute-done | bytes 786464 | tf_op jit(solution)/shard_map/cond/branch_1_fun/ppermute | solution.py:228
  235.6 5.4 %sum_tiles.9 = (bf16[24,128,128]{2,1,0:T(8,128)(2,1)S(1)}, bf16[24,128,128]{2,1,0:T(8,128)(2,1)S(1)}, bf16[24,128,128]{2,1,0:T(8,128)(2,1)S(1)}) custom-call(s32[2,256]{1,0:T(2,128)S(1)} %get-tuple-element.99.order_ref, s32[2,313]{1,0:T(2,128)S(1)} %fusion.bounds_ref, bf16[128,128,128]{2,1,0:T(8,128)(2,1)} %get-tuple-element.103.refs_0_, ...), custom_call_target="tpu_custom_call" | custom-call | flops 1000 | bytes 1000 | tf_op jit(solution)/shard_map/cond/branch_1_fun/sum_tiles/pallas_call | solution.py:151
  242.7 8.2 %collective-permute-done.25.refs_1_.refs_26_.refs_17_ = bf16[24,128,128]{2,1,0:T(8,128)(2,1)S(1)} collective-permute-done((bf16[24,128,128]{2,1,0:T(8,128)(2,1)S(1)}, bf16[24,128,128]{2,1,0:T(8,128)(2,1)S(1)}, u32[]{:S(2)}, u32[]{:S(2)}) %collective-permute-start.25) | collective-permute-done | bytes 786464 | tf_op jit(solution)/shard_map/cond/branch_1_fun/ppermute | solution.py:228
  258.6 7.2 %collective-permute-done.28.refs_1_.refs_27_.refs_18_ = bf16[24,128,128]{2,1,0:T(8,128)(2,1)S(1)} collective-permute-done((bf16[24,128,128]{2,1,0:T(8,128)(2,1)S(1)}, bf16[24,128,128]{2,1,0:T(8,128)(2,1)S(1)}, u32[]{:S(2)}, u32[]{:S(2)}) %collective-permute-start.28) | collective-permute-done | bytes 786464 | tf_op jit(solution)/shard_map/cond/branch_1_fun/ppermute | solution.py:228
  267.3 15.3 %collective-permute-done.29.refs_1_.refs_28_.refs_19_ = bf16[24,128,128]{2,1,0:T(8,128)(2,1)S(1)} collective-permute-done((bf16[24,128,128]{2,1,0:T(8,128)(2,1)S(1)}, bf16[24,128,128]{2,1,0:T(8,128)(2,1)S(1)}, u32[]{:S(2)}, u32[]{:S(2)}) %collective-permute-start.29) | collective-permute-done | bytes 786464 | tf_op jit(solution)/shard_map/cond/branch_1_fun/ppermute | solution.py:228
  286.6 13.1 %collective-permute-done.33.refs_21_ = bf16[24,128,128]{2,1,0:T(8,128)(2,1)} collective-permute-done((bf16[24,128,128]{2,1,0:T(8,128)(2,1)}, bf16[24,128,128]{2,1,0:T(8,128)(2,1)}, u32[]{:S(2)}, u32[]{:S(2)}) %collective-permute-start.33) | collective-permute-done | bytes 786464 | tf_op jit(solution)/shard_map/cond/branch_1_fun/ppermute | solution.py:228
  299.6 25.9 %contract_panels.2.refs_26_ = f32[3072,2048]{1,0:T(8,128)} custom-call(s32[2]{0:T(128)} %pad_add_fusion.place_ref, s32[384]{0:T(512)} %get-tuple-element.200.first_ref, s32[384]{0:T(512)} %get-tuple-element.199.second_ref, bf16[24,128,128]{2,1,0:T(8,128)(2,1)} %copy-done.35, bf16[24,128,128]{2,1,0:T(8,128)(2,1)} %copy-done.27, ...), custom_call_target="tpu_custom_call" | custom-call | flops 1000 | bytes 1000 | tf_op jit(solution)/shard_map/cond/branch_1_fun/contract_panels/pallas_call | solution.py:353
  325.6 5.4 %collective-permute-done.32.refs_21_ = bf16[24,128,128]{2,1,0:T(8,128)(2,1)S(1)} collective-permute-done((bf16[24,128,128]{2,1,0:T(8,128)(2,1)}, bf16[24,128,128]{2,1,0:T(8,128)(2,1)S(1)}, u32[]{:S(2)}, u32[]{:S(2)}) %collective-permute-start.32) | collective-permute-done | bytes 786464 | tf_op jit(solution)/shard_map/cond/branch_1_fun/ppermute | solution.py:228
  331.9 27.3 %contract_panels.3 = bf16[3072,2048]{1,0:T(8,128)(2,1)} custom-call(s32[2]{0:T(128)} %pad_add_fusion.place_ref, s32[384]{0:T(512)} %get-tuple-element.200.first_ref, s32[384]{0:T(512)} %get-tuple-element.199.second_ref, bf16[24,128,128]{2,1,0:T(8,128)(2,1)} %copy-done.9, bf16[24,128,128]{2,1,0:T(8,128)(2,1)} %copy-done.25, bf16[24,128,128]{2,1,0:T(8,128)(2,1)} %copy-done.4, ...), custom_call_target="tpu_custom_call" | custom-call | flops 1000 | bytes 1000 | tf_op jit(solution)/shard_map/cond/branch_1_fun/contract_panels/pallas_call | solution.py:353
  (229 shorter events, 62.3 us)
Async XLA Ops:
  16.6 53.7 %all-to-all-start.4 = ((bf16[128,128,128]{2,1,0:T(8,128)(2,1)}), bf16[128,128,128]{2,1,0:T(8,128)(2,1)}, u32[]{:S(2)}, u32[]{:S(2)}) async-start(bf16[128,128,128]{2,1,0:T(8,128)(2,1)} %copy-done.3), calls=%async_computation.4 | async-start | bytes 8388608 | tf_op jit(solution)/shard_map/all_to_all | solution.py:395
  70.4 56.2 %all-to-all-start = ((bf16[128,128,128]{2,1,0:T(8,128)(2,1)}), bf16[128,128,128]{2,1,0:T(8,128)(2,1)}, u32[]{:S(2)}, u32[]{:S(2)}) async-start(bf16[128,128,128]{2,1,0:T(8,128)(2,1)} %get-tuple-element.104), calls=%async_computation | async-start | bytes 8388608 | tf_op jit(solution)/shard_map/cond/branch_1_fun/all_to_all | solution.py:395
  79.5 22.1 %collective-permute-start.1 = (bf16[24,128,128]{2,1,0:T(8,128)(2,1)S(1)}, bf16[24,128,128]{2,1,0:T(8,128)(2,1)S(1)}, u32[]{:S(2)}, u32[]{:S(2)}) collective-permute-start(bf16[24,128,128]{2,1,0:T(8,128)(2,1)S(1)} %get-tuple-element.109.refs_0_), channel_id=1, source_target_pairs={{8,16},{16,8},{9,17},{17,9},{10,18},{18,10},{11,19},{19,11},{12,20... | collective-permute-start | bytes 2359304 | tf_op jit(solution)/shard_map/cond/branch_1_fun/ppermute | solution.py:219
  80.3 23.3 %collective-permute-start = (bf16[24,128,128]{2,1,0:T(8,128)(2,1)S(1)}, bf16[24,128,128]{2,1,0:T(8,128)(2,1)S(1)}, u32[]{:S(2)}, u32[]{:S(2)}) collective-permute-start(bf16[24,128,128]{2,1,0:T(8,128)(2,1)S(1)} %get-tuple-element.107.one_ref), channel_id=1, source_target_pairs={{0,8},{24,16},{1,9},{25,17},{2,10},{26,18},{3,11},{27,19},{4,12},{... | collective-permute-start | bytes 2359304 | tf_op jit(solution)/shard_map/cond/branch_1_fun/ppermute | solution.py:212
  85.7 22.3 %collective-permute-start.5 = (bf16[24,128,128]{2,1,0:T(8,128)(2,1)S(1)}, bf16[24,128,128]{2,1,0:T(8,128)(2,1)S(1)}, u32[]{:S(2)}, u32[]{:S(2)}) collective-permute-start(bf16[24,128,128]{2,1,0:T(8,128)(2,1)S(1)} %get-tuple-element.105.refs_1_), channel_id=1, source_target_pairs={{8,0},{16,24},{9,1},{17,25},{10,2},{18,26},{11,3},{19,27},{12,4},{... | collective-permute-start | bytes 2359304 | tf_op jit(solution)/shard_map/cond/branch_1_fun/ppermute | solution.py:228
  94.9 24.6 %collective-permute-start.3 = (bf16[24,128,128]{2,1,0:T(8,128)(2,1)S(1)}, bf16[24,128,128]{2,1,0:T(8,128)(2,1)S(1)}, u32[]{:S(2)}, u32[]{:S(2)}) collective-permute-start(bf16[24,128,128]{2,1,0:T(8,128)(2,1)S(1)} %get-tuple-element.111.one_ref), channel_id=1, source_target_pairs={{0,8},{24,16},{1,9},{25,17},{2,10},{26,18},{3,11},{27,19},{4,12},{... | collective-permute-start | bytes 2359304 | tf_op jit(solution)/shard_map/cond/branch_1_fun/ppermute | solution.py:212
  101.9 21.8 %collective-permute-start.6 = (bf16[24,128,128]{2,1,0:T(8,128)(2,1)S(1)}, bf16[24,128,128]{2,1,0:T(8,128)(2,1)S(1)}, u32[]{:S(2)}, u32[]{:S(2)}) collective-permute-start(bf16[24,128,128]{2,1,0:T(8,128)(2,1)S(1)} %add_tiles.18.refs_0_), channel_id=1, source_target_pairs={{8,0},{16,24},{9,1},{17,25},{10,2},{18,26},{11,3},{19,27},{12,4},{... | collective-permute-start | bytes 2359304 | tf_op jit(solution)/shard_map/cond/branch_1_fun/ppermute | solution.py:228
  103.7 19.9 %collective-permute-start.2 = (bf16[24,128,128]{2,1,0:T(8,128)(2,1)S(1)}, bf16[24,128,128]{2,1,0:T(8,128)(2,1)S(1)}, u32[]{:S(2)}, u32[]{:S(2)}) collective-permute-start(bf16[24,128,128]{2,1,0:T(8,128)(2,1)S(1)} %add_tiles.19.refs_0_.refs_2_), channel_id=1, source_target_pairs={{8,16},{16,8},{9,17},{17,9},{10,18},{18,10},{11,19},{19,11},{12,20... | collective-permute-start | bytes 2359304 | tf_op jit(solution)/shard_map/cond/branch_1_fun/ppermute | solution.py:219
  121.3 21.9 %collective-permute-start.10 = (bf16[24,128,128]{2,1,0:T(8,128)(2,1)}, bf16[24,128,128]{2,1,0:T(8,128)(2,1)}, u32[]{:S(2)}, u32[]{:S(2)}) collective-permute-start(bf16[24,128,128]{2,1,0:T(8,128)(2,1)} %add_tiles.20.refs_0_), channel_id=1, source_target_pairs={{8,0},{16,24},{9,1},{17,25},{10,2},{18,26},{11,3},{19,27},{12,4},{... | collective-permute-start | bytes 2359304 | tf_op jit(solution)/shard_map/cond/branch_1_fun/ppermute | solution.py:228
  122.6 59.5 %collective-permute-start.15 = (bf16[512,2048]{1,0:T(8,128)(2,1)}, bf16[512,2048]{1,0:T(8,128)(2,1)S(1)}, u32[]{:S(2)}, u32[]{:S(2)}) collective-permute-start(bf16[512,2048]{1,0:T(8,128)(2,1)} %get-tuple-element.122.refs_29_.refs_22_), channel_id=1, source_target_pairs={{0,7},{1,0},{2,1},{3,2},{4,3},{5,4},{6,5},{7,6},{8,15},{9,8},{10,9... | collective-permute-start | bytes 6291464 | tf_op jit(solution)/shard_map/cond/branch_1_fun/ppermute | solution.py:34
  144.5 29.3 %collective-permute-start.11 = (bf16[24,128,128]{2,1,0:T(8,128)(2,1)S(1)}, bf16[24,128,128]{2,1,0:T(8,128)(2,1)S(1)}, u32[]{:S(2)}, u32[]{:S(2)}) collective-permute-start(bf16[24,128,128]{2,1,0:T(8,128)(2,1)S(1)} %add_tiles.23.refs_0_), channel_id=1, source_target_pairs={{8,0},{16,24},{9,1},{17,25},{10,2},{18,26},{11,3},{19,27},{12,4},{... | collective-permute-start | bytes 2359304 | tf_op jit(solution)/shard_map/cond/branch_1_fun/ppermute | solution.py:228
  145.8 30.4 %collective-permute-start.8 = (bf16[24,128,128]{2,1,0:T(8,128)(2,1)S(1)}, bf16[24,128,128]{2,1,0:T(8,128)(2,1)S(1)}, u32[]{:S(2)}, u32[]{:S(2)}) collective-permute-start(bf16[24,128,128]{2,1,0:T(8,128)(2,1)S(1)} %get-tuple-element.113.refs_0_.refs_4_), channel_id=1, source_target_pairs={{8,16},{16,8},{9,17},{17,9},{10,18},{18,10},{11,19},{19,11},{12,20... | collective-permute-start | bytes 2359304 | tf_op jit(solution)/shard_map/cond/branch_1_fun/ppermute | solution.py:219
  146.5 30.6 %collective-permute-start.7 = (bf16[24,128,128]{2,1,0:T(8,128)(2,1)S(1)}, bf16[24,128,128]{2,1,0:T(8,128)(2,1)S(1)}, u32[]{:S(2)}, u32[]{:S(2)}) collective-permute-start(bf16[24,128,128]{2,1,0:T(8,128)(2,1)S(1)} %get-tuple-element.115.one_ref), channel_id=1, source_target_pairs={{0,8},{24,16},{1,9},{25,17},{2,10},{26,18},{3,11},{27,19},{4,12},{... | collective-permute-start | bytes 2359304 | tf_op jit(solution)/shard_map/cond/branch_1_fun/ppermute | solution.py:212
  160.7 28.8 %collective-permute-start.14 = (bf16[24,128,128]{2,1,0:T(8,128)(2,1)S(1)}, bf16[24,128,128]{2,1,0:T(8,128)(2,1)S(1)}, u32[]{:S(2)}, u32[]{:S(2)}) collective-permute-start(bf16[24,128,128]{2,1,0:T(8,128)(2,1)S(1)} %get-tuple-element.121), channel_id=1, source_target_pairs={{8,0},{16,24},{9,1},{17,25},{10,2},{18,26},{11,3},{19,27},{12,4},{... | collective-permute-start | bytes 2359304 | tf_op jit(solution)/shard_map/cond/branch_1_fun/ppermute | solution.py:228
  173.8 48.8 %collective-permute-start.22 = (bf16[512,2048]{1,0:T(8,128)(2,1)}, bf16[512,2048]{1,0:T(8,128)(2,1)S(1)}, u32[]{:S(2)}, u32[]{:S(2)}) collective-permute-start(bf16[512,2048]{1,0:T(8,128)(2,1)} %get-tuple-element.122.refs_29_.refs_22_), channel_id=1, source_target_pairs={{0,6},{1,7},{2,0},{3,1},{4,2},{5,3},{6,4},{7,5},{8,14},{9,15},{10,... | collective-permute-start | bytes 6291464 | tf_op jit(solution)/shard_map/cond/branch_1_fun/ppermute | solution.py:34
  176.2 21.7 %collective-permute-start.13 = (bf16[24,128,128]{2,1,0:T(8,128)(2,1)S(1)}, bf16[24,128,128]{2,1,0:T(8,128)(2,1)S(1)}, u32[]{:S(2)}, u32[]{:S(2)}) collective-permute-start(bf16[24,128,128]{2,1,0:T(8,128)(2,1)S(1)} %get-tuple-element.114.refs_5_.refs_1_), channel_id=1, source_target_pairs={{8,16},{16,8},{9,17},{17,9},{10,18},{18,10},{11,19},{19,11},{12,20... | collective-permute-start | bytes 2359304 | tf_op jit(solution)/shard_map/cond/branch_1_fun/ppermute | solution.py:219
  177.1 25.4 %collective-permute-start.12 = (bf16[24,128,128]{2,1,0:T(8,128)(2,1)S(1)}, bf16[24,128,128]{2,1,0:T(8,128)(2,1)S(1)}, u32[]{:S(2)}, u32[]{:S(2)}) collective-permute-start(bf16[24,128,128]{2,1,0:T(8,128)(2,1)S(1)} %get-tuple-element.118.one_ref), channel_id=1, source_target_pairs={{0,8},{24,16},{1,9},{25,17},{2,10},{26,18},{3,11},{27,19},{4,12},{... | collective-permute-start | bytes 2359304 | tf_op jit(solution)/shard_map/cond/branch_1_fun/ppermute | solution.py:212
  182.0 21.4 %collective-permute-start.17 = (bf16[24,128,128]{2,1,0:T(8,128)(2,1)S(1)}, bf16[24,128,128]{2,1,0:T(8,128)(2,1)S(1)}, u32[]{:S(2)}, u32[]{:S(2)}) collective-permute-start(bf16[24,128,128]{2,1,0:T(8,128)(2,1)S(1)} %add_tiles.25.refs_2_.refs_6_), channel_id=1, source_target_pairs={{8,16},{16,8},{9,17},{17,9},{10,18},{18,10},{11,19},{19,11},{12,20... | collective-permute-start | bytes 2359304 | tf_op jit(solution)/shard_map/cond/branch_1_fun/ppermute | solution.py:219
  189.5 20.3 %collective-permute-start.18 = (bf16[24,128,128]{2,1,0:T(8,128)(2,1)S(1)}, bf16[24,128,128]{2,1,0:T(8,128)(2,1)S(1)}, u32[]{:S(2)}, u32[]{:S(2)}) collective-permute-start(bf16[24,128,128]{2,1,0:T(8,128)(2,1)S(1)} %add_tiles.24.refs_0_), channel_id=1, source_target_pairs={{8,0},{16,24},{9,1},{17,25},{10,2},{18,26},{11,3},{19,27},{12,4},{... | collective-permute-start | bytes 2359304 | tf_op jit(solution)/shard_map/cond/branch_1_fun/ppermute | solution.py:228
  197.9 20.0 %collective-permute-start.16 = (bf16[24,128,128]{2,1,0:T(8,128)(2,1)S(1)}, bf16[24,128,128]{2,1,0:T(8,128)(2,1)S(1)}, u32[]{:S(2)}, u32[]{:S(2)}) collective-permute-start(bf16[24,128,128]{2,1,0:T(8,128)(2,1)S(1)} %get-tuple-element.120.refs_0_.one_ref), channel_id=1, source_target_pairs={{0,8},{24,16},{1,9},{25,17},{2,10},{26,18},{3,11},{27,19},{4,12},{... | collective-permute-start | bytes 2359304 | tf_op jit(solution)/shard_map/cond/branch_1_fun/ppermute | solution.py:212
  202.7 21.2 %collective-permute-start.20 = (bf16[24,128,128]{2,1,0:T(8,128)(2,1)S(1)}, bf16[24,128,128]{2,1,0:T(8,128)(2,1)S(1)}, u32[]{:S(2)}, u32[]{:S(2)}) collective-permute-start(bf16[24,128,128]{2,1,0:T(8,128)(2,1)S(1)} %add_tiles.27.refs_0_.refs_7_.refs_3_), channel_id=1, source_target_pairs={{8,16},{16,8},{9,17},{17,9},{10,18},{18,10},{11,19},{19,11},{12,20... | collective-permute-start | bytes 2359304 | tf_op jit(solution)/shard_map/cond/branch_1_fun/ppermute | solution.py:219
  203.5 30.6 %collective-permute-start.21 = (bf16[24,128,128]{2,1,0:T(8,128)(2,1)S(1)}, bf16[24,128,128]{2,1,0:T(8,128)(2,1)S(1)}, u32[]{:S(2)}, u32[]{:S(2)}) collective-permute-start(bf16[24,128,128]{2,1,0:T(8,128)(2,1)S(1)} %add_tiles.26.refs_0_), channel_id=1, source_target_pairs={{8,0},{16,24},{9,1},{17,25},{10,2},{18,26},{11,3},{19,27},{12,4},{... | collective-permute-start | bytes 2359304 | tf_op jit(solution)/shard_map/cond/branch_1_fun/ppermute | solution.py:228
  209.8 47.4 %collective-permute-start.30 = (bf16[512,2048]{1,0:T(8,128)(2,1)}, bf16[512,2048]{1,0:T(8,128)(2,1)S(1)}, u32[]{:S(2)}, u32[]{:S(2)}) collective-permute-start(bf16[512,2048]{1,0:T(8,128)(2,1)} %get-tuple-element.122.refs_29_.refs_22_), channel_id=1, source_target_pairs={{0,5},{1,6},{2,7},{3,0},{4,1},{5,2},{6,3},{7,4},{8,13},{9,14},{10,... | collective-permute-start | bytes 6291464 | tf_op jit(solution)/shard_map/cond/branch_1_fun/ppermute | solution.py:34
  217.9 23.3 %collective-permute-start.19 = (bf16[24,128,128]{2,1,0:T(8,128)(2,1)S(1)}, bf16[24,128,128]{2,1,0:T(8,128)(2,1)S(1)}, u32[]{:S(2)}, u32[]{:S(2)}) collective-permute-start(bf16[24,128,128]{2,1,0:T(8,128)(2,1)S(1)} %get-tuple-element.124.one_ref), channel_id=1, source_target_pairs={{0,8},{24,16},{1,9},{25,17},{2,10},{26,18},{3,11},{27,19},{4,12},{... | collective-permute-start | bytes 2359304 | tf_op jit(solution)/shard_map/cond/branch_1_fun/ppermute | solution.py:212
  222.6 28.3 %collective-permute-start.25 = (bf16[24,128,128]{2,1,0:T(8,128)(2,1)S(1)}, bf16[24,128,128]{2,1,0:T(8,128)(2,1)S(1)}, u32[]{:S(2)}, u32[]{:S(2)}) collective-permute-start(bf16[24,128,128]{2,1,0:T(8,128)(2,1)S(1)} %add_tiles.28.refs_0_), channel_id=1, source_target_pairs={{8,0},{16,24},{9,1},{17,25},{10,2},{18,26},{11,3},{19,27},{12,4},{... | collective-permute-start | bytes 2359304 | tf_op jit(solution)/shard_map/cond/branch_1_fun/ppermute | solution.py:228
  223.9 27.7 %collective-permute-start.24 = (bf16[24,128,128]{2,1,0:T(8,128)(2,1)S(1)}, bf16[24,128,128]{2,1,0:T(8,128)(2,1)S(1)}, u32[]{:S(2)}, u32[]{:S(2)}) collective-permute-start(bf16[24,128,128]{2,1,0:T(8,128)(2,1)S(1)} %add_tiles.29.refs_2_.refs_8_.refs_4_), channel_id=1, source_target_pairs={{8,16},{16,8},{9,17},{17,9},{10,18},{18,10},{11,19},{19,11},{12,20... | collective-permute-start | bytes 2359304 | tf_op jit(solution)/shard_map/cond/branch_1_fun/ppermute | solution.py:219
  234.1 20.9 %collective-permute-start.23 = (bf16[24,128,128]{2,1,0:T(8,128)(2,1)S(1)}, bf16[24,128,128]{2,1,0:T(8,128)(2,1)S(1)}, u32[]{:S(2)}, u32[]{:S(2)}) collective-permute-start(bf16[24,128,128]{2,1,0:T(8,128)(2,1)S(1)} %get-tuple-element.127.one_ref), channel_id=1, source_target_pairs={{0,8},{24,16},{1,9},{25,17},{2,10},{26,18},{3,11},{27,19},{4,12},{... | collective-permute-start | bytes 2359304 | tf_op jit(solution)/shard_map/cond/branch_1_fun/ppermute | solution.py:212
  241.2 24.6 %collective-permute-start.28 = (bf16[24,128,128]{2,1,0:T(8,128)(2,1)S(1)}, bf16[24,128,128]{2,1,0:T(8,128)(2,1)S(1)}, u32[]{:S(2)}, u32[]{:S(2)}) collective-permute-start(bf16[24,128,128]{2,1,0:T(8,128)(2,1)S(1)} %add_tiles.30.refs_0_), channel_id=1, source_target_pairs={{8,0},{16,24},{9,1},{17,25},{10,2},{18,26},{11,3},{19,27},{12,4},{... | collective-permute-start | bytes 2359304 | tf_op jit(solution)/shard_map/cond/branch_1_fun/ppermute | solution.py:228
  255.9 26.7 %collective-permute-start.29 = (bf16[24,128,128]{2,1,0:T(8,128)(2,1)S(1)}, bf16[24,128,128]{2,1,0:T(8,128)(2,1)S(1)}, u32[]{:S(2)}, u32[]{:S(2)}) collective-permute-start(bf16[24,128,128]{2,1,0:T(8,128)(2,1)S(1)} %add_tiles.32.refs_0_), channel_id=1, source_target_pairs={{8,0},{16,24},{9,1},{17,25},{10,2},{18,26},{11,3},{19,27},{12,4},{... | collective-permute-start | bytes 2359304 | tf_op jit(solution)/shard_map/cond/branch_1_fun/ppermute | solution.py:228
  257.3 42.4 %collective-permute-start.33 = (bf16[24,128,128]{2,1,0:T(8,128)(2,1)}, bf16[24,128,128]{2,1,0:T(8,128)(2,1)}, u32[]{:S(2)}, u32[]{:S(2)}) collective-permute-start(bf16[24,128,128]{2,1,0:T(8,128)(2,1)} %add_tiles.22.refs_2_), channel_id=1, source_target_pairs={{8,0},{16,24},{9,1},{17,25},{10,2},{18,26},{11,3},{19,27},{12,4},{... | collective-permute-start | bytes 2359304 | tf_op jit(solution)/shard_map/cond/branch_1_fun/ppermute | solution.py:228
  266.0 59.6 %collective-permute-start.31 = (bf16[24,128,128]{2,1,0:T(8,128)(2,1)S(1)}, bf16[24,128,128]{2,1,0:T(8,128)(2,1)S(1)}, u32[]{:S(2)}, u32[]{:S(2)}) collective-permute-start(bf16[24,128,128]{2,1,0:T(8,128)(2,1)S(1)} %add_tiles.34.refs_0_), channel_id=1, source_target_pairs={{8,0},{16,24},{9,1},{17,25},{10,2},{18,26},{11,3},{19,27},{12,4},{... | collective-permute-start | bytes 2359304 | tf_op jit(solution)/shard_map/cond/branch_1_fun/ppermute | solution.py:228
  283.8 47.2 %collective-permute-start.32 = (bf16[24,128,128]{2,1,0:T(8,128)(2,1)}, bf16[24,128,128]{2,1,0:T(8,128)(2,1)S(1)}, u32[]{:S(2)}, u32[]{:S(2)}) collective-permute-start(bf16[24,128,128]{2,1,0:T(8,128)(2,1)} %add_tiles.35), channel_id=1, source_target_pairs={{8,0},{16,24},{9,1},{17,25},{10,2},{18,26},{11,3},{19,27},{12,4},{... | collective-permute-start | bytes 2359304 | tf_op jit(solution)/shard_map/cond/branch_1_fun/ppermute | solution.py:228
  (45 other events, 669.0 us)
